TPU v7x, 128 devices: a whole 4x4x4 slice. The times are simulated.
128 devices in a mesh: query: 8 (over y, core), index: 16 (over z, x).
Axes of the slice: x: 4, y: 4, z: 4, core: 2. Of those that a mesh axis runs over, the one named last changes fastest.
Arguments:
- tokens: bfloat16 [131072, 768], P(('query', 'index')), may hold values from -24 to 24
- w_in: bfloat16 [768, 3072], replicated, may hold values from -0.21875 to 0.21875
- bias_in: float32 [3072], replicated, may hold values from -3 to 3
- w_out: bfloat16 [3072, 768], replicated, may hold values from -0.109375 to 0.109375
- bias_out: float32 [768], replicated, may hold values from -3 to 3
- gain: float32 [768], replicated, may hold values from 0.5 to 1.5
- shift: float32 [768], replicated, may hold values from -0.5 to 0.5
- slab: bfloat16 [65536, 768], P('index')
- owners: int32 [2048, 64, 1], P(('query', 'index')), may hold values from 0 to 15; in each aligned block of 1024 rows (0 to 1023, 1024 to 2047, ..., all dimensions but the last counted through in order) at most 192 rows name the same one
- offsets: int32 [2048, 64], P(('query', 'index')), may hold values from 0 to 4095
- reader_weights: float32 [2048, 64], P(('query', 'index')), may hold values from 0.01 to 1
Outputs:
- token_grads: bfloat16 [131072, 768], P(('query', 'index'))
- layer_grads: float32 [3072, 1536], P(('query', 'index'))
Inputs may be any that keep to these rules, and one draw needn't show every extreme that they name: `owners`: among the rows of one device, no shard number appears more than 192 times, and some shard appears exactly 192 times.
All inputs are finite; a program needn't handle non-finite values.
Results may differ from a plain program's by a relative error of at most 0.0082.
Values may be sent and summed in bfloat16 or wider, within the bound.
No kernel may reach another device: no remote copies, remote signals or barrier semaphores. Data moves between devices by JAX's collectives and lax.ppermute only.
A program may use at most 192 MiB of HBM per device.

v0:
```python
import jax
import jax.numpy as jnp
from jax import lax
from jax.sharding import PartitionSpec as P

loss_scale = 256.0
norm_eps = 1e-12


def gelu_tanh(value):
    return jax.nn.gelu(value, approximate=True)


def body(
    tokens, w_in, bias_in, w_out, bias_out, gain, shift, slab, owners, offsets, reader_weights
):
    shards = lax.axis_size("index")
    devices = lax.axis_size("query") * lax.axis_size("index")
    questions = offsets.shape[0]
    picks = offsets.shape[1]
    width = tokens.shape[1]
    length = tokens.shape[0] // questions
    slots = questions * picks
    capacity = 3 * slots // shards
    flat_owner = owners.reshape(slots)
    flat_offset = offsets.reshape(slots)
    member = (flat_owner[:, None] == jnp.arange(shards, dtype=jnp.int32)[None, :]).astype(jnp.int32)
    before = jnp.cumsum(member, axis=0) - member
    rank_in = jnp.sum(before * member, axis=1)
    position = flat_owner * capacity + rank_in
    pre = jnp.dot(tokens, w_in, preferred_element_type=jnp.float32) + bias_in
    hidden = gelu_tanh(pre).astype(jnp.bfloat16)
    resid = (
        tokens.astype(jnp.float32)
        + jnp.dot(hidden, w_out, preferred_element_type=jnp.float32)
        + bias_out
    )
    centre = jnp.mean(resid, axis=-1, keepdims=True)
    spread = jnp.mean(jnp.square(resid - centre), axis=-1, keepdims=True)
    rstd = lax.rsqrt(spread + norm_eps)
    normed = (resid - centre) * rstd
    query = jnp.mean((normed * gain + shift).reshape(questions, length, width), axis=1)
    target = reader_weights / jnp.sum(reader_weights, axis=-1, keepdims=True)
    wanted = jnp.zeros((shards * capacity,), jnp.int32).at[position].set(flat_offset)
    arrived = lax.all_to_all(
        wanted.reshape(shards, capacity), "index", split_axis=0, concat_axis=0, tiled=True
    )
    fetched = slab[arrived.reshape(shards * capacity)].reshape(shards, capacity, width)
    returned = lax.all_to_all(fetched, "index", split_axis=0, concat_axis=0, tiled=True)
    rows = returned.reshape(shards * capacity, width)[position].reshape(questions, picks, width)
    rows_wide = rows.astype(jnp.float32)
    scores = jnp.einsum("qd,qkd->qk", query, rows_wide, precision=lax.Precision.HIGHEST)
    prob = jax.nn.softmax(scores, axis=-1)
    coef = loss_scale * (prob - target)
    query_grad = jnp.einsum("qk,qkd->qd", coef, rows_wide, precision=lax.Precision.HIGHEST)
    upper = jnp.repeat(query_grad / length, length, axis=0) * gain
    resid_grad = (
        upper
        - jnp.mean(upper, axis=-1, keepdims=True)
        - normed * jnp.mean(upper * normed, axis=-1, keepdims=True)
    ) * rstd
    out_grad = resid_grad.astype(jnp.bfloat16)
    hid_grad = jnp.dot(out_grad, w_out.T, preferred_element_type=jnp.float32)
    _, pull = jax.vjp(gelu_tanh, pre)
    pre_grad = pull(hid_grad)[0].astype(jnp.bfloat16)
    token_grads = (
        resid_grad + jnp.dot(pre_grad, w_in.T, preferred_element_type=jnp.float32)
    ).astype(jnp.bfloat16)
    first = lax.dot_general(
        pre_grad, tokens, (((0,), (0,)), ((), ())), preferred_element_type=jnp.float32
    )
    second = lax.dot_general(
        hidden, out_grad, (((0,), (0,)), ((), ())), preferred_element_type=jnp.float32
    )
    summed = lax.psum_scatter(
        jnp.concatenate([first, second], axis=1),
        ("query", "index"),
        scatter_dimension=0,
        tiled=True,
    )
    return (token_grads, summed / devices)


def solution(mesh):
    placed = (
        P(("query", "index"), None),
        P(),
        P(),
        P(),
        P(),
        P(),
        P(),
        P("index", None),
        P(("query", "index"), None, None),
        P(("query", "index"), None),
        P(("query", "index"), None),
    )
    return jax.shard_map(
        body,
        mesh=mesh,
        in_specs=placed,
        out_specs=(P(("query", "index"), None), P(("query", "index"), None)),
        check_vma=False,
    )
```

profile of v0, /device:TPU:0, one launch (start us, length us, event | category | flops | bytes accessed | tf_op | source)
XLA Modules:
  0.0 446.3 jit_solution(2050989761401319608)
XLA Ops:
  7.2 0.8 reshape.169
  7.9 0.8 eq.29
  8.7 0.5 broadcast.189
  9.2 1.4 fusion.23
  10.6 0.1 eq.25
  10.7 0.1 mul.126
  10.8 4.5 %reduce-window.6 = s32[16,8,128]{2,1,0:T(8,128)S(1)} reduce-window(s32[16,8,128]{2,1,0:T(8,128)S(1)} %fusion.16, s32[]{:T(128)} %constant.16.clone.1), window={size=1x1x128 pad=0_0x0_0x127_0}, to_apply=%region_3.4 | reduce-window | flops 2080768 | bytes 131076 | tf_op jit(solution)/shard_map/reduce-window
  15.3 0.1 slice.12
  15.4 0.1 copy.16
  15.5 0.1 copy.17
  15.6 0.1 broadcast_add_fusion
  15.7 4.3 scatter_custom_fusion
  20.1 0.1 all_to_all.9
  20.2 15.3 %all_to_all.14 = s32[16,1,192]{2,1,0:T(1,128)S(1)} all-to-all(s32[16,1,192]{2,1,0:T(1,128)S(1)} %all_to_all.9), channel_id=1, replica_groups=mesh['query'=8,'index'=16] {'index'}, dimensions={0} | all-to-all | bytes 24576 | tf_op jit(solution)/shard_map/all_to_all | solution.py:45
  35.6 0.1 reshape.144
  35.7 18.2 %gather_fusion = bf16[3072,768]{1,0:T(8,128)(2,1)} fusion(bf16[4096,768]{1,0:T(8,128)(2,1)} %param.18, s32[3072]{0:T(1024)S(1)} %broadcast_clamp_fusion), kind=kCustom, calls=%fused_computation | custom fusion | bytes 9449472 | tf_op jit(solution)/shard_map/gather | solution.py:48
  53.8 0.0 copy-start.1
  53.8 0.0 copy-start.3
  53.8 4.7 %all-to-all-start.1 = ((bf16[16,192,768]{2,1,0:T(8,128)(2,1)}), bf16[16,192,768]{2,1,0:T(8,128)(2,1)}, u32[]{:S(2)}, u32[]{:S(2)}) async-start(bf16[16,192,768]{2,1,0:T(8,128)(2,1)} %bitcast.68), calls=%async_computation.1 | async-start | bytes 9437184 | tf_op jit(solution)/shard_map/all_to_all | solution.py:49
  58.6 0.2 reduce-scatter.4.cloned.1.call-start
  58.8 0.0 copy-done.1
  58.8 0.1 reduce_sum.80
  58.9 0.0 copy-done.3
  58.9 0.0 copy-start.4
  58.9 0.0 copy-start.6
  58.9 0.0 copy-start.7
  59.0 7.0 %fusion.25 = f32[1024,3072]{1,0:T(8,128)S(1)} fusion(bf16[1024,768]{1,0:T(8,128)(2,1)S(1)} %copy-done.3, bf16[768,3072]{1,0:T(8,128)(2,1)} %param.12), kind=kOutput, calls=%fused_computation.58 | convolution fusion | flops 4831838208 | bytes 18874368 | tf_op jit(solution)/shard_map/dot_general | solution.py:31
  66.0 0.0 copy-done.4
  66.0 0.0 copy-done.6
  66.0 0.0 copy-done.7
  66.0 0.0 copy-start.8
  66.0 0.0 copy-start
  66.0 0.0 copy-start.2
  66.0 13.9 %fusion.24 = (f32[1024]{0:T(1024)S(1)}, f32[1024,768]{1,0:T(8,128)S(1)}) fusion(f32[768]{0:T(1024)S(1)} %copy-done.7, bf16[3072,768]{1,0:T(8,128)(2,1)} %param.14, f32[1024,3072]{1,0:T(8,128)S(1)} %fusion.25, f32[3072]{0:T(1024)S(1)} %copy-done.6, bf16[1024,768]{1,0:T(8,128)(2,1)S(1)} %copy-done.4), kind=kOutput, calls=%fused_computation.57 | convolution fusion | flops 4866440192 | bytes 22039552 | tf_op jit(solution)/shard_map/dot_general | solution.py:35
  79.9 0.0 copy-done.8
  79.9 0.5 multiply_reduce_fusion.1
  80.4 0.0 copy-done
  80.4 0.0 copy-done.2
  80.4 0.8 bitcast_reduce_fusion
  81.3 45.1 %all-to-all-done.1 = bf16[16,192,768]{2,1,0:T(8,128)(2,1)} async-done(((bf16[16,192,768]{2,1,0:T(8,128)(2,1)}), bf16[16,192,768]{2,1,0:T(8,128)(2,1)}, u32[]{:S(2)}, u32[]{:S(2)}) %all-to-all-start.1) | async-done | bytes 4718624 | tf_op jit(solution)/shard_map/all_to_all | solution.py:49
  126.3 8.5 %gather_fusion.1 = bf16[1024,768]{1,0:T(8,128)(2,1)} fusion(bf16[3072,768]{1,0:T(8,128)(2,1)} %bitcast.8, s32[1024]{0:T(1024)S(1)} %broadcast_clamp_fusion.1), kind=kCustom, calls=%fused_computation.1 | custom fusion | bytes 3149824 | tf_op jit(solution)/shard_map/gather | solution.py:50
  134.8 2.7 fusion.17
  137.6 0.1 reduce_max.9
  137.7 0.2 fusion.19
  137.9 0.1 subtract_multiply_fusion.1
  138.0 2.1 fusion.26
  140.1 0.6 fusion.11
  140.8 0.2 multiply_reduce_fusion
  141.0 0.1 div.51
  141.1 1.0 fusion.12
  142.1 16.5 %fusion.6 = bf16[1024,3072]{1,0:T(8,128)(2,1)} fusion(f32[1024,3072]{1,0:T(8,128)} %copy-done.8, f32[3072]{0:T(1024)S(1)} %copy-done.6, bf16[1024,768]{1,0:T(8,128)(2,1)S(1)} %fusion.12, bf16[3072,768]{1,0:T(8,128)(2,1)} %param.14), kind=kOutput, calls=%fused_computation.12 | convolution fusion | flops 4897898496 | bytes 25178112 | tf_op jit(solution)/shard_map/dot_general | solution.py:63
  158.6 0.0 copy-start.5
  158.6 9.3 %fusion.22 = f32[3072,768]{0,1:T(8,128)S(1)} fusion(bf16[1024,768]{1,0:T(8,128)(2,1)S(1)} %fusion.12, f32[1024,3072]{1,0:T(8,128)} %copy-done.8, f32[3072]{0:T(1024)S(1)} %copy-done.6), kind=kOutput, calls=%fused_computation.55 | convolution fusion | flops 4863295488 | bytes 23605248 | tf_op jit(solution)/shard_map/dot_general | solution.py:72
  167.9 0.0 copy-done.5
  167.9 7.5 %fusion.27 = f32[3072,768]{0,1:T(8,128)S(1)} fusion(bf16[1024,3072]{1,0:T(8,128)(2,1)} %fusion.6, bf16[1024,768]{1,0:T(8,128)(2,1)S(1)} %copy-done.5), kind=kOutput, calls=%fused_computation.60 | convolution fusion | flops 4831838208 | bytes 17301504 | tf_op jit(solution)/shard_map/dot_general | solution.py:69
  175.4 7.1 %pad_maximum_fusion = f32[3072,1536]{0,1:T(8,128)} fusion(f32[3072,768]{0,1:T(8,128)S(1)} %fusion.22, f32[3072,768]{0,1:T(8,128)S(1)} %fusion.27), kind=kLoop, calls=%fused_computation.3 | loop fusion | flops 4718592 | bytes 37748736 | tf_op jit(solution)/shard_map/concatenate | solution.py:76
  182.5 18.7 %copy.23 = f32[3072,1536]{1,0:T(8,128)} copy(f32[3072,1536]{0,1:T(8,128)} %pad_maximum_fusion) | data formatting | bytes 37748736
  201.2 0.0 reduce-scatter.4.cloned.1.call-update
  201.2 9.7 %add_convert_fusion = bf16[1024,768]{1,0:T(8,128)(2,1)} fusion(f32[1024,768]{1,0:T(8,128)S(1)} %get-tuple-element.9, bf16[1024,3072]{1,0:T(8,128)(2,1)} %fusion.6, bf16[768,3072]{1,0:T(8,128)(2,1)} %param.12, f32[1024]{0:T(1024)S(1)} %broadcast_multiply_fusion.2, f32[1024]{0:T(1024)S(1)} %div.51, f32[16,768]{1,0:T(8,128)S(1)} %bitcast_multiply_fusion.1, ...), kind=kOutput, calls=%fused_computation.21 | convolution fusion | flops 4838916096 | bytes 15797248 | tf_op jit(solution)/shard_map/dot_general | solution.py:67
  210.9 226.4 %reduce-scatter.4.cloned.1.call-done = f32[24,1536]{1,0:T(8,128)} async-done(((f32[3072,1536]{1,0:T(8,128)}), f32[24,1536]{1,0:T(8,128)}) %reduce-scatter.4.cloned.1.call-update) | async-done | bytes 147472
  437.3 1.2 copy.24
  438.5 0.1 broadcast_multiply_fusion
  438.6 0.9 copy.18
  (15 shorter events, 0.2 us)
Async XLA Ops:
  53.8 4.9 %copy-start.1 = (f32[16,64]{1,0:T(8,128)S(1)}, f32[16,64]{1,0:T(8,128)}, u32[]{:S(2)}) copy-start(f32[16,64]{1,0:T(8,128)} %param.21) | copy-start | bytes 12292
  53.8 5.1 %copy-start.3 = (bf16[1024,768]{1,0:T(8,128)(2,1)S(1)}, bf16[1024,768]{1,0:T(8,128)(2,1)}, u32[]{:S(2)}) copy-start(bf16[1024,768]{1,0:T(8,128)(2,1)} %param.11) | copy-start | bytes 4718596
  53.8 72.5 %all-to-all-start.1 = ((bf16[16,192,768]{2,1,0:T(8,128)(2,1)}), bf16[16,192,768]{2,1,0:T(8,128)(2,1)}, u32[]{:S(2)}, u32[]{:S(2)}) async-start(bf16[16,192,768]{2,1,0:T(8,128)(2,1)} %bitcast.68), calls=%async_computation.1 | async-start | bytes 9437184 | tf_op jit(solution)/shard_map/all_to_all | solution.py:49
  58.6 378.8 %reduce-scatter.4.cloned.1.call-start = ((), (), s32[]{:S(2)}) async-start(), calls=%async_computation.3 | async-start | bytes 19021824
  58.9 7.1 %copy-start.4 = (bf16[1024,768]{1,0:T(8,128)(2,1)S(1)}, bf16[1024,768]{1,0:T(8,128)(2,1)}, u32[]{:S(2)}) copy-start(bf16[1024,768]{1,0:T(8,128)(2,1)} %param.11) | copy-start | bytes 4718596
  58.9 7.1 %copy-start.6 = (f32[3072]{0:T(1024)S(1)}, f32[3072]{0:T(1024)}, u32[]{:S(2)}) copy-start(f32[3072]{0:T(1024)} %param.13) | copy-start | bytes 36868
  58.9 7.1 %copy-start.7 = (f32[768]{0:T(1024)S(1)}, f32[768]{0:T(1024)}, u32[]{:S(2)}) copy-start(f32[768]{0:T(1024)} %param.15) | copy-start | bytes 9220
  66.0 13.9 %copy-start.8 = (f32[1024,3072]{1,0:T(8,128)}, f32[1024,3072]{1,0:T(8,128)S(1)}, u32[]{:S(2)}) copy-start(f32[1024,3072]{1,0:T(8,128)S(1)} %fusion.25) | copy-start | bytes 37748740
  66.0 14.4 %copy-start = (f32[768]{0:T(1024)S(1)}, f32[768]{0:T(1024)}, u32[]{:S(2)}) copy-start(f32[768]{0:T(1024)} %param.16) | copy-start | bytes 9220
  66.0 14.4 %copy-start.2 = (f32[768]{0:T(1024)S(1)}, f32[768]{0:T(1024)}, u32[]{:S(2)}) copy-start(f32[768]{0:T(1024)} %param.17) | copy-start | bytes 9220
  158.6 9.3 %copy-start.5 = (bf16[1024,768]{1,0:T(8,128)(2,1)S(1)}, bf16[1024,768]{1,0:T(8,128)(2,1)}, u32[]{:S(2)}) copy-start(bf16[1024,768]{1,0:T(8,128)(2,1)} %param.11) | copy-start | bytes 4718596
Sparse Core Ops, SparseCore 0:
  201.4 235.9 reduce-scatter.3
where the time goes:
time: 447 us; the launch traced here: 446 us
  waiting for transfers between devices  272 us (61%)
  matrix products  68.7 us (15%)
  local copies, waits for them, and re-layouts  54.5 us (12%)
  other arithmetic  17 us (4%)
  blocking collectives  15.3 us (3%)
  between operations  14.3 us (3%)
  starting transfers between devices  4.93 us (1%)
    unnamed x2, waiting for transfers between devices  226 us
    all_to_all x1, waiting for transfers between devices, body(): lax.all_to_all(fetched, 'index', split_axis=0, concat_axis=0, tiled=True)  45.1 us
    unnamed x22, local copies, waits for them, and re-layouts  21.3 us
    gather x1, local copies, waits for them, and re-layouts, body(): slab[arrived.reshape(shards * capacity)].reshape(shards, capacity, width)  18.2 us
    dot_general x1, matrix products, body(): hid_grad = jnp.dot(out_grad, w_out.T, preferred_element_type=jnp.float32)  16.5 us
    all_to_all x1, blocking collectives, body(): lax.all_to_all(wanted.reshape(shards, capacity), 'index', split_axis=0, c...  15.3 us
    dot_general x1, matrix products, body(): jnp.dot(hidden, w_out, preferred_element_type=jnp.float32)  13.9 us
    dot_general x1, matrix products, body(): jnp.dot(pre_grad, w_in.T, preferred_element_type=jnp.float32)  9.68 us
  transfers between devices with their start and end apart: 2, of which 2 were waited for; matrix products, arithmetic and copies ran while one was open for 7% of the time, Pallas kernels for 0%

commit v1 on v0

--- a/solution.py
+++ b/solution.py
@@ -5,6 +5,50 @@
 
 loss_scale = 256.0
 norm_eps = 1e-12
+every = ("query", "index")
+
+
+def shifted(value, core, along_y):
+    pairs = []
+    for query in range(8):
+        y, c = query // 2, query % 2
+        to = ((y + along_y) % 4) * 2 + (c + core) % 2
+        pairs += [(query * 16 + i, to * 16 + i) for i in range(16)]
+    return lax.ppermute(value, every, pairs)
+
+
+def pair_sum(part):
+    cols = part.shape[1]
+    core = lax.axis_index("query") % 2
+    whole = part.reshape(4, 2, 16, 24, cols)
+    away = lax.dynamic_index_in_dim(whole, 1 - core, 1, keepdims=False).astype(jnp.bfloat16)
+    kept = lax.dynamic_index_in_dim(whole, core, 1, keepdims=False)
+    return kept + shifted(away, 1, 0).astype(jnp.float32)
+
+
+def over_y(value):
+    y = lax.axis_index("query") // 2
+    total = lax.dynamic_index_in_dim(value, y, 0, keepdims=False)
+    got = []
+    for step in (1, 3, 2):
+        away = lax.dynamic_index_in_dim(value, (y + step) % 4, 0, keepdims=False)
+        got.append(shifted(away.astype(jnp.bfloat16), 0, step))
+    for piece in got:
+        total = total + piece.astype(jnp.float32)
+    return total
+
+
+def over_index(value):
+    came = lax.all_to_all(value.astype(jnp.bfloat16), "index", 0, 0, tiled=True)
+    return jnp.sum(came.astype(jnp.float32), axis=0)
+
+
+def summed_rows(part):
+    chip = pair_sum(part)
+    half = chip.shape[-1] // 2
+    left = over_index(over_y(chip[..., :half]))
+    right = over_y(over_index(chip[..., half:].transpose(1, 0, 2, 3)))
+    return jnp.concatenate([left, right], axis=1)
 
 
 def gelu_tanh(value):
@@ -72,12 +116,7 @@
     second = lax.dot_general(
         hidden, out_grad, (((0,), (0,)), ((), ())), preferred_element_type=jnp.float32
     )
-    summed = lax.psum_scatter(
-        jnp.concatenate([first, second], axis=1),
-        ("query", "index"),
-        scatter_dimension=0,
-        tiled=True,
-    )
+    summed = jnp.concatenate([summed_rows(first), summed_rows(second)], axis=1)
     return (token_grads, summed / devices)
 
 

time: 447 us -> 288 us (0.64)
  waiting for transfers between devices: 272 us -> 79.4 us
  starting transfers between devices: 4.93 us -> 41 us
  between operations: 14.3 us -> 1.44 us
  other arithmetic: 17 us -> 25 us
    unnamed x2 -> x0, waiting for transfers between devices: 226 us -> none
    all_to_all x0 -> x4, waiting for transfers between devices: none -> 21.6 us  [over_index(): came = lax.all_to_all(value.astype(jnp.bfloat16), 'index', 0, 0, tiled=True)]
    ppermute x0 -> x14, starting transfers between devices: none -> 18.1 us  [shifted(): return lax.ppermute(value, every, pairs)]
    all_to_all x0 -> x4, starting transfers between devices: none -> 17.7 us  [over_index(): came = lax.all_to_all(value.astype(jnp.bfloat16), 'index', 0, 0, tiled=True)]
    unnamed x22 -> x37, local copies, waits for them, and re-layouts: 21.3 us -> 8.11 us
    ppermute x0 -> x14, waiting for transfers between devices: none -> 12.4 us  [shifted(): return lax.ppermute(value, every, pairs)]
    convert_element_type x0 -> x8, local copies, waits for them, and re-layouts: none -> 11 us  [the longest x2 5.66 us: over_index(): came = lax.all_to_all(value.astype(jnp.bfloat16), 'index', 0, 0, tiled=True)]
    concatenate x1 -> x0, other arithmetic: 7.14 us -> none  [body(): jnp.concatenate([first, second], axis=1)]
  transfers between devices with their start and end apart: 2 -> 19, of which waited for: 2 -> 9; matrix products, arithmetic and copies ran while one was open for 7% -> 22% of each run, Pallas kernels for 0% -> 0%
where the time goes in v1:
time: 288 us; the launch traced here: 284 us
  waiting for transfers between devices  79.4 us (28%)
  matrix products  68.6 us (24%)
  local copies, waits for them, and re-layouts  52.9 us (18%)
  starting transfers between devices  41 us (14%)
  other arithmetic  25 us (9%)
  blocking collectives  15.3 us (5%)
    all_to_all x1, waiting for transfers between devices, body(): lax.all_to_all(fetched, 'index', split_axis=0, concat_axis=0, tiled=True)  45.4 us
    all_to_all x4, waiting for transfers between devices, over_index(): came = lax.all_to_all(value.astype(jnp.bfloat16), 'index', 0, 0, tiled=True)  21.6 us
    gather x1, local copies, waits for them, and re-layouts, body(): slab[arrived.reshape(shards * capacity)].reshape(shards, capacity, width)  18.2 us
    ppermute x14, starting transfers between devices, shifted(): return lax.ppermute(value, every, pairs)  18.1 us
    all_to_all x4, starting transfers between devices, over_index(): came = lax.all_to_all(value.astype(jnp.bfloat16), 'index', 0, 0, tiled=True)  17.7 us
    all_to_all x1, blocking collectives, body(): lax.all_to_all(wanted.reshape(shards, capacity), 'index', split_axis=0, c...  15.3 us
    dot_general x1, matrix products, body(): hid_grad = jnp.dot(out_grad, w_out.T, preferred_element_type=jnp.float32)  14.5 us
    dot_general x1, matrix products, body(): jnp.dot(hidden, w_out, preferred_element_type=jnp.float32)  13.9 us
  transfers between devices with their start and end apart: 19, of which 9 were waited for; matrix products, arithmetic and copies ran while one was open for 22% of the time, Pallas kernels for 0%

profile of v1, /device:TPU:0, one launch (start us, length us, event | category | flops | bytes accessed | tf_op | source)
XLA Modules:
  0.0 283.5 jit_solution(6966012331376967246)
XLA Ops:
  0.6 0.5 broadcast.194
  1.1 1.4 fusion.49
  2.6 0.8 eq.44
  3.4 4.5 %reduce-window.6 = s32[16,8,128]{2,1,0:T(8,128)S(1)} reduce-window(s32[16,8,128]{2,1,0:T(8,128)S(1)} %fusion.32, s32[]{:T(128)} %constant.154.clone.1), window={size=1x1x128 pad=0_0x0_0x127_0}, to_apply=%region_3.4 | reduce-window | flops 2080768 | bytes 131076 | tf_op jit(solution)/shard_map/reduce-window
  8.4 0.8 reshape.191
  9.2 4.3 %scatter_custom_fusion = s32[3072]{0:T(1024)S(1)} fusion(s32[1024]{0:T(1024)S(1)} %bitcast.164, s32[1024]{0:T(1024)S(1)} %reshape.191, s32[]{:T(128)} %constant.154.clone.1), kind=kCustom, calls=%fused_computation.99 | custom fusion | bytes 12292 | tf_op jit(solution)/shard_map/scatter | solution.py:88
  13.6 15.3 %all_to_all.34 = s32[16,1,192]{2,1,0:T(1,128)S(1)} all-to-all(s32[16,1,192]{2,1,0:T(1,128)S(1)} %all_to_all.21), channel_id=1, replica_groups=mesh['query'=8,'index'=16] {'index'}, dimensions={0} | all-to-all | bytes 24576 | tf_op jit(solution)/shard_map/all_to_all | solution.py:89
  29.1 18.2 %gather_fusion = bf16[3072,768]{1,0:T(8,128)(2,1)} fusion(bf16[4096,768]{1,0:T(8,128)(2,1)} %param.18, s32[3072]{0:T(1024)S(1)} %broadcast_clamp_fusion), kind=kCustom, calls=%fused_computation | custom fusion | bytes 9449472 | tf_op jit(solution)/shard_map/gather | solution.py:92
  47.3 5.2 %all-to-all-start.1 = ((bf16[16,192,768]{2,1,0:T(8,128)(2,1)}), bf16[16,192,768]{2,1,0:T(8,128)(2,1)}, u32[]{:S(2)}, u32[]{:S(2)}) async-start(bf16[16,192,768]{2,1,0:T(8,128)(2,1)} %bitcast.148), calls=%async_computation.1 | async-start | bytes 9437184 | tf_op jit(solution)/shard_map/all_to_all | solution.py:93
  52.7 7.0 %fusion.51 = f32[1024,3072]{1,0:T(8,128)S(1)} fusion(bf16[1024,768]{1,0:T(8,128)(2,1)S(1)} %copy-done.11, bf16[768,3072]{1,0:T(8,128)(2,1)} %param.12), kind=kOutput, calls=%fused_computation.113 | convolution fusion | flops 4831838208 | bytes 18874368 | tf_op jit(solution)/shard_map/dot_general | solution.py:75
  59.8 13.9 %fusion.50 = (f32[1024]{0:T(1024)S(1)}, f32[1024,768]{1,0:T(8,128)S(1)}) fusion(f32[768]{0:T(1024)S(1)} %copy-done.15, bf16[3072,768]{1,0:T(8,128)(2,1)} %param.14, f32[1024,3072]{1,0:T(8,128)S(1)} %fusion.51, f32[3072]{0:T(1024)S(1)} %copy-done.14, bf16[1024,768]{1,0:T(8,128)(2,1)S(1)} %copy-done.12), kind=kOutput, calls=%fused_computation.112 | convolution fusion | flops 4866440192 | bytes 22039552 | tf_op jit(solution)/shard_map/dot_general | solution.py:79
  74.2 0.8 bitcast_reduce_fusion
  75.0 45.4 %all-to-all-done.1 = bf16[16,192,768]{2,1,0:T(8,128)(2,1)} async-done(((bf16[16,192,768]{2,1,0:T(8,128)(2,1)}), bf16[16,192,768]{2,1,0:T(8,128)(2,1)}, u32[]{:S(2)}, u32[]{:S(2)}) %all-to-all-start.1) | async-done | bytes 4718624 | tf_op jit(solution)/shard_map/all_to_all | solution.py:93
  120.4 8.7 %gather_fusion.1 = bf16[1024,768]{1,0:T(8,128)(2,1)} fusion(bf16[3072,768]{1,0:T(8,128)(2,1)} %bitcast.8, s32[1024]{0:T(1024)S(1)} %broadcast_clamp_fusion.1), kind=kCustom, calls=%fused_computation.1 | custom fusion | bytes 3149824 | tf_op jit(solution)/shard_map/gather | solution.py:94
  129.1 2.7 fusion.33
  132.2 2.1 fusion.52
  134.4 0.6 fusion.11
  135.3 1.0 fusion.14
  136.3 14.5 %fusion.6 = bf16[1024,3072]{1,0:T(8,128)(2,1)S(1)} fusion(f32[1024,3072]{1,0:T(8,128)} %copy-done.17, f32[3072]{0:T(1024)S(1)} %copy-done.14, bf16[1024,768]{1,0:T(8,128)(2,1)S(1)} %fusion.14, bf16[3072,768]{1,0:T(8,128)(2,1)} %param.14), kind=kOutput, calls=%fused_computation.11 | convolution fusion | flops 4897898496 | bytes 25178112 | tf_op jit(solution)/shard_map/dot_general | solution.py:107
  150.9 13.3 %fusion.48 = f32[3072,768]{1,0:T(8,128)S(1)} fusion(bf16[1024,768]{1,0:T(8,128)(2,1)S(1)} %fusion.14, f32[1024,3072]{1,0:T(8,128)} %copy-done.17, f32[3072]{0:T(1024)S(1)} %copy-done.14), kind=kOutput, calls=%fused_computation.110 | convolution fusion | flops 4863295488 | bytes 23605248 | tf_op jit(solution)/shard_map/dot_general | solution.py:116
  164.2 1.7 fusion.13
  166.1 0.6 copy-done.13
  166.7 5.4 %fusion.53 = f32[3072,768]{1,0:T(8,128)S(1)} fusion(bf16[1024,3072]{1,0:T(8,128)(2,1)S(1)} %fusion.6, bf16[1024,768]{1,0:T(8,128)(2,1)S(1)} %copy-done.13), kind=kOutput, calls=%fused_computation.115 | convolution fusion | flops 4831838208 | bytes 17301504 | tf_op jit(solution)/shard_map/dot_general | solution.py:113
  172.1 3.6 %copy-done.4 = f32[3072,768]{1,0:T(8,128)} copy-done((f32[3072,768]{1,0:T(8,128)}, f32[3072,768]{1,0:T(8,128)S(1)}, u32[]{:S(2)}) %copy-start.4) | copy-done | bytes 9437208
  175.7 1.7 fusion.12
  177.4 3.8 %bitcast_add_fusion = f32[4,16,24,768]{3,2,0,1:T(8,128)S(1)} fusion(bf16[4,16,24,768]{3,2,0,1:T(8,128)(2,1)} %collective-permute-done.7, f32[4,2,16,24,768]{4,3,2,1,0:T(8,128)} %bitcast.154, s32[]{:T(128)S(6)} %select_n.105), kind=kLoop, calls=%fused_computation.15 | loop fusion | flops 2359296 | bytes 11796484 | tf_op jit(solution)/shard_map/add | solution.py:26
  181.4 0.9 fusion.27
  182.3 3.2 %collective-permute-start.10 = (bf16[16,24,384]{2,1,0:T(8,128)(2,1)S(1)}, bf16[16,24,384]{2,1,0:T(8,128)(2,1)S(1)}, u32[]{:S(2)}, u32[]{:S(2)}) collective-permute-start(bf16[16,24,384]{2,1,0:T(8,128)(2,1)S(1)} %get-tuple-element.8), channel_id=1, source_target_pairs={{0,64},{1,65},{2,66},{3,67},{4,68},{5,69},{6,70},{7,71},{8,72},{9,... | collective-permute-start | bytes 884744 | tf_op jit(solution)/shard_map/ppermute | solution.py:17
  185.5 1.1 collective-permute-start.9
  186.5 1.0 collective-permute-start.8
  187.5 2.4 bitcast_add_fusion.1
  190.1 1.9 copy-done.1
  192.0 1.0 fusion.25
  193.1 0.7 copy-done.3
  193.8 1.1 collective-permute-start.3
  194.8 2.3 collective-permute-start.2
  197.1 0.7 copy-done.7
  197.8 2.5 collective-permute-done.9
  200.4 2.2 fusion.19
  202.6 4.5 %all-to-all-start.4 = ((bf16[16,24,384]{2,1,0:T(8,128)(2,1)}), bf16[16,24,384]{2,1,0:T(8,128)(2,1)S(1)}, u32[]{:S(2)}, u32[]{:S(2)}) async-start(bf16[16,24,384]{2,1,0:T(8,128)(2,1)} %fusion.19), calls=%async_computation.4 | async-start | bytes 589824 | tf_op jit(solution)/shard_map/all_to_all | solution.py:42
  207.1 5.6 %collective-permute-done.2 = bf16[16,24,384]{2,1,0:T(8,128)(2,1)} collective-permute-done((bf16[16,24,384]{2,1,0:T(8,128)(2,1)}, bf16[16,24,384]{2,1,0:T(8,128)(2,1)}, u32[]{:S(2)}, u32[]{:S(2)}) %collective-permute-start.2) | collective-permute-done | bytes 294944 | tf_op jit(solution)/shard_map/ppermute | solution.py:17
  212.7 2.2 fusion.22
  214.9 1.0 all-to-all-done.4
  215.9 4.2 %all-to-all-start.2 = ((bf16[16,24,384]{2,1,0:T(8,128)(2,1)}), bf16[16,24,384]{2,1,0:T(8,128)(2,1)}, u32[]{:S(2)}, u32[]{:S(2)}) async-start(bf16[16,24,384]{2,1,0:T(8,128)(2,1)} %fusion.22), calls=%async_computation.2 | async-start | bytes 589824 | tf_op jit(solution)/shard_map/all_to_all | solution.py:42
  220.1 2.8 fusion.16
  222.9 6.1 %all-to-all-done.2 = bf16[16,24,384]{2,1,0:T(8,128)(2,1)} async-done(((bf16[16,24,384]{2,1,0:T(8,128)(2,1)}), bf16[16,24,384]{2,1,0:T(8,128)(2,1)}, u32[]{:S(2)}, u32[]{:S(2)}) %all-to-all-start.2) | async-done | bytes 294944 | tf_op jit(solution)/shard_map/all_to_all | solution.py:42
  229.0 4.4 %all-to-all-start.5 = ((bf16[16,4,24,384]{3,2,1,0:T(8,128)(2,1)}), bf16[16,4,24,384]{3,2,1,0:T(8,128)(2,1)}, u32[]{:S(2)}, u32[]{:S(2)}) async-start(bf16[16,4,24,384]{3,2,1,0:T(8,128)(2,1)} %fusion.16), calls=%async_computation.5 | async-start | bytes 2359296 | tf_op jit(solution)/shard_map/all_to_all | solution.py:42
  233.4 2.8 %fusion.15 = bf16[16,4,24,384]{3,2,1,0:T(8,128)(2,1)} fusion(f32[4,16,24,768]{3,2,0,1:T(8,128)} %copy-done.1), kind=kLoop, calls=%fused_computation.37 | loop fusion | bytes 2359296 | tf_op jit(solution)/shard_map/convert_element_type | solution.py:42
  236.2 14.5 %all-to-all-done.5 = bf16[16,4,24,384]{3,2,1,0:T(8,128)(2,1)} async-done(((bf16[16,4,24,384]{3,2,1,0:T(8,128)(2,1)}), bf16[16,4,24,384]{3,2,1,0:T(8,128)(2,1)}, u32[]{:S(2)}, u32[]{:S(2)}) %all-to-all-start.5) | async-done | bytes 1179680 | tf_op jit(solution)/shard_map/all_to_all | solution.py:42
  250.7 4.6 %all-to-all-start.3 = ((bf16[16,4,24,384]{3,2,1,0:T(8,128)(2,1)}), bf16[16,4,24,384]{3,2,1,0:T(8,128)(2,1)}, u32[]{:S(2)}, u32[]{:S(2)}) async-start(bf16[16,4,24,384]{3,2,1,0:T(8,128)(2,1)} %fusion.15), calls=%async_computation.3 | async-start | bytes 2359296 | tf_op jit(solution)/shard_map/all_to_all | solution.py:42
  255.3 9.7 %add_convert_fusion = bf16[1024,768]{1,0:T(8,128)(2,1)} fusion(f32[1024,768]{1,0:T(8,128)S(1)} %get-tuple-element.17, bf16[1024,3072]{1,0:T(8,128)(2,1)} %copy-done.16, bf16[768,3072]{1,0:T(8,128)(2,1)} %param.12, f32[1024]{0:T(1024)S(1)} %broadcast_multiply_fusion.1, f32[1024]{0:T(1024)S(1)} %div.62, f32[16,768]{1,0:T(8,128)S(1)} %bitcast_multiply_fusion.1, ...), kind=kOutput, calls=%fused_computation.24 | convolution fusion | flops 4838916096 | bytes 15797248 | tf_op jit(solution)/shard_map/dot_general | solution.py:111
  265.0 1.0 convert_reduce_fusion.3
  266.1 1.4 convert_reduce_fusion
  267.5 3.1 %collective-permute-start.13 = (bf16[24,384]{1,0:T(8,128)(2,1)S(1)}, bf16[24,384]{1,0:T(8,128)(2,1)S(1)}, u32[]{:S(2)}, u32[]{:S(2)}) collective-permute-start(bf16[24,384]{1,0:T(8,128)(2,1)S(1)} %get-tuple-element.14), channel_id=1, source_target_pairs={{0,64},{1,65},{2,66},{3,67},{4,68},{5,69},{6,70},{7,71},{8,72},{9,... | collective-permute-start | bytes 55304 | tf_op jit(solution)/shard_map/ppermute | solution.py:17
  270.6 1.1 collective-permute-start.12
  271.7 0.9 collective-permute-start.11
  272.6 1.4 convert_reduce_fusion.1
  274.1 2.2 collective-permute-start.6
  276.3 1.3 collective-permute-start.5
  277.6 0.7 collective-permute-start.4
  278.3 1.1 collective-permute-done.6
  279.4 0.6 collective-permute-done.5
  280.0 2.5 collective-permute-done.4
  282.6 0.7 maximum_multiply_fusion
  (81 shorter events, 2.9 us)
Async XLA Ops:
  47.3 5.3 %copy-start.9 = (f32[16,64]{1,0:T(8,128)S(1)}, f32[16,64]{1,0:T(8,128)}, u32[]{:S(2)}) copy-start(f32[16,64]{1,0:T(8,128)} %param.21) | copy-start | bytes 12292
  47.3 5.4 %copy-start.11 = (bf16[1024,768]{1,0:T(8,128)(2,1)S(1)}, bf16[1024,768]{1,0:T(8,128)(2,1)}, u32[]{:S(2)}) copy-start(bf16[1024,768]{1,0:T(8,128)(2,1)} %param.11) | copy-start | bytes 4718596
  47.3 73.1 %all-to-all-start.1 = ((bf16[16,192,768]{2,1,0:T(8,128)(2,1)}), bf16[16,192,768]{2,1,0:T(8,128)(2,1)}, u32[]{:S(2)}, u32[]{:S(2)}) async-start(bf16[16,192,768]{2,1,0:T(8,128)(2,1)} %bitcast.148), calls=%async_computation.1 | async-start | bytes 9437184 | tf_op jit(solution)/shard_map/all_to_all | solution.py:93
  52.7 7.1 %copy-start.12 = (bf16[1024,768]{1,0:T(8,128)(2,1)S(1)}, bf16[1024,768]{1,0:T(8,128)(2,1)}, u32[]{:S(2)}) copy-start(bf16[1024,768]{1,0:T(8,128)(2,1)} %param.11) | copy-start | bytes 4718596
  52.7 7.1 %copy-start.14 = (f32[3072]{0:T(1024)S(1)}, f32[3072]{0:T(1024)}, u32[]{:S(2)}) copy-start(f32[3072]{0:T(1024)} %param.13) | copy-start | bytes 36868
  52.7 7.1 %copy-start.15 = (f32[768]{0:T(1024)S(1)}, f32[768]{0:T(1024)}, u32[]{:S(2)}) copy-start(f32[768]{0:T(1024)} %param.15) | copy-start | bytes 9220
  59.8 13.9 %copy-start.17 = (f32[1024,3072]{1,0:T(8,128)}, f32[1024,3072]{1,0:T(8,128)S(1)}, u32[]{:S(2)}) copy-start(f32[1024,3072]{1,0:T(8,128)S(1)} %fusion.51) | copy-start | bytes 37748740
  59.8 14.4 %copy-start.8 = (f32[768]{0:T(1024)S(1)}, f32[768]{0:T(1024)}, u32[]{:S(2)}) copy-start(f32[768]{0:T(1024)} %param.16) | copy-start | bytes 9220
  59.8 14.4 %copy-start.10 = (f32[768]{0:T(1024)S(1)}, f32[768]{0:T(1024)}, u32[]{:S(2)}) copy-start(f32[768]{0:T(1024)} %param.17) | copy-start | bytes 9220
  150.9 15.2 %copy-start.16 = (bf16[1024,3072]{1,0:T(8,128)(2,1)}, bf16[1024,3072]{1,0:T(8,128)(2,1)S(1)}, u32[]{:S(2)}) copy-start(bf16[1024,3072]{1,0:T(8,128)(2,1)S(1)} %fusion.6) | copy-start | bytes 18874372
  164.2 7.9 %copy-start.6 = (f32[3072,768]{1,0:T(8,128)}, f32[3072,768]{1,0:T(8,128)S(1)}, u32[]{:S(2)}) copy-start(f32[3072,768]{1,0:T(8,128)S(1)} %fusion.48) | copy-start | bytes 28311556
  164.2 2.5 copy-start.13
  165.9 11.5 %collective-permute-start.7 = (bf16[4,16,24,768]{3,2,0,1:T(8,128)(2,1)}, bf16[4,16,24,768]{3,2,0,1:T(8,128)(2,1)}, u32[]{:S(2)}, u32[]{:S(2)}) collective-permute-start(bf16[4,16,24,768]{3,2,0,1:T(8,128)(2,1)} %fusion.13), channel_id=1, source_target_pairs={{0,16},{1,17},{2,18},{3,19},{4,20},{5,21},{6,22},{7,23},{8,24},{9,... | collective-permute-start | bytes 7077896 | tf_op jit(solution)/shard_map/ppermute | solution.py:17
  172.1 3.6 %copy-start.4 = (f32[3072,768]{1,0:T(8,128)}, f32[3072,768]{1,0:T(8,128)S(1)}, u32[]{:S(2)}) copy-start(f32[3072,768]{1,0:T(8,128)S(1)} %fusion.53) | copy-start | bytes 28311556
  177.4 10.1 %collective-permute-start = (bf16[4,16,24,768]{3,2,0,1:T(8,128)(2,1)}, bf16[4,16,24,768]{3,2,0,1:T(8,128)(2,1)}, u32[]{:S(2)}, u32[]{:S(2)}) collective-permute-start(bf16[4,16,24,768]{3,2,0,1:T(8,128)(2,1)} %fusion.12), channel_id=1, source_target_pairs={{0,16},{1,17},{2,18},{3,19},{4,20},{5,21},{6,22},{7,23},{8,24},{9,... | collective-permute-start | bytes 7077896 | tf_op jit(solution)/shard_map/ppermute | solution.py:17
  177.4 10.1 %copy-start.5 = (f32[3072,768]{1,0:T(8,128)S(1)}, f32[3072,768]{1,0:T(8,128)}, u32[]{:S(2)}) copy-start(f32[3072,768]{1,0:T(8,128)} %copy-done.4) | copy-start | bytes 28311556
  181.2 8.7 %copy-start = (f32[4,16,24,768]{3,2,0,1:T(8,128)}, f32[4,16,24,768]{3,2,0,1:T(8,128)S(1)}, u32[]{:S(2)}) copy-start(f32[4,16,24,768]{3,2,0,1:T(8,128)S(1)} %bitcast_add_fusion) | copy-start | bytes 14155780
  181.4 6.1 %copy-start.2 = (f32[4,16,24,384]{3,2,0,1:T(8,128)}, f32[4,16,24,384]{3,2,0,1:T(8,128)S(1)}, u32[]{:S(2)}) copy-start(f32[4,16,24,384]{3,2,0,1:T(8,128)S(1)} %slice.34) | copy-start | bytes 7077892
  182.3 14.8 %collective-permute-start.10 = (bf16[16,24,384]{2,1,0:T(8,128)(2,1)S(1)}, bf16[16,24,384]{2,1,0:T(8,128)(2,1)S(1)}, u32[]{:S(2)}, u32[]{:S(2)}) collective-permute-start(bf16[16,24,384]{2,1,0:T(8,128)(2,1)S(1)} %get-tuple-element.8), channel_id=1, source_target_pairs={{0,64},{1,65},{2,66},{3,67},{4,68},{5,69},{6,70},{7,71},{8,72},{9,... | collective-permute-start | bytes 884744 | tf_op jit(solution)/shard_map/ppermute | solution.py:17
  185.5 14.9 %collective-permute-start.9 = (bf16[16,24,384]{2,1,0:T(8,128)(2,1)}, bf16[16,24,384]{2,1,0:T(8,128)(2,1)}, u32[]{:S(2)}, u32[]{:S(2)}) collective-permute-start(bf16[16,24,384]{2,1,0:T(8,128)(2,1)} %get-tuple-element.9), channel_id=1, source_target_pairs={{0,96},{1,97},{2,98},{3,99},{4,100},{5,101},{6,102},{7,103},{8,104... | collective-permute-start | bytes 884744 | tf_op jit(solution)/shard_map/ppermute | solution.py:17
  186.5 13.9 %collective-permute-start.8 = (bf16[16,24,384]{2,1,0:T(8,128)(2,1)S(1)}, bf16[16,24,384]{2,1,0:T(8,128)(2,1)}, u32[]{:S(2)}, u32[]{:S(2)}) collective-permute-start(bf16[16,24,384]{2,1,0:T(8,128)(2,1)S(1)} %get-tuple-element.7), channel_id=1, source_target_pairs={{0,32},{1,33},{2,34},{3,35},{4,36},{5,37},{6,38},{7,39},{8,40},{9,... | collective-permute-start | bytes 884744 | tf_op jit(solution)/shard_map/ppermute | solution.py:17
  189.9 2.1 copy-start.1
  192.0 1.7 copy-start.3
  193.8 13.3 %collective-permute-start.3 = (bf16[16,24,384]{2,1,0:T(8,128)(2,1)}, bf16[16,24,384]{2,1,0:T(8,128)(2,1)}, u32[]{:S(2)}, u32[]{:S(2)}) collective-permute-start(bf16[16,24,384]{2,1,0:T(8,128)(2,1)} %get-tuple-element.5), channel_id=1, source_target_pairs={{0,64},{1,65},{2,66},{3,67},{4,68},{5,69},{6,70},{7,71},{8,72},{9,... | collective-permute-start | bytes 884744 | tf_op jit(solution)/shard_map/ppermute | solution.py:17
  194.8 17.8 %collective-permute-start.2 = (bf16[16,24,384]{2,1,0:T(8,128)(2,1)}, bf16[16,24,384]{2,1,0:T(8,128)(2,1)}, u32[]{:S(2)}, u32[]{:S(2)}) collective-permute-start(bf16[16,24,384]{2,1,0:T(8,128)(2,1)} %get-tuple-element.6), channel_id=1, source_target_pairs={{0,96},{1,97},{2,98},{3,99},{4,100},{5,101},{6,102},{7,103},{8,104... | collective-permute-start | bytes 884744 | tf_op jit(solution)/shard_map/ppermute | solution.py:17
  197.1 0.7 copy-start.7
  197.8 14.8 %collective-permute-start.1 = (bf16[16,24,384]{2,1,0:T(8,128)(2,1)}, bf16[16,24,384]{2,1,0:T(8,128)(2,1)}, u32[]{:S(2)}, u32[]{:S(2)}) collective-permute-start(bf16[16,24,384]{2,1,0:T(8,128)(2,1)} %get-tuple-element.4), channel_id=1, source_target_pairs={{0,32},{1,33},{2,34},{3,35},{4,36},{5,37},{6,38},{7,39},{8,40},{9,... | collective-permute-start | bytes 884744 | tf_op jit(solution)/shard_map/ppermute | solution.py:17
  202.6 13.3 %all-to-all-start.4 = ((bf16[16,24,384]{2,1,0:T(8,128)(2,1)}), bf16[16,24,384]{2,1,0:T(8,128)(2,1)S(1)}, u32[]{:S(2)}, u32[]{:S(2)}) async-start(bf16[16,24,384]{2,1,0:T(8,128)(2,1)} %fusion.19), calls=%async_computation.4 | async-start | bytes 589824 | tf_op jit(solution)/shard_map/all_to_all | solution.py:42
  215.9 13.1 %all-to-all-start.2 = ((bf16[16,24,384]{2,1,0:T(8,128)(2,1)}), bf16[16,24,384]{2,1,0:T(8,128)(2,1)}, u32[]{:S(2)}, u32[]{:S(2)}) async-start(bf16[16,24,384]{2,1,0:T(8,128)(2,1)} %fusion.22), calls=%async_computation.2 | async-start | bytes 589824 | tf_op jit(solution)/shard_map/all_to_all | solution.py:42
  229.0 21.7 %all-to-all-start.5 = ((bf16[16,4,24,384]{3,2,1,0:T(8,128)(2,1)}), bf16[16,4,24,384]{3,2,1,0:T(8,128)(2,1)}, u32[]{:S(2)}, u32[]{:S(2)}) async-start(bf16[16,4,24,384]{3,2,1,0:T(8,128)(2,1)} %fusion.16), calls=%async_computation.5 | async-start | bytes 2359296 | tf_op jit(solution)/shard_map/all_to_all | solution.py:42
  250.7 22.0 %all-to-all-start.3 = ((bf16[16,4,24,384]{3,2,1,0:T(8,128)(2,1)}), bf16[16,4,24,384]{3,2,1,0:T(8,128)(2,1)}, u32[]{:S(2)}, u32[]{:S(2)}) async-start(bf16[16,4,24,384]{3,2,1,0:T(8,128)(2,1)} %fusion.15), calls=%async_computation.3 | async-start | bytes 2359296 | tf_op jit(solution)/shard_map/all_to_all | solution.py:42
  267.5 10.1 %collective-permute-start.13 = (bf16[24,384]{1,0:T(8,128)(2,1)S(1)}, bf16[24,384]{1,0:T(8,128)(2,1)S(1)}, u32[]{:S(2)}, u32[]{:S(2)}) collective-permute-start(bf16[24,384]{1,0:T(8,128)(2,1)S(1)} %get-tuple-element.14), channel_id=1, source_target_pairs={{0,64},{1,65},{2,66},{3,67},{4,68},{5,69},{6,70},{7,71},{8,72},{9,... | collective-permute-start | bytes 55304 | tf_op jit(solution)/shard_map/ppermute | solution.py:17
  270.6 7.7 %collective-permute-start.12 = (bf16[24,384]{1,0:T(8,128)(2,1)S(1)}, bf16[24,384]{1,0:T(8,128)(2,1)S(1)}, u32[]{:S(2)}, u32[]{:S(2)}) collective-permute-start(bf16[24,384]{1,0:T(8,128)(2,1)S(1)} %get-tuple-element.15), channel_id=1, source_target_pairs={{0,96},{1,97},{2,98},{3,99},{4,100},{5,101},{6,102},{7,103},{8,104... | collective-permute-start | bytes 55304 | tf_op jit(solution)/shard_map/ppermute | solution.py:17
  271.7 6.6 %collective-permute-start.11 = (bf16[24,384]{1,0:T(8,128)(2,1)S(1)}, bf16[24,384]{1,0:T(8,128)(2,1)S(1)}, u32[]{:S(2)}, u32[]{:S(2)}) collective-permute-start(bf16[24,384]{1,0:T(8,128)(2,1)S(1)} %get-tuple-element.13), channel_id=1, source_target_pairs={{0,32},{1,33},{2,34},{3,35},{4,36},{5,37},{6,38},{7,39},{8,40},{9,... | collective-permute-start | bytes 55304 | tf_op jit(solution)/shard_map/ppermute | solution.py:17
  274.1 5.3 %collective-permute-start.6 = (bf16[24,384]{1,0:T(8,128)(2,1)S(1)}, bf16[24,384]{1,0:T(8,128)(2,1)S(1)}, u32[]{:S(2)}, u32[]{:S(2)}) collective-permute-start(bf16[24,384]{1,0:T(8,128)(2,1)S(1)} %get-tuple-element.11), channel_id=1, source_target_pairs={{0,64},{1,65},{2,66},{3,67},{4,68},{5,69},{6,70},{7,71},{8,72},{9,... | collective-permute-start | bytes 55304 | tf_op jit(solution)/shard_map/ppermute | solution.py:17
  276.3 3.8 %collective-permute-start.5 = (bf16[24,384]{1,0:T(8,128)(2,1)S(1)}, bf16[24,384]{1,0:T(8,128)(2,1)S(1)}, u32[]{:S(2)}, u32[]{:S(2)}) collective-permute-start(bf16[24,384]{1,0:T(8,128)(2,1)S(1)} %get-tuple-element.12), channel_id=1, source_target_pairs={{0,96},{1,97},{2,98},{3,99},{4,100},{5,101},{6,102},{7,103},{8,104... | collective-permute-start | bytes 55304 | tf_op jit(solution)/shard_map/ppermute | solution.py:17
  277.6 5.0 %collective-permute-start.4 = (bf16[24,384]{1,0:T(8,128)(2,1)S(1)}, bf16[24,384]{1,0:T(8,128)(2,1)S(1)}, u32[]{:S(2)}, u32[]{:S(2)}) collective-permute-start(bf16[24,384]{1,0:T(8,128)(2,1)S(1)} %get-tuple-element.10), channel_id=1, source_target_pairs={{0,32},{1,33},{2,34},{3,35},{4,36},{5,37},{6,38},{7,39},{8,40},{9,... | collective-permute-start | bytes 55304 | tf_op jit(solution)/shard_map/ppermute | solution.py:17

commit v2 on v0

v2 whole, which is shorter than its diff:
```python
import jax
import jax.numpy as jnp
from jax import lax
from jax.experimental import pallas as pl
from jax.experimental.pallas import tpu as pltpu
from jax.sharding import PartitionSpec as P

loss_scale = 256.0
norm_eps = 1e-12
every = ("query", "index")
MIB = 1 << 20
low = -1e30
params = pltpu.CompilerParams(vmem_limit_bytes=56 * MIB)
light = pl.CostEstimate(flops=1000, bytes_accessed=1000, transcendentals=0)
anywhere = pl.BlockSpec(memory_space=pl.ANY)


def halves(value):
    first = value.astype(jnp.bfloat16)
    return first, (value - first.astype(jnp.float32)).astype(jnp.bfloat16)


def dot_rows(left, right):
    return lax.dot_general(left, right, (((1,), (1,)), ((), ())), preferred_element_type=jnp.float32)


def columns_dot(left, right):
    return lax.dot_general(left, right, (((0,), (0,)), ((), ())), preferred_element_type=jnp.float32)


def exchange(value):
    return lax.all_to_all(value, "index", 0, 0, tiled=True)


def shifted(value, core, along_y):
    pairs = []
    for query in range(8):
        y, c = query // 2, query % 2
        to = ((y + along_y) % 4) * 2 + (c + core) % 2
        pairs += [(query * 16 + i, to * 16 + i) for i in range(16)]
    return lax.ppermute(value, every, pairs)


def whole(*shape):
    return pl.BlockSpec(shape, lambda *_: (0,) * len(shape))


def slope(pre):
    square = pre * pre
    bend = jnp.tanh(pre * (0.7978845608028654 + 0.035677408136300125 * square))
    share = 0.5 + 0.5 * bend
    value = pre * share
    grad = share + (value - value * share) * (1.5957691216057308 + 0.21406444881780074 * square)
    return value, grad


def forward_kernel(
    tokens_ref, w_in_ref, bias_in_ref, w_out_ref, bias_out_ref, gain_ref, shift_ref, table_ref,
    hidden_ref, slope_ref, normed_ref, rstd_ref, ask_ref, resid, query,
):
    step = pl.program_id(0)

    @pl.when(step == 0)
    def _():
        resid[...] = tokens_ref[...].astype(jnp.float32) + bias_out_ref[...]

    for part in range(4):
        rows = slice(part * 256, part * 256 + 256)
        pre = jnp.dot(tokens_ref[rows, :], w_in_ref[...], preferred_element_type=jnp.float32) + bias_in_ref[...]
        value, grad = slope(pre)
        value = value.astype(jnp.bfloat16)
        hidden_ref[rows, :] = value
        slope_ref[rows, :] = grad.astype(jnp.bfloat16)
        resid[rows, :] += jnp.dot(value, w_out_ref[...], preferred_element_type=jnp.float32)

    @pl.when(step == pl.num_programs(0) - 1)
    def _():
        for q in range(16):
            rows = slice(q * 64, q * 64 + 64)
            here = resid[rows, :]
            away = here - jnp.mean(here, axis=-1, keepdims=True)
            rstd = lax.rsqrt(jnp.mean(away * away, axis=-1, keepdims=True) + norm_eps)
            normed = away * rstd
            normed_ref[rows, :] = normed
            rstd_ref[rows, :] = rstd
            query[q : q + 1, :] = (
                jnp.sum(normed, axis=0, keepdims=True) * (1 / 64) * gain_ref[...] + shift_ref[...]
            )
        upper, lower = halves(query[...])
        for to in range(16):
            ask_ref[to, :, :768] = upper
            ask_ref[to, :, 768:1536] = lower
            ask_ref[to, :, 1536:] = table_ref[...]


def forward(tokens, w_in, bias_in, w_out, bias_out, gain, shift, table):
    block = 512
    units = pl.BlockSpec((1024, block), lambda j: (0, j))
    return pl.pallas_call(
        forward_kernel,
        grid=(3072 // block,),
        in_specs=[
            whole(1024, 768),
            pl.BlockSpec((768, block), lambda j: (0, j)),
            pl.BlockSpec((1, block), lambda j: (0, j)),
            pl.BlockSpec((block, 768), lambda j: (j, 0)),
            whole(1, 768),
            whole(1, 768),
            whole(1, 768),
            whole(16, 512),
        ],
        out_specs=(units, units, whole(1024, 768), whole(1024, 1), whole(16, 16, 2048)),
        out_shape=(
            jax.ShapeDtypeStruct((1024, 3072), jnp.bfloat16),
            jax.ShapeDtypeStruct((1024, 3072), jnp.bfloat16),
            jax.ShapeDtypeStruct((1024, 768), jnp.float32),
            jax.ShapeDtypeStruct((1024, 1), jnp.float32),
            jax.ShapeDtypeStruct((16, 16, 2048), jnp.bfloat16),
        ),
        scratch_shapes=[pltpu.VMEM((1024, 768), jnp.float32), pltpu.VMEM((16, 768), jnp.float32)],
        compiler_params=params,
        cost_estimate=light,
    )(
        tokens, w_in, bias_in.reshape(1, -1), w_out, bias_out.reshape(1, -1),
        gain.reshape(1, -1), shift.reshape(1, -1), table,
    )


def score_kernel(
    me_ref, ask_ref, slab_hbm, weight_ref, share_ref, stat_ref, count, scores, slab, sems
):
    loads = []
    for block in range(8):
        rows = pl.ds(block * 512, 512)
        loads.append(pltpu.make_async_copy(slab_hbm.at[rows], slab.at[rows], sems.at[block]))
        loads[-1].start()
    me = me_ref[0].astype(jnp.float32)
    turn = (lax.broadcasted_iota(jnp.int32, (1, 512), 1) // 64).astype(jnp.float32)
    row = lax.broadcasted_iota(jnp.int32, (256, 512), 0).astype(jnp.float32)
    line = lax.broadcasted_iota(jnp.int32, (128, 512), 0).astype(jnp.float32)

    def source(s, carry):
        meta = ask_ref[s, :, 1536:].astype(jnp.float32)
        for g in range(2):
            owner, high, spot, upper, lower = [meta[2 * f + g : 2 * f + g + 1] for f in range(5)]
            key = jnp.where(owner == me, high * 8.0 + turn, -1.0)
            left = jnp.where(row == key, 1.0, 0.0).astype(jnp.bfloat16)
            hit = line == spot
            right = jnp.concatenate(
                [jnp.where(hit, 1.0, 0.0), jnp.where(hit, upper, 0.0), jnp.where(hit, lower, 0.0)], axis=0
            ).astype(jnp.bfloat16)
            out = dot_rows(left, right)
            at = pl.ds(pl.multiple_of(s * 16 + g * 8, 8), 8)
            count[:, at, :] = out[:, :128].reshape(32, 8, 128)
            share_ref[:, at, :] = (out[:, 128:256] + out[:, 256:]).reshape(32, 8, 128)
        return carry

    lax.fori_loop(0, 16, source, 0, unroll=2)
    both = jnp.concatenate(
        [ask_ref[:, :, :768].reshape(256, 768), ask_ref[:, :, 768:1536].reshape(256, 768)], axis=0
    )
    top = jnp.full((256, 128), low, jnp.float32)
    for block in range(8):
        loads[block].wait()
        got = dot_rows(both, slab[block * 512 : block * 512 + 512])
        got = got[:256] + got[256:]
        for i in range(4):
            part = got[:, i * 128 : i * 128 + 128]
            scores[block * 4 + i] = part
            top = jnp.maximum(top, jnp.where(count[block * 4 + i] > 0, part, low))
    top = jnp.max(top, axis=1, keepdims=True)
    mass = jnp.zeros((256, 128), jnp.float32)
    for high in range(32):
        here = count[high]
        part = jnp.where(here > 0, here * jnp.exp(jnp.minimum(scores[high] - top, 0.0)), 0.0)
        mass = mass + part
        weight_ref[high] = part
    mass = jnp.sum(mass, axis=1, keepdims=True)
    lane = lax.broadcasted_iota(jnp.int32, (256, 128), 1)
    stat = jnp.transpose(jnp.where(lane == 0, top, mass))[:8]
    for to in range(16):
        stat_ref[to] = stat


def score(me, asked, slab):
    vmem = pl.BlockSpec(memory_space=pltpu.VMEM)
    return pl.pallas_call(
        score_kernel,
        out_shape=(
            jax.ShapeDtypeStruct((32, 256, 128), jnp.float32),
            jax.ShapeDtypeStruct((32, 256, 128), jnp.float32),
            jax.ShapeDtypeStruct((16, 8, 256), jnp.float32),
        ),
        in_specs=[pl.BlockSpec(memory_space=pltpu.SMEM), vmem, anywhere],
        out_specs=(vmem, vmem, vmem),
        scratch_shapes=[
            pltpu.VMEM((32, 256, 128), jnp.float32),
            pltpu.VMEM((32, 256, 128), jnp.float32),
            pltpu.VMEM((4096, 768), jnp.bfloat16),
            pltpu.SemaphoreType.DMA((8,)),
        ],
        compiler_params=params,
        cost_estimate=light,
    )(me, asked, slab)


def pull_kernel(me_ref, stat_ref, weight_ref, share_ref, slab_ref, out_ref, factor, total):
    step = pl.program_id(0)

    @pl.when(step == 0)
    def _():
        stats = stat_ref[...]
        tops, masses = stats[:, 0], stats[:, 1]
        best = jnp.max(tops, axis=0, keepdims=True)
        mass = jnp.sum(jnp.exp(tops - best) * masses, axis=0, keepdims=True)
        mine = stat_ref[me_ref[0]][0:1]
        line = loss_scale * jnp.exp(mine - best) / mass
        factor[...] = jnp.transpose(jnp.broadcast_to(line, (128, 256)))
        total[...] = jnp.zeros_like(total)

    coef = jnp.concatenate(
        [weight_ref[i] * factor[...] - loss_scale * share_ref[i] for i in range(4)], axis=1
    )
    both = jnp.concatenate(halves(coef), axis=0)
    got = jnp.dot(both, slab_ref[...], preferred_element_type=jnp.float32)
    total[...] += got[:256] + got[256:]

    @pl.when(step == 7)
    def _():
        out_ref[...] = total[...].astype(jnp.bfloat16)


def pull(me, stats, weight, share, slab):
    quarter = pl.BlockSpec((4, 256, 128), lambda j, me: (j, 0, 0))
    return pl.pallas_call(
        pull_kernel,
        grid_spec=pltpu.PrefetchScalarGridSpec(
            num_scalar_prefetch=1,
            grid=(8,),
            in_specs=[whole(16, 8, 256), quarter, quarter, pl.BlockSpec((512, 768), lambda j, me: (j, 0))],
            out_specs=whole(256, 768),
            scratch_shapes=[pltpu.VMEM((256, 128), jnp.float32), pltpu.VMEM((256, 768), jnp.float32)],
        ),
        out_shape=jax.ShapeDtypeStruct((256, 768), jnp.bfloat16),
        compiler_params=params,
        cost_estimate=light,
    )(me, stats, weight, share, slab)


def resid_kernel(came_ref, normed_ref, rstd_ref, gain_ref, resid_grad_ref, out_grad_ref, ups):
    step = pl.program_id(0)

    @pl.when(step == 0)
    def _():
        ups[...] = jnp.sum(came_ref[...].astype(jnp.float32), axis=0) * (1 / 64) * gain_ref[...]

    for q in range(4):
        up = ups[pl.ds(step * 4 + q, 1), :]
        rows = slice(q * 64, q * 64 + 64)
        normed = normed_ref[rows, :]
        along = jnp.mean(up * normed, axis=-1, keepdims=True)
        grad = (up - jnp.mean(up, axis=-1, keepdims=True) - normed * along) * rstd_ref[rows, :]
        resid_grad_ref[rows, :] = grad
        out_grad_ref[rows, :] = grad.astype(jnp.bfloat16)


def resid_gradient(came, normed, rstd, gain):
    rows = pl.BlockSpec((256, 768), lambda j: (j, 0))
    return pl.pallas_call(
        resid_kernel,
        grid=(4,),
        in_specs=[
            whole(16, 16, 768),
            rows,
            pl.BlockSpec((256, 1), lambda j: (j, 0)),
            whole(1, 768),
        ],
        out_specs=(rows, rows),
        out_shape=(
            jax.ShapeDtypeStruct((1024, 768), jnp.float32),
            jax.ShapeDtypeStruct((1024, 768), jnp.bfloat16),
        ),
        scratch_shapes=[pltpu.VMEM((16, 768), jnp.float32)],
        compiler_params=params,
        cost_estimate=light,
    )(came, normed, rstd, gain.reshape(1, -1))


def pair_kernel(place_ref, grad_ref, came_ref, *refs):
    own_ref, one_ref, three_ref, two_ref, right_ref = refs[-5:]
    for out, step in ((own_ref, 0), (one_ref, 1), (three_ref, 3), (two_ref, 2)):
        at = (place_ref[1] + step) % 4
        got = grad_ref[at, 0, :, :384] + came_ref[at, :, :384].astype(jnp.float32)
        out[...] = got.astype(out.dtype)
    right = [grad_ref[y, 0, :, 384:] + came_ref[y, :, 384:].astype(jnp.float32) for y in range(4)]
    for i in range(2):
        rows = slice(i * 24, i * 24 + 24)
        right_ref[i] = jnp.concatenate([part[rows] for part in right], axis=0).astype(jnp.bfloat16)


def pair(place, grad, came, *after):
    piece = pl.BlockSpec((48, 384), lambda j, place: (j, 0))
    return pl.pallas_call(
        pair_kernel,
        grid_spec=pltpu.PrefetchScalarGridSpec(
            num_scalar_prefetch=1,
            grid=(8,),
            in_specs=[
                pl.BlockSpec((4, 1, 48, 768), lambda j, place: (0, place[0], j, 0)),
                pl.BlockSpec((4, 48, 768), lambda j, place: (0, j, 0)),
            ]
            + [anywhere] * len(after),
            out_specs=(piece,) * 4 + (pl.BlockSpec((2, 96, 384), lambda j, place: (j, 0, 0)),),
        ),
        out_shape=(jax.ShapeDtypeStruct((384, 384), jnp.float32),)
        + (jax.ShapeDtypeStruct((384, 384), jnp.bfloat16),) * 3
        + (jax.ShapeDtypeStruct((16, 96, 384), jnp.bfloat16),),
        compiler_params=params,
        cost_estimate=light,
    )(place, grad, came, *after)


def away_part(grad, core):
    return lax.dynamic_index_in_dim(grad, 1 - core, 1, keepdims=False).astype(jnp.bfloat16)


def left_kernel(own_a, one_a, three_a, two_a, own_b, one_b, three_b, two_b, *refs):
    out_ref = refs[-1]
    for side, own, parts in ((0, own_a, (one_a, three_a, two_a)), (1, own_b, (one_b, three_b, two_b))):
        total = own[...]
        for part in parts:
            total = total + part[...].astype(jnp.float32)
        out_ref[:, side * 384 : side * 384 + 384] = total.astype(jnp.bfloat16)


def left_sums(first, second, *after):
    vmem = pl.BlockSpec(memory_space=pltpu.VMEM)
    return pl.pallas_call(
        left_kernel,
        in_specs=[vmem] * 8 + [anywhere] * len(after),
        out_specs=vmem,
        out_shape=jax.ShapeDtypeStruct((384, 768), jnp.bfloat16),
        compiler_params=params,
        cost_estimate=light,
    )(*first, *second, *after)


def right_kernel(y_ref, first_ref, second_ref, own_ref, one_ref, three_ref, two_ref, total):
    total[:, :384] = jnp.sum(first_ref[...].astype(jnp.float32), axis=0)
    total[:, 384:] = jnp.sum(second_ref[...].astype(jnp.float32), axis=0)
    for out, step in ((own_ref, 0), (one_ref, 1), (three_ref, 3), (two_ref, 2)):
        at = (y_ref[0] + step) % 4
        out[...] = total[pl.ds(pl.multiple_of(at * 24, 8), 24), :]


def right_sums(y, first, second):
    vmem = pl.BlockSpec(memory_space=pltpu.VMEM)
    return pl.pallas_call(
        right_kernel,
        in_specs=[pl.BlockSpec(memory_space=pltpu.SMEM), vmem, vmem],
        out_specs=(vmem,) * 4,
        out_shape=(jax.ShapeDtypeStruct((24, 768), jnp.float32),) * 4,
        scratch_shapes=[pltpu.VMEM((96, 768), jnp.float32)],
        compiler_params=params,
        cost_estimate=light,
    )(y, first, second)


def last_kernel(devices, left_ref, own_ref, one_ref, three_ref, two_ref, out_ref):
    left = jnp.sum(left_ref[...].astype(jnp.float32), axis=0) / devices
    right = (own_ref[...] + one_ref[...] + three_ref[...] + two_ref[...]) / devices
    for side in range(2):
        cols = slice(side * 384, side * 384 + 384)
        out_ref[:, side * 768 : side * 768 + 384] = left[:, cols]
        out_ref[:, side * 768 + 384 : side * 768 + 768] = right[:, cols]


def last_sums(devices, left, *right):
    vmem = pl.BlockSpec(memory_space=pltpu.VMEM)
    return pl.pallas_call(
        lambda *refs: last_kernel(devices, *refs),
        in_specs=[vmem] * 5,
        out_specs=vmem,
        out_shape=jax.ShapeDtypeStruct((24, 1536), jnp.float32),
        compiler_params=params,
        cost_estimate=light,
    )(left, *right)


def body(
    tokens, w_in, bias_in, w_out, bias_out, gain, shift, slab, owners, offsets, reader_weights
):
    devices = lax.axis_size("query") * lax.axis_size("index")
    me = lax.axis_index("index")[None]
    y = lax.axis_index("query") // 2
    core = lax.axis_index("query") % 2
    place = jnp.stack([core, y])

    target = reader_weights / jnp.sum(reader_weights, axis=-1, keepdims=True)
    fields = (owners[..., 0], offsets // 128, offsets % 128) + halves(target)
    table = jnp.stack([field.astype(jnp.bfloat16).reshape(2, 512) for field in fields]).reshape(10, 512)
    table = jnp.pad(table, ((0, 6), (0, 0)))

    hidden, slopes, normed, rstd, ask = forward(
        tokens, w_in, bias_in, w_out, bias_out, gain, shift, table
    )
    weight, share, stat = score(me, exchange(ask), slab)
    partial = pull(me, exchange(stat), weight, share, slab)
    came = exchange(partial.reshape(16, 16, 768))
    resid_grad, out_grad = resid_gradient(came, normed, rstd, gain)

    def stage_one(left, right, *after):
        grad = columns_dot(left, right).reshape(4, 2, 384, 768)
        over_core = shifted(away_part(grad, core), 1, 0)
        own, one, three, two, packed = pair(place, grad, over_core, *after)
        moved = [shifted(piece, 0, step) for piece, step in ((one, 1), (three, 3), (two, 2))]
        return (own, *moved), exchange(packed)

    left_second, right_second = stage_one(hidden, out_grad)
    pre_grad = (
        jnp.dot(out_grad, w_out.T, preferred_element_type=jnp.float32) * slopes.astype(jnp.float32)
    ).astype(jnp.bfloat16)
    left_first, right_first = stage_one(pre_grad, tokens, right_second)
    token_grads = (
        resid_grad + jnp.dot(pre_grad, w_in.T, preferred_element_type=jnp.float32)
    ).astype(jnp.bfloat16)

    left = exchange(left_sums(left_first, left_second, token_grads).reshape(16, 24, 768))
    own, one, three, two = right_sums(y[None], right_first, right_second)
    right = [own] + [shifted(piece, 0, step) for piece, step in ((one, 1), (three, 3), (two, 2))]
    return (token_grads, last_sums(devices, left, *right))


def solution(mesh):
    placed = (
        P(("query", "index"), None),
        P(),
        P(),
        P(),
        P(),
        P(),
        P(),
        P("index", None),
        P(("query", "index"), None, None),
        P(("query", "index"), None),
        P(("query", "index"), None),
    )
    return jax.shard_map(
        body,
        mesh=mesh,
        in_specs=placed,
        out_specs=(P(("query", "index"), None), P(("query", "index"), None)),
        check_vma=False,
    )
```

time: 447 us -> 231 us (0.52)
  waiting for transfers between devices: 272 us -> 49.2 us
  Pallas kernels: 0 us -> 75.4 us
  matrix products: 68.7 us -> 28.9 us
  local copies, waits for them, and re-layouts: 54.5 us -> 18.8 us
  starting transfers between devices: 4.93 us -> 40.5 us
  between operations: 14.3 us -> 0.88 us
  other arithmetic: 17 us -> 3.64 us
    unnamed x2 -> x0, waiting for transfers between devices: 226 us -> none
    pallas_call x0 -> x9, Pallas kernels: none -> 75.4 us  [the longest x1 22.2 us: forward(): pl.pallas_call(forward_kernel, grid=(3072 // block,), in_specs=[whole(102...]
    dot_general x7 -> x3, matrix products: 59 us -> 18.9 us  [the longest x2 10.4 us: columns_dot(): lax.dot_general(left, right, (((0,), (0,)), ((), ())), preferred_element_...]
    gather x2 -> x0, local copies, waits for them, and re-layouts: 26.7 us -> none  [the longest x1 18.2 us: body(): slab[arrived.reshape(shards * capacity)].reshape(shards, capacity, width)]
    all_to_all x1 -> x5, starting transfers between devices: 4.7 us -> 26 us  [exchange(): return lax.all_to_all(value, 'index', 0, 0, tiled=True)]
    ppermute x0 -> x11, starting transfers between devices: none -> 14.6 us  [shifted(): return lax.ppermute(value, every, pairs)]
    unnamed x22 -> x42, local copies, waits for them, and re-layouts: 21.3 us -> 10.7 us
    concatenate x1 -> x0, other arithmetic: 7.14 us -> none  [body(): jnp.concatenate([first, second], axis=1)]
  transfers between devices with their start and end apart: 2 -> 16, of which waited for: 2 -> 7; matrix products, arithmetic and copies ran while one was open for 7% -> 8% of each run, Pallas kernels for 0% -> 9%
where the time goes in v2:
time: 231 us; the launch traced here: 230 us
  Pallas kernels  75.4 us (33%)
  waiting for transfers between devices  49.2 us (21%)
  starting transfers between devices  40.5 us (18%)
  matrix products  28.9 us (13%)
  local copies, waits for them, and re-layouts  18.8 us (8%)
  blocking collectives  12.2 us (5%)
  other arithmetic  3.64 us (2%)
    all_to_all x5, waiting for transfers between devices, exchange(): return lax.all_to_all(value, 'index', 0, 0, tiled=True)  45.8 us
    all_to_all x5, starting transfers between devices, exchange(): return lax.all_to_all(value, 'index', 0, 0, tiled=True)  26 us
    pallas_call x1, Pallas kernels, forward(): pl.pallas_call(forward_kernel, grid=(3072 // block,), in_specs=[whole(102...  22.2 us
    pallas_call x1, Pallas kernels, score(): pl.pallas_call(score_kernel, out_shape=(jax.ShapeDtypeStruct((32, 256, 12...  15.1 us
    pallas_call x2, Pallas kernels, pair(): pl.pallas_call(pair_kernel, grid_spec=pltpu.PrefetchScalarGridSpec(num_sc...  15 us
    ppermute x11, starting transfers between devices, shifted(): return lax.ppermute(value, every, pairs)  14.6 us
    all_to_all x1, blocking collectives, exchange(): return lax.all_to_all(value, 'index', 0, 0, tiled=True)  12.2 us
    unnamed x42, local copies, waits for them, and re-layouts  10.7 us
  transfers between devices with their start and end apart: 16, of which 7 were waited for; matrix products, arithmetic and copies ran while one was open for 8% of the time, Pallas kernels for 9%

profile of v2, /device:TPU:0, one launch (start us, length us, event | category | flops | bytes accessed | tf_op | source)
XLA Modules:
  0.0 229.6 jit_solution(12013693346723291756)
XLA Ops:
  0.6 1.3 reshape.48.gain_ref
  1.9 1.3 reshape.47.bias_out_ref
  3.2 1.3 reshape.49.shift_ref
  4.5 0.7 convert_reduce_fusion
  5.2 0.1 convert_element_type.52
  5.3 0.8 reduce_sum.9
  6.1 0.8 subtract_convert_fusion
  6.9 0.1 stack_reshape.16
  7.0 0.1 stack_reshape.15
  7.1 0.7 fusion.3
  7.8 0.1 stack_reshape.14
  7.9 0.1 stack_reshape.13
  8.0 0.6 pad.4.table_ref
  8.6 22.2 %shard_map.122 = (bf16[1024,3072]{1,0:T(8,128)(2,1)}, bf16[1024,3072]{1,0:T(8,128)(2,1)}, f32[1024,768]{1,0:T(8,128)}, f32[1024,1]{1,0:T(8,128)}, bf16[16,16,2048]{2,1,0:T(8,128)(2,1)}) custom-call(bf16[1024,768]{1,0:T(8,128)(2,1)} %tokens_ref.1, bf16[768,3072]{1,0:T(8,128)(2,1)} %w_in_ref.1, f32[1,3072]{1,0:T(1,128)} %bitcast.34, ...), custom_call_target="tpu_custom_call" | custom-call | flops 1000 | bytes 1000 | tf_op jit(solution)/shard_map/pallas_call | solution.py:99
  30.8 8.0 %all-to-all-start = ((bf16[16,16,2048]{2,1,0:T(8,128)(2,1)}), bf16[16,16,2048]{2,1,0:T(8,128)(2,1)S(1)}, u32[]{:S(2)}, u32[]{:S(2)}) async-start(bf16[16,16,2048]{2,1,0:T(8,128)(2,1)} %get-tuple-element.26), calls=%async_computation | async-start | bytes 2097152 | tf_op jit(solution)/shard_map/all_to_all | solution.py:32
  38.8 17.6 %all-to-all-done.ask_ref = bf16[16,16,2048]{2,1,0:T(8,128)(2,1)S(1)} async-done(((bf16[16,16,2048]{2,1,0:T(8,128)(2,1)}), bf16[16,16,2048]{2,1,0:T(8,128)(2,1)S(1)}, u32[]{:S(2)}, u32[]{:S(2)}) %all-to-all-start) | async-done | bytes 1048608 | tf_op jit(solution)/shard_map/all_to_all | solution.py:32
  56.5 1.0 copy-done.4
  57.4 15.1 %shard_map.123 = (f32[32,256,128]{2,1,0:T(8,128)}, f32[32,256,128]{2,1,0:T(8,128)}, f32[16,8,256]{2,1,0:T(8,128)}) custom-call(s32[1]{0:T(128)} %bitcast.me_ref, bf16[16,16,2048]{2,1,0:T(8,128)(2,1)} %copy-done.4, bf16[4096,768]{1,0:T(8,128)(2,1)} %slab_ref.1), custom_call_target="tpu_custom_call" | custom-call | flops 1000 | bytes 1000 | tf_op jit(solution)/shard_map/pallas_call | solution.py:187
  72.5 12.2 %all_to_all.30.stat_ref = f32[16,8,256]{2,1,0:T(8,128)} all-to-all(f32[16,8,256]{2,1,0:T(8,128)} %get-tuple-element.27), channel_id=1, replica_groups=mesh['query'=8,'index'=16] {'index'}, dimensions={0} | all-to-all | bytes 262144 | tf_op jit(solution)/shard_map/all_to_all | solution.py:32
  84.7 10.3 %shard_map.124 = bf16[256,768]{1,0:T(8,128)(2,1)} custom-call(s32[1]{0:T(128)} %bitcast.me_ref, f32[16,8,256]{2,1,0:T(8,128)} %all_to_all.30.stat_ref, f32[32,256,128]{2,1,0:T(8,128)} %get-tuple-element.28.weight_ref, f32[32,256,128]{2,1,0:T(8,128)} %get-tuple-element.29.share_ref, bf16[4096,768]{1,0:T(8,128)(2,1)} %slab_ref.1), custom_call_target="tpu_custom_call" | custom-call | flops 1000 | bytes 1000 | tf_op jit(solution)/shard_map/pallas_call | solution.py:235
  95.0 3.7 %all-to-all-start.2 = ((bf16[16,16,768]{2,1,0:T(8,128)(2,1)}), bf16[16,16,768]{2,1,0:T(8,128)(2,1)S(1)}, u32[]{:S(2)}, u32[]{:S(2)}) async-start(bf16[16,16,768]{2,1,0:T(8,128)(2,1)} %bitcast.33), calls=%async_computation.2 | async-start | bytes 786432 | tf_op jit(solution)/shard_map/all_to_all | solution.py:32
  98.8 9.2 %all-to-all-done.2.came_ref = bf16[16,16,768]{2,1,0:T(8,128)(2,1)S(1)} async-done(((bf16[16,16,768]{2,1,0:T(8,128)(2,1)}), bf16[16,16,768]{2,1,0:T(8,128)(2,1)S(1)}, u32[]{:S(2)}, u32[]{:S(2)}) %all-to-all-start.2) | async-done | bytes 393248 | tf_op jit(solution)/shard_map/all_to_all | solution.py:32
  107.9 0.8 copy-done.7
  108.7 5.3 %shard_map.125 = (f32[1024,768]{1,0:T(8,128)}, bf16[1024,768]{1,0:T(8,128)(2,1)}) custom-call(bf16[16,16,768]{2,1,0:T(8,128)(2,1)} %copy-done.7, f32[1024,768]{1,0:T(8,128)} %get-tuple-element.30.normed_ref, f32[1024,1]{1,0:T(8,128)} %get-tuple-element.31.rstd_ref, f32[1,768]{1,0:T(1,128)} %reshape.48.gain_ref), custom_call_target="tpu_custom_call" | custom-call | flops 1000 | bytes 1000 | tf_op jit(solution)/shard_map/pallas_call | solution.py:269
  114.0 8.5 %multiply_convert_fusion = bf16[1024,3072]{1,0:T(8,128)(2,1)S(1)} fusion(bf16[1024,3072]{1,0:T(8,128)(2,1)} %get-tuple-element.34, bf16[1024,768]{1,0:T(8,128)(2,1)} %get-tuple-element.33, bf16[3072,768]{1,0:T(8,128)(2,1)} %w_out_ref.1), kind=kOutput, calls=%fused_computation | convolution fusion | flops 4841275392 | bytes 18874368 | tf_op jit(solution)/shard_map/dot_general | solution.py:421
  122.6 5.2 %fusion.8 = f32[3072,768]{1,0:T(8,128)S(1)} fusion(bf16[1024,3072]{1,0:T(8,128)(2,1)S(1)} %bitcast.36, bf16[1024,768]{1,0:T(8,128)(2,1)S(1)} %copy-done.15), kind=kOutput, calls=%fused_computation.27 | convolution fusion | flops 4831838208 | bytes 17301504 | tf_op jit(solution)/shard_map/dot_general | solution.py:28
  127.8 0.0 copy-start.8
  127.8 1.6 fusion.1
  129.4 2.8 %copy-done.1 = f32[3072,768]{1,0:T(8,128)} copy-done((f32[3072,768]{1,0:T(8,128)}, f32[3072,768]{1,0:T(8,128)S(1)}, u32[]{:S(2)}) %copy-start.1) | copy-done | bytes 9437208
  132.2 0.0 collective-permute-start.1
  132.2 5.2 %fusion.7 = f32[3072,768]{1,0:T(8,128)S(1)} fusion(bf16[1024,3072]{1,0:T(8,128)(2,1)S(1)} %multiply_convert_fusion, bf16[1024,768]{1,0:T(8,128)(2,1)S(1)} %copy-done.8), kind=kOutput, calls=%fused_computation.26 | convolution fusion | flops 4831838208 | bytes 17301504 | tf_op jit(solution)/shard_map/dot_general | solution.py:28
  137.4 3.6 %copy-done = f32[3072,768]{1,0:T(8,128)} copy-done((f32[3072,768]{1,0:T(8,128)}, f32[3072,768]{1,0:T(8,128)S(1)}, u32[]{:S(2)}) %copy-start) | copy-done | bytes 9437208
  141.1 1.7 fusion
  142.7 0.5 collective-permute-start
  143.2 0.6 pad_add_fusion.place_ref
  143.9 7.4 %shard_map.126 = (f32[384,384]{1,0:T(8,128)}, bf16[384,384]{1,0:T(8,128)(2,1)}, bf16[384,384]{1,0:T(8,128)(2,1)}, bf16[384,384]{1,0:T(8,128)(2,1)}, bf16[16,96,384]{2,1,0:T(8,128)(2,1)}) custom-call(s32[2]{0:T(128)} %pad_add_fusion.place_ref, f32[4,2,384,768]{3,2,1,0:T(8,128)} %bitcast.31, bf16[4,384,768]{2,1,0:T(8,128)(2,1)} %collective-permute-done.1.came_ref), custom_call_target="tpu_custom_call" | custom-call | flops 1000 | bytes 1000 | tf_op jit(solution)/shard_map/pallas_call | solution.py:303
  151.3 3.7 %all-to-all-start.3 = ((bf16[16,96,384]{2,1,0:T(8,128)(2,1)}), bf16[16,96,384]{2,1,0:T(8,128)(2,1)S(1)}, u32[]{:S(2)}, u32[]{:S(2)}) async-start(bf16[16,96,384]{2,1,0:T(8,128)(2,1)} %get-tuple-element.36), calls=%async_computation.3 | async-start | bytes 2359296 | tf_op jit(solution)/shard_map/all_to_all | solution.py:32
  155.0 1.6 collective-permute-start.5
  156.7 1.7 collective-permute-start.6
  158.3 2.0 collective-permute-start.7
  160.3 14.7 %all-to-all-done.3.refs_0_.second_ref = bf16[16,96,384]{2,1,0:T(8,128)(2,1)S(1)} async-done(((bf16[16,96,384]{2,1,0:T(8,128)(2,1)}), bf16[16,96,384]{2,1,0:T(8,128)(2,1)S(1)}, u32[]{:S(2)}, u32[]{:S(2)}) %all-to-all-start.3) | async-done | bytes 1179680 | tf_op jit(solution)/shard_map/all_to_all | solution.py:32
  175.0 1.1 copy-done.2
  176.1 7.5 %shard_map.127 = (f32[384,384]{1,0:T(8,128)}, bf16[384,384]{1,0:T(8,128)(2,1)}, bf16[384,384]{1,0:T(8,128)(2,1)}, bf16[384,384]{1,0:T(8,128)(2,1)}, bf16[16,96,384]{2,1,0:T(8,128)(2,1)}) custom-call(s32[2]{0:T(128)} %pad_add_fusion.place_ref, f32[4,2,384,768]{3,2,1,0:T(8,128)} %bitcast.29, bf16[4,384,768]{2,1,0:T(8,128)(2,1)} %copy-done.5, ...), custom_call_target="tpu_custom_call" | custom-call | flops 1000 | bytes 1000 | tf_op jit(solution)/shard_map/pallas_call | solution.py:303
  183.6 3.7 %all-to-all-start.5 = ((bf16[16,96,384]{2,1,0:T(8,128)(2,1)}), bf16[16,96,384]{2,1,0:T(8,128)(2,1)S(1)}, u32[]{:S(2)}, u32[]{:S(2)}) async-start(bf16[16,96,384]{2,1,0:T(8,128)(2,1)} %get-tuple-element.45), calls=%async_computation.5 | async-start | bytes 2359296 | tf_op jit(solution)/shard_map/all_to_all | solution.py:32
  187.3 1.6 collective-permute-start.2
  188.9 1.7 collective-permute-start.3
  190.6 0.0 collective-permute-done.5.one_b
  190.6 2.0 collective-permute-start.4
  192.6 10.0 %add_convert_fusion.refs_0_ = bf16[1024,768]{1,0:T(8,128)(2,1)} fusion(f32[1024,768]{1,0:T(8,128)} %get-tuple-element.32, bf16[1024,3072]{1,0:T(8,128)(2,1)} %copy-done.16, bf16[768,3072]{1,0:T(8,128)(2,1)} %w_in_ref.1), kind=kOutput, calls=%fused_computation.3 | convolution fusion | flops 4833411072 | bytes 15728640 | tf_op jit(solution)/shard_map/dot_general | solution.py:425
  202.6 0.0 collective-permute-done.6.three_b
  202.6 0.0 collective-permute-done.7.two_b
  202.6 0.2 collective-permute-done.3.three_a
  202.8 1.7 collective-permute-done.4.two_a
  204.5 0.7 copy-done.11
  205.2 2.8 %shard_map.128 = bf16[384,768]{1,0:T(8,128)(2,1)} custom-call(f32[384,384]{1,0:T(8,128)} %get-tuple-element.37.own_a, bf16[384,384]{1,0:T(8,128)(2,1)} %copy-done.9, bf16[384,384]{1,0:T(8,128)(2,1)} %copy-done.10, bf16[384,384]{1,0:T(8,128)(2,1)} %copy-done.11, f32[384,384]{1,0:T(8,128)} %get-tuple-element.41.own_b, ...), custom_call_target="tpu_custom_call" | custom-call | flops 1000 | bytes 1000 | tf_op jit(solution)/shard_map/pallas_call | solution.py:338
  208.1 6.9 %all-to-all-start.4 = ((bf16[16,24,768]{2,1,0:T(8,128)(2,1)}), bf16[16,24,768]{2,1,0:T(8,128)(2,1)S(1)}, u32[]{:S(2)}, u32[]{:S(2)}) async-start(bf16[16,24,768]{2,1,0:T(8,128)(2,1)} %bitcast.32), calls=%async_computation.4 | async-start | bytes 1179648 | tf_op jit(solution)/shard_map/all_to_all | solution.py:32
  215.0 2.7 %shard_map.129 = (f32[24,768]{1,0:T(8,128)}, f32[24,768]{1,0:T(8,128)}, f32[24,768]{1,0:T(8,128)}, f32[24,768]{1,0:T(8,128)}) custom-call(s32[1]{0:T(128)} %bitcast.4.y_ref, bf16[16,96,384]{2,1,0:T(8,128)(2,1)} %copy-done.3, bf16[16,96,384]{2,1,0:T(8,128)(2,1)} %copy-done.2), custom_call_target="tpu_custom_call" | custom-call | flops 1000 | bytes 1000 | tf_op jit(solution)/shard_map/pallas_call | solution.py:358
  217.7 1.1 collective-permute-start.8
  218.8 2.1 collective-permute-start.9
  220.9 0.2 collective-permute-start.10
  221.1 4.3 %all-to-all-done.4.refs_0_ = bf16[16,24,768]{2,1,0:T(8,128)(2,1)S(1)} async-done(((bf16[16,24,768]{2,1,0:T(8,128)(2,1)}), bf16[16,24,768]{2,1,0:T(8,128)(2,1)S(1)}, u32[]{:S(2)}, u32[]{:S(2)}) %all-to-all-start.4) | async-done | bytes 589856 | tf_op jit(solution)/shard_map/all_to_all | solution.py:32
  225.5 1.5 collective-permute-done.10.refs_4_
  227.0 0.6 copy-done.14
  227.6 1.9 shard_map.130
  (43 shorter events, 0.1 us)
Async XLA Ops:
  30.8 25.6 %all-to-all-start = ((bf16[16,16,2048]{2,1,0:T(8,128)(2,1)}), bf16[16,16,2048]{2,1,0:T(8,128)(2,1)S(1)}, u32[]{:S(2)}, u32[]{:S(2)}) async-start(bf16[16,16,2048]{2,1,0:T(8,128)(2,1)} %get-tuple-element.26), calls=%async_computation | async-start | bytes 2097152 | tf_op jit(solution)/shard_map/all_to_all | solution.py:32
  56.5 1.0 copy-start.4
  95.0 12.9 %all-to-all-start.2 = ((bf16[16,16,768]{2,1,0:T(8,128)(2,1)}), bf16[16,16,768]{2,1,0:T(8,128)(2,1)S(1)}, u32[]{:S(2)}, u32[]{:S(2)}) async-start(bf16[16,16,768]{2,1,0:T(8,128)(2,1)} %bitcast.33), calls=%async_computation.2 | async-start | bytes 786432 | tf_op jit(solution)/shard_map/all_to_all | solution.py:32
  107.9 0.8 copy-start.7
  108.7 13.9 %slice-start = ((s8[6291456]{0:T(1024)(128)(4,1)}), s8[2097152]{0:T(1024)(128)(4,1)S(1)}, s32[]{:S(2)}) async-start(s8[6291456]{0:T(1024)(128)(4,1)} %bitcast.35), calls=%async_computation.6 | async-start | bytes 4194304
  114.0 8.6 %slice-start.1 = ((s8[6291456]{0:T(1024)(128)(4,1)}), s8[4194304]{0:T(1024)(128)(4,1)S(1)}, s32[]{:S(2)}) async-start(s8[6291456]{0:T(1024)(128)(4,1)} %bitcast.35), calls=%async_computation.7 | async-start | bytes 8388608
  114.0 8.6 %copy-start.15 = (bf16[1024,768]{1,0:T(8,128)(2,1)S(1)}, bf16[1024,768]{1,0:T(8,128)(2,1)}, u32[]{:S(2)}) copy-start(bf16[1024,768]{1,0:T(8,128)(2,1)} %get-tuple-element.33) | copy-start | bytes 4718596
  122.6 9.7 %copy-start.16 = (bf16[1024,3072]{1,0:T(8,128)(2,1)}, bf16[1024,3072]{1,0:T(8,128)(2,1)S(1)}, u32[]{:S(2)}) copy-start(bf16[1024,3072]{1,0:T(8,128)(2,1)S(1)} %multiply_convert_fusion) | copy-start | bytes 18874372
  127.8 4.4 %copy-start.1 = (f32[3072,768]{1,0:T(8,128)}, f32[3072,768]{1,0:T(8,128)S(1)}, u32[]{:S(2)}) copy-start(f32[3072,768]{1,0:T(8,128)S(1)} %fusion.8) | copy-start | bytes 28311556
  127.8 4.4 %copy-start.8 = (bf16[1024,768]{1,0:T(8,128)(2,1)S(1)}, bf16[1024,768]{1,0:T(8,128)(2,1)}, u32[]{:S(2)}) copy-start(bf16[1024,768]{1,0:T(8,128)(2,1)} %tokens_ref.1) | copy-start | bytes 4718596
  132.2 11.6 %collective-permute-start.1 = (bf16[4,384,768]{2,1,0:T(8,128)(2,1)}, bf16[4,384,768]{2,1,0:T(8,128)(2,1)}, u32[]{:S(2)}, u32[]{:S(2)}) collective-permute-start(bf16[4,384,768]{2,1,0:T(8,128)(2,1)} %fusion.1), channel_id=1, source_target_pairs={{0,16},{1,17},{2,18},{3,19},{4,20},{5,21},{6,22},{7,23},{8,24},{9,... | collective-permute-start | bytes 7077896 | tf_op jit(solution)/shard_map/ppermute | solution.py:41
  137.4 3.6 %copy-start = (f32[3072,768]{1,0:T(8,128)}, f32[3072,768]{1,0:T(8,128)S(1)}, u32[]{:S(2)}) copy-start(f32[3072,768]{1,0:T(8,128)S(1)} %fusion.7) | copy-start | bytes 28311556
  142.7 17.6 %collective-permute-start = (bf16[4,384,768]{2,1,0:T(8,128)(2,1)}, bf16[4,384,768]{2,1,0:T(8,128)(2,1)S(1)}, u32[]{:S(2)}, u32[]{:S(2)}) collective-permute-start(bf16[4,384,768]{2,1,0:T(8,128)(2,1)} %fusion), channel_id=1, source_target_pairs={{0,16},{1,17},{2,18},{3,19},{4,20},{5,21},{6,22},{7,23},{8,24},{9,... | collective-permute-start | bytes 7077896 | tf_op jit(solution)/shard_map/ppermute | solution.py:41
  151.3 23.7 %all-to-all-start.3 = ((bf16[16,96,384]{2,1,0:T(8,128)(2,1)}), bf16[16,96,384]{2,1,0:T(8,128)(2,1)S(1)}, u32[]{:S(2)}, u32[]{:S(2)}) async-start(bf16[16,96,384]{2,1,0:T(8,128)(2,1)} %get-tuple-element.36), calls=%async_computation.3 | async-start | bytes 2359296 | tf_op jit(solution)/shard_map/all_to_all | solution.py:32
  155.0 35.6 %collective-permute-start.5 = (bf16[384,384]{1,0:T(8,128)(2,1)}, bf16[384,384]{1,0:T(8,128)(2,1)}, u32[]{:S(2)}, u32[]{:S(2)}) collective-permute-start(bf16[384,384]{1,0:T(8,128)(2,1)} %get-tuple-element.42), channel_id=1, source_target_pairs={{0,32},{1,33},{2,34},{3,35},{4,36},{5,37},{6,38},{7,39},{8,40},{9,... | collective-permute-start | bytes 884744 | tf_op jit(solution)/shard_map/ppermute | solution.py:41
  156.7 45.9 %collective-permute-start.6 = (bf16[384,384]{1,0:T(8,128)(2,1)}, bf16[384,384]{1,0:T(8,128)(2,1)}, u32[]{:S(2)}, u32[]{:S(2)}) collective-permute-start(bf16[384,384]{1,0:T(8,128)(2,1)} %get-tuple-element.43), channel_id=1, source_target_pairs={{0,96},{1,97},{2,98},{3,99},{4,100},{5,101},{6,102},{7,103},{8,104... | collective-permute-start | bytes 884744 | tf_op jit(solution)/shard_map/ppermute | solution.py:41
  158.3 44.3 %collective-permute-start.7 = (bf16[384,384]{1,0:T(8,128)(2,1)}, bf16[384,384]{1,0:T(8,128)(2,1)}, u32[]{:S(2)}, u32[]{:S(2)}) collective-permute-start(bf16[384,384]{1,0:T(8,128)(2,1)} %get-tuple-element.44), channel_id=1, source_target_pairs={{0,64},{1,65},{2,66},{3,67},{4,68},{5,69},{6,70},{7,71},{8,72},{9,... | collective-permute-start | bytes 884744 | tf_op jit(solution)/shard_map/ppermute | solution.py:41
  160.3 14.7 %copy-start.5 = (bf16[4,384,768]{2,1,0:T(8,128)(2,1)}, bf16[4,384,768]{2,1,0:T(8,128)(2,1)S(1)}, u32[]{:S(2)}) copy-start(bf16[4,384,768]{2,1,0:T(8,128)(2,1)S(1)} %collective-permute-done.came_ref) | copy-start | bytes 7077892
  175.0 1.1 copy-start.2
  183.6 24.5 %all-to-all-start.5 = ((bf16[16,96,384]{2,1,0:T(8,128)(2,1)}), bf16[16,96,384]{2,1,0:T(8,128)(2,1)S(1)}, u32[]{:S(2)}, u32[]{:S(2)}) async-start(bf16[16,96,384]{2,1,0:T(8,128)(2,1)} %get-tuple-element.45), calls=%async_computation.5 | async-start | bytes 2359296 | tf_op jit(solution)/shard_map/all_to_all | solution.py:32
  187.3 15.3 %collective-permute-start.2 = (bf16[384,384]{1,0:T(8,128)(2,1)}, bf16[384,384]{1,0:T(8,128)(2,1)S(1)}, u32[]{:S(2)}, u32[]{:S(2)}) collective-permute-start(bf16[384,384]{1,0:T(8,128)(2,1)} %get-tuple-element.38), channel_id=1, source_target_pairs={{0,32},{1,33},{2,34},{3,35},{4,36},{5,37},{6,38},{7,39},{8,40},{9,... | collective-permute-start | bytes 884744 | tf_op jit(solution)/shard_map/ppermute | solution.py:41
  188.9 13.9 %collective-permute-start.3 = (bf16[384,384]{1,0:T(8,128)(2,1)}, bf16[384,384]{1,0:T(8,128)(2,1)S(1)}, u32[]{:S(2)}, u32[]{:S(2)}) collective-permute-start(bf16[384,384]{1,0:T(8,128)(2,1)} %get-tuple-element.39), channel_id=1, source_target_pairs={{0,96},{1,97},{2,98},{3,99},{4,100},{5,101},{6,102},{7,103},{8,104... | collective-permute-start | bytes 884744 | tf_op jit(solution)/shard_map/ppermute | solution.py:41
  190.6 13.9 %collective-permute-start.4 = (bf16[384,384]{1,0:T(8,128)(2,1)}, bf16[384,384]{1,0:T(8,128)(2,1)S(1)}, u32[]{:S(2)}, u32[]{:S(2)}) collective-permute-start(bf16[384,384]{1,0:T(8,128)(2,1)} %get-tuple-element.40), channel_id=1, source_target_pairs={{0,64},{1,65},{2,66},{3,67},{4,68},{5,69},{6,70},{7,71},{8,72},{9,... | collective-permute-start | bytes 884744 | tf_op jit(solution)/shard_map/ppermute | solution.py:41
  202.6 1.9 copy-start.9
  202.8 1.7 copy-start.10
  204.5 0.7 copy-start.11
  208.1 6.9 %copy-start.3 = (bf16[16,96,384]{2,1,0:T(8,128)(2,1)}, bf16[16,96,384]{2,1,0:T(8,128)(2,1)S(1)}, u32[]{:S(2)}) copy-start(bf16[16,96,384]{2,1,0:T(8,128)(2,1)S(1)} %all-to-all-done.5.first_ref) | copy-start | bytes 3538948
  208.1 17.4 %all-to-all-start.4 = ((bf16[16,24,768]{2,1,0:T(8,128)(2,1)}), bf16[16,24,768]{2,1,0:T(8,128)(2,1)S(1)}, u32[]{:S(2)}, u32[]{:S(2)}) async-start(bf16[16,24,768]{2,1,0:T(8,128)(2,1)} %bitcast.32), calls=%async_computation.4 | async-start | bytes 1179648 | tf_op jit(solution)/shard_map/all_to_all | solution.py:32
  217.7 7.7 %collective-permute-start.8 = (f32[24,768]{1,0:T(8,128)}, f32[24,768]{1,0:T(8,128)S(1)}, u32[]{:S(2)}, u32[]{:S(2)}) collective-permute-start(f32[24,768]{1,0:T(8,128)} %get-tuple-element.47), channel_id=1, source_target_pairs={{0,32},{1,33},{2,34},{3,35},{4,36},{5,37},{6,38},{7,39},{8,40},{9,... | collective-permute-start | bytes 221192 | tf_op jit(solution)/shard_map/ppermute | solution.py:41
  218.8 6.6 %collective-permute-start.9 = (f32[24,768]{1,0:T(8,128)}, f32[24,768]{1,0:T(8,128)S(1)}, u32[]{:S(2)}, u32[]{:S(2)}) collective-permute-start(f32[24,768]{1,0:T(8,128)} %get-tuple-element.48), channel_id=1, source_target_pairs={{0,96},{1,97},{2,98},{3,99},{4,100},{5,101},{6,102},{7,103},{8,104... | collective-permute-start | bytes 221192 | tf_op jit(solution)/shard_map/ppermute | solution.py:41
  220.9 6.1 %collective-permute-start.10 = (f32[24,768]{1,0:T(8,128)}, f32[24,768]{1,0:T(8,128)S(1)}, u32[]{:S(2)}, u32[]{:S(2)}) collective-permute-start(f32[24,768]{1,0:T(8,128)} %get-tuple-element.49), channel_id=1, source_target_pairs={{0,64},{1,65},{2,66},{3,67},{4,68},{5,69},{6,70},{7,71},{8,72},{9,... | collective-permute-start | bytes 221192 | tf_op jit(solution)/shard_map/ppermute | solution.py:41
  225.4 1.6 copy-start.6
  225.4 1.6 copy-start.12
  225.5 1.6 copy-start.13
  227.0 0.6 copy-start.14

commit v3 on v2

v3 whole, which is shorter than its diff:
```python
import jax
import jax.numpy as jnp
from jax import lax
from jax.experimental import pallas as pl
from jax.experimental.pallas import tpu as pltpu
from jax.sharding import PartitionSpec as P

loss_scale = 256.0
norm_eps = 1e-12
every = ("query", "index")
MIB = 1 << 20
low = -1e30


def limit(mib):
    return pltpu.CompilerParams(vmem_limit_bytes=mib * MIB)


def cost(us):
    return pl.CostEstimate(flops=us * 1_000_000_000, bytes_accessed=1000, transcendentals=0)
anywhere = pl.BlockSpec(memory_space=pl.ANY)


def halves(value):
    first = value.astype(jnp.bfloat16)
    return first, (value - first.astype(jnp.float32)).astype(jnp.bfloat16)


def dot_rows(left, right):
    return lax.dot_general(left, right, (((1,), (1,)), ((), ())), preferred_element_type=jnp.float32)


def columns_dot(left, right):
    return lax.dot_general(left, right, (((0,), (0,)), ((), ())), preferred_element_type=jnp.float32)


def exchange(value):
    return lax.all_to_all(value, "index", 0, 0, tiled=True)


def shifted(value, core, along_y):
    pairs = []
    for query in range(8):
        y, c = query // 2, query % 2
        to = ((y + along_y) % 4) * 2 + (c + core) % 2
        pairs += [(query * 16 + i, to * 16 + i) for i in range(16)]
    return lax.ppermute(value, every, pairs)


def whole(*shape):
    return pl.BlockSpec(shape, lambda *_: (0,) * len(shape))


def slope(pre):
    square = pre * pre
    bend = jnp.tanh(pre * (0.7978845608028654 + 0.035677408136300125 * square))
    share = 0.5 + 0.5 * bend
    value = pre * share
    grad = share + (value - value * share) * (1.5957691216057308 + 0.21406444881780074 * square)
    return value, grad


def forward_kernel(
    tokens_ref, w_in_ref, bias_in_ref, w_out_ref, vectors_ref,
    hidden_ref, slope_ref, normed_ref, rstd_ref, ask_ref, resid, query,
):
    step = pl.program_id(0)

    @pl.when(step == 0)
    def _():
        resid[...] = tokens_ref[...].astype(jnp.float32) + vectors_ref[:, :768]

    for part in range(4):
        rows = slice(part * 256, part * 256 + 256)
        pre = jnp.dot(tokens_ref[rows, :], w_in_ref[...], preferred_element_type=jnp.float32) + bias_in_ref[...]
        value, grad = slope(pre)
        value = value.astype(jnp.bfloat16)
        hidden_ref[rows, :] = value
        slope_ref[rows, :] = grad.astype(jnp.bfloat16)
        resid[rows, :] += jnp.dot(value, w_out_ref[...], preferred_element_type=jnp.float32)

    @pl.when(step == pl.num_programs(0) - 1)
    def _():
        for q in range(16):
            rows = slice(q * 64, q * 64 + 64)
            here = resid[rows, :]
            away = here - jnp.mean(here, axis=-1, keepdims=True)
            rstd = lax.rsqrt(jnp.mean(away * away, axis=-1, keepdims=True) + norm_eps)
            normed = away * rstd
            normed_ref[rows, :] = normed
            rstd_ref[rows, :] = rstd
            query[q : q + 1, :] = (
                jnp.sum(normed, axis=0, keepdims=True) * (1 / 64) * vectors_ref[:, 768:1536] + vectors_ref[:, 1536:2304]
            )
        upper, lower = halves(query[...])
        for to in range(16):
            ask_ref[to, :, :768] = upper
            ask_ref[to, :, 768:] = lower


def forward(tokens, w_in, bias_in, w_out, vectors):
    block = 512
    units = pl.BlockSpec((1024, block), lambda j: (0, j))
    return pl.pallas_call(
        forward_kernel,
        grid=(3072 // block,),
        in_specs=[
            whole(1024, 768),
            pl.BlockSpec((768, block), lambda j: (0, j)),
            pl.BlockSpec((1, block), lambda j: (0, j)),
            pl.BlockSpec((block, 768), lambda j: (j, 0)),
            whole(1, 3072),
        ],
        out_specs=(units, units, whole(1024, 768), whole(1024, 1), whole(16, 16, 1536)),
        out_shape=(
            jax.ShapeDtypeStruct((1024, 3072), jnp.bfloat16),
            jax.ShapeDtypeStruct((1024, 3072), jnp.bfloat16),
            jax.ShapeDtypeStruct((1024, 768), jnp.float32),
            jax.ShapeDtypeStruct((1024, 1), jnp.float32),
            jax.ShapeDtypeStruct((16, 16, 1536), jnp.bfloat16),
        ),
        scratch_shapes=[pltpu.VMEM((1024, 768), jnp.float32), pltpu.VMEM((16, 768), jnp.float32)],
        compiler_params=limit(36),
        cost_estimate=cost(20),
    )(tokens, w_in, bias_in.reshape(1, -1), w_out, vectors)


def table_kernel(owner_ref, offset_ref, weight_ref, out_ref):
    weight = weight_ref[...]
    target = weight / jnp.sum(weight, axis=-1, keepdims=True)
    offset = offset_ref[...]
    upper, lower = halves(target)
    fields = [
        owner_ref[...].astype(jnp.float32),
        (offset // 128).astype(jnp.float32),
        (offset % 128).astype(jnp.float32),
        upper.astype(jnp.float32),
        lower.astype(jnp.float32),
    ]
    rows = [
        jnp.concatenate([field[g * 8 + i : g * 8 + i + 1] for i in range(8)], axis=1)
        for field in fields
        for g in range(2)
    ]
    rows = jnp.concatenate(rows + [jnp.zeros((6, 512), jnp.float32)], axis=0).astype(jnp.bfloat16)
    for to in range(16):
        out_ref[to] = rows


def table(owners, offsets, reader_weights):
    vmem = pl.BlockSpec(memory_space=pltpu.VMEM)
    return pl.pallas_call(
        table_kernel,
        in_specs=[vmem] * 3,
        out_specs=vmem,
        out_shape=jax.ShapeDtypeStruct((16, 16, 512), jnp.bfloat16),
        compiler_params=limit(16),
        cost_estimate=cost(1),
    )(owners, offsets, reader_weights)


def picks_kernel(me_ref, table_ref, after_ref, count_ref, share_ref):
    me = me_ref[0].astype(jnp.float32)
    turn = (lax.broadcasted_iota(jnp.int32, (1, 512), 1) // 64).astype(jnp.float32)
    row = lax.broadcasted_iota(jnp.int32, (256, 512), 0).astype(jnp.float32)
    line = lax.broadcasted_iota(jnp.int32, (128, 512), 0).astype(jnp.float32)

    def source(s, carry):
        meta = table_ref[s].astype(jnp.float32)
        for g in range(2):
            owner, high, spot, upper, lower = [meta[2 * f + g : 2 * f + g + 1] for f in range(5)]
            key = jnp.where(owner == me, high * 8.0 + turn, -1.0)
            left = jnp.where(row == key, 1.0, 0.0).astype(jnp.bfloat16)
            hit = line == spot
            right = jnp.concatenate(
                [jnp.where(hit, 1.0, 0.0), jnp.where(hit, upper, 0.0), jnp.where(hit, lower, 0.0)], axis=0
            ).astype(jnp.bfloat16)
            out = dot_rows(left, right)
            at = pl.ds(pl.multiple_of(s * 16 + g * 8, 8), 8)
            count_ref[:, at, :] = out[:, :128].reshape(32, 8, 128)
            share_ref[:, at, :] = (out[:, 128:256] + out[:, 256:]).reshape(32, 8, 128)
        return carry

    lax.fori_loop(0, 16, source, 0, unroll=2)


def picks(me, asked, after):
    vmem = pl.BlockSpec(memory_space=pltpu.VMEM)
    return pl.pallas_call(
        picks_kernel,
        out_shape=(jax.ShapeDtypeStruct((32, 256, 128), jnp.float32),) * 2,
        in_specs=[pl.BlockSpec(memory_space=pltpu.SMEM), vmem, anywhere],
        out_specs=(vmem, vmem),
        compiler_params=limit(24),
        cost_estimate=cost(10),
    )(me, asked, after)


def score_kernel(ask_ref, count_ref, slab_hbm, weight_ref, stat_ref, scores, slab, sems):
    loads = []
    for block in range(8):
        rows = pl.ds(block * 512, 512)
        loads.append(pltpu.make_async_copy(slab_hbm.at[rows], slab.at[rows], sems.at[block]))
        loads[-1].start()
    both = jnp.concatenate(
        [ask_ref[:, :, :768].reshape(256, 768), ask_ref[:, :, 768:].reshape(256, 768)], axis=0
    )
    top = jnp.full((256, 128), low, jnp.float32)
    for block in range(8):
        loads[block].wait()
        got = dot_rows(both, slab[block * 512 : block * 512 + 512])
        got = got[:256] + got[256:]
        for i in range(4):
            part = got[:, i * 128 : i * 128 + 128]
            scores[block * 4 + i] = part
            top = jnp.maximum(top, jnp.where(count_ref[block * 4 + i] > 0, part, low))
    top = jnp.max(top, axis=1, keepdims=True)
    mass = jnp.zeros((256, 128), jnp.float32)
    for high in range(32):
        here = count_ref[high]
        part = jnp.where(here > 0, here * jnp.exp(jnp.minimum(scores[high] - top, 0.0)), 0.0)
        mass = mass + part
        weight_ref[high] = part
    mass = jnp.sum(mass, axis=1, keepdims=True)
    lane = lax.broadcasted_iota(jnp.int32, (256, 128), 1)
    stat = jnp.transpose(jnp.where(lane == 0, top, mass))[:8]
    for to in range(16):
        stat_ref[to] = stat


def score(asked, count, slab):
    vmem = pl.BlockSpec(memory_space=pltpu.VMEM)
    return pl.pallas_call(
        score_kernel,
        out_shape=(
            jax.ShapeDtypeStruct((32, 256, 128), jnp.float32),
            jax.ShapeDtypeStruct((16, 8, 256), jnp.float32),
        ),
        in_specs=[vmem, vmem, pl.BlockSpec(memory_space=pltpu.MemorySpace.HBM)],
        out_specs=(vmem, vmem),
        scratch_shapes=[
            pltpu.VMEM((32, 256, 128), jnp.float32),
            pltpu.VMEM((4096, 768), jnp.bfloat16),
            pltpu.SemaphoreType.DMA((8,)),
        ],
        compiler_params=limit(28),
        cost_estimate=cost(8),
    )(asked, count, slab)


def pull_kernel(me_ref, stat_ref, weight_ref, share_ref, slab_ref, out_ref, factor, total):
    step = pl.program_id(0)

    @pl.when(step == 0)
    def _():
        stats = stat_ref[...]
        tops, masses = stats[:, 0], stats[:, 1]
        best = jnp.max(tops, axis=0, keepdims=True)
        mass = jnp.sum(jnp.exp(tops - best) * masses, axis=0, keepdims=True)
        mine = stat_ref[me_ref[0]][0:1]
        line = loss_scale * jnp.exp(mine - best) / mass
        factor[...] = jnp.transpose(jnp.broadcast_to(line, (128, 256)))
        total[...] = jnp.zeros_like(total)

    coef = jnp.concatenate(
        [weight_ref[i] * factor[...] - loss_scale * share_ref[i] for i in range(4)], axis=1
    )
    both = jnp.concatenate(halves(coef), axis=0)
    got = jnp.dot(both, slab_ref[...], preferred_element_type=jnp.float32)
    total[...] += got[:256] + got[256:]

    @pl.when(step == 7)
    def _():
        out_ref[...] = total[...].astype(jnp.bfloat16)


def pull(me, stats, weight, share, slab):
    quarter = pl.BlockSpec((4, 256, 128), lambda j, me: (j, 0, 0))
    return pl.pallas_call(
        pull_kernel,
        grid_spec=pltpu.PrefetchScalarGridSpec(
            num_scalar_prefetch=1,
            grid=(8,),
            in_specs=[whole(16, 8, 256), quarter, quarter, pl.BlockSpec((512, 768), lambda j, me: (j, 0))],
            out_specs=whole(256, 768),
            scratch_shapes=[pltpu.VMEM((256, 128), jnp.float32), pltpu.VMEM((256, 768), jnp.float32)],
        ),
        out_shape=jax.ShapeDtypeStruct((256, 768), jnp.bfloat16),
        compiler_params=limit(16),
        cost_estimate=cost(5),
    )(me, stats, weight, share, slab)


def resid_kernel(came_ref, normed_ref, rstd_ref, vectors_ref, resid_grad_ref, out_grad_ref, ups):
    step = pl.program_id(0)

    @pl.when(step == 0)
    def _():
        ups[...] = jnp.sum(came_ref[...].astype(jnp.float32), axis=0) * (1 / 64) * vectors_ref[:, 768:1536]

    for q in range(4):
        up = ups[pl.ds(step * 4 + q, 1), :]
        rows = slice(q * 64, q * 64 + 64)
        normed = normed_ref[rows, :]
        along = jnp.mean(up * normed, axis=-1, keepdims=True)
        grad = (up - jnp.mean(up, axis=-1, keepdims=True) - normed * along) * rstd_ref[rows, :]
        resid_grad_ref[rows, :] = grad
        out_grad_ref[rows, :] = grad.astype(jnp.bfloat16)


def resid_gradient(came, normed, rstd, vectors):
    rows = pl.BlockSpec((256, 768), lambda j: (j, 0))
    return pl.pallas_call(
        resid_kernel,
        grid=(4,),
        in_specs=[
            whole(16, 16, 768),
            rows,
            pl.BlockSpec((256, 1), lambda j: (j, 0)),
            whole(1, 3072),
        ],
        out_specs=(rows, rows),
        out_shape=(
            jax.ShapeDtypeStruct((1024, 768), jnp.float32),
            jax.ShapeDtypeStruct((1024, 768), jnp.bfloat16),
        ),
        scratch_shapes=[pltpu.VMEM((16, 768), jnp.float32)],
        compiler_params=limit(16),
        cost_estimate=cost(2),
    )(came, normed, rstd, vectors)


def weight_kernel(place_ref, left_ref, right_ref, away_ref, kept_ref):
    got = columns_dot(left_ref[...], right_ref[...])
    core = place_ref[0]
    for mine in range(2):

        @pl.when(core == mine)
        def _():
            kept_ref[0] = got[mine * 384 : mine * 384 + 384].astype(jnp.bfloat16)
            away_ref[0] = got[384 - mine * 384 : 768 - mine * 384].astype(jnp.bfloat16)


def weight_sums(place, left, right):
    return pl.pallas_call(
        weight_kernel,
        grid_spec=pltpu.PrefetchScalarGridSpec(
            num_scalar_prefetch=1,
            grid=(4,),
            in_specs=[pl.BlockSpec((1024, 768), lambda j, place: (0, j)), whole(1024, 768)],
            out_specs=(pl.BlockSpec((1, 384, 768), lambda j, place: (j, 0, 0)),) * 2,
        ),
        out_shape=(jax.ShapeDtypeStruct((4, 384, 768), jnp.bfloat16),) * 2,
        compiler_params=limit(56),
        cost_estimate=cost(40),
    )(place, left, right)


def second_kernel(place_ref, kept_ref, came_ref, carry_ref, own_ref, one_ref, three_ref, two_ref, carried_ref):
    for out, step in ((own_ref, 0), (one_ref, 1), (three_ref, 3), (two_ref, 2)):
        at = (place_ref[1] + step) % 4
        out[...] = (kept_ref[at].astype(jnp.float32) + came_ref[at].astype(jnp.float32)).astype(out.dtype)


def second_pair(place, kept, came, carry):
    block = lambda j, place: (0, j, 0)
    piece = pl.BlockSpec((96, 768), lambda j, place: (j, 0))
    return pl.pallas_call(
        second_kernel,
        grid_spec=pltpu.PrefetchScalarGridSpec(
            num_scalar_prefetch=1,
            grid=(4,),
            in_specs=[pl.BlockSpec((4, 96, 768), block), pl.BlockSpec((4, 96, 768), block), anywhere],
            out_specs=(piece,) * 4 + (anywhere,),
        ),
        out_shape=(jax.ShapeDtypeStruct((384, 768), jnp.float32),)
        + (jax.ShapeDtypeStruct((384, 768), jnp.bfloat16),) * 3
        + (jax.ShapeDtypeStruct(carry.shape, carry.dtype),),
        input_output_aliases={3: 4},
        compiler_params=limit(56),
        cost_estimate=cost(5),
    )(place, kept, came, carry)


def first_kernel(place_ref, kept_ref, came_ref, *refs):
    own_ref, one_ref, three_ref, two_ref, right_ref = refs[-6:-1]
    for out, step in ((own_ref, 0), (one_ref, 1), (three_ref, 3), (two_ref, 2)):
        at = (place_ref[1] + step) % 4
        got = kept_ref[at, :, :384].astype(jnp.float32) + came_ref[at, :, :384].astype(jnp.float32)
        out[...] = got.astype(out.dtype)
    right = [
        kept_ref[y, :, 384:].astype(jnp.float32) + came_ref[y, :, 384:].astype(jnp.float32) for y in range(4)
    ]
    for i in range(4):
        rows = slice(i * 24, i * 24 + 24)
        right_ref[i] = jnp.concatenate([part[rows] for part in right], axis=0).astype(jnp.bfloat16)


def first_pair(place, kept, came, carry, *after):
    block = lambda j, place: (0, j, 0)
    piece = pl.BlockSpec((96, 384), lambda j, place: (j, 0))
    return pl.pallas_call(
        first_kernel,
        grid_spec=pltpu.PrefetchScalarGridSpec(
            num_scalar_prefetch=1,
            grid=(4,),
            in_specs=[pl.BlockSpec((4, 96, 768), block), pl.BlockSpec((4, 96, 768), block)]
            + [anywhere] * (1 + len(after)),
            out_specs=(piece,) * 4 + (pl.BlockSpec((4, 96, 384), lambda j, place: (j, 0, 0)), anywhere),
        ),
        out_shape=(jax.ShapeDtypeStruct((384, 384), jnp.float32),)
        + (jax.ShapeDtypeStruct((384, 384), jnp.bfloat16),) * 3
        + (
            jax.ShapeDtypeStruct((16, 96, 384), jnp.bfloat16),
            jax.ShapeDtypeStruct(carry.shape, carry.dtype),
        ),
        input_output_aliases={3: 5},
        compiler_params=limit(56),
        cost_estimate=cost(5),
    )(place, kept, came, carry, *after)


def hold(carry, *after):
    return pl.pallas_call(
        lambda *refs: None,
        in_specs=[anywhere] * (1 + len(after)),
        out_specs=anywhere,
        out_shape=jax.ShapeDtypeStruct(carry.shape, carry.dtype),
        input_output_aliases={0: 0},
        compiler_params=limit(56),
        cost_estimate=cost(1),
    )(carry, *after)


def mark_kernel(own_ref, out_ref):
    out_ref[...] = own_ref[...]


def mark(own):
    tile = pl.BlockSpec((8, 128), lambda j: (0, 0))
    return pl.pallas_call(
        mark_kernel,
        grid=(1,),
        in_specs=[tile],
        out_specs=tile,
        out_shape=jax.ShapeDtypeStruct((8, 128), jnp.float32),
        compiler_params=limit(56),
        cost_estimate=cost(100),
    )(own)


def left_kernel(*refs):
    out_ref = refs[-1]
    for parts, cols in ((refs[:4], slice(0, 384)), (refs[4:8], slice(384, 1152))):
        total = parts[0][...]
        for part in parts[1:]:
            total = total + part[...].astype(jnp.float32)
        out_ref[:, cols] = total.astype(jnp.bfloat16)


def left_sums(first, second, after):
    narrow, wide = (pl.BlockSpec((96, n), lambda j: (j, 0)) for n in (384, 768))
    return pl.pallas_call(
        left_kernel,
        grid=(4,),
        in_specs=[narrow] * 4 + [wide] * 4 + [anywhere],
        out_specs=pl.BlockSpec((96, 1152), lambda j: (j, 0)),
        out_shape=jax.ShapeDtypeStruct((384, 1152), jnp.bfloat16),
        compiler_params=limit(56),
        cost_estimate=cost(2),
    )(*first, *second, after)


def right_kernel(y_ref, came_ref, after_ref, own_ref, one_ref, three_ref, two_ref, total):
    total[...] = jnp.sum(came_ref[...].astype(jnp.float32), axis=0)
    for out, step in ((own_ref, 0), (one_ref, 1), (three_ref, 3), (two_ref, 2)):
        at = (y_ref[0] + step) % 4
        out[...] = total[pl.ds(pl.multiple_of(at * 24, 8), 24), :]


def right_sums(y, came, after):
    vmem = pl.BlockSpec(memory_space=pltpu.VMEM)
    return pl.pallas_call(
        right_kernel,
        in_specs=[pl.BlockSpec(memory_space=pltpu.SMEM), vmem, anywhere],
        out_specs=(vmem,) * 4,
        out_shape=(jax.ShapeDtypeStruct((24, 384), jnp.float32),) * 4,
        scratch_shapes=[pltpu.VMEM((96, 384), jnp.float32)],
        compiler_params=limit(8),
        cost_estimate=cost(1),
    )(y, came, after)


def last_kernel(devices, left_ref, own_ref, one_ref, three_ref, two_ref, out_ref):
    left = jnp.sum(left_ref[...].astype(jnp.float32), axis=0) / devices
    right = (own_ref[...] + one_ref[...] + three_ref[...] + two_ref[...]) / devices
    out_ref[:, :384] = left[:, :384]
    out_ref[:, 384:768] = right
    out_ref[:, 768:] = left[:, 384:]


def last_sums(devices, left, *right):
    vmem = pl.BlockSpec(memory_space=pltpu.VMEM)
    return pl.pallas_call(
        lambda *refs: last_kernel(devices, *refs),
        in_specs=[vmem] * 5,
        out_specs=vmem,
        out_shape=jax.ShapeDtypeStruct((24, 1536), jnp.float32),
        compiler_params=limit(8),
        cost_estimate=cost(1),
    )(left, *right)


def body(
    tokens, w_in, bias_in, w_out, bias_out, gain, shift, slab, owners, offsets, reader_weights
):
    devices = lax.axis_size("query") * lax.axis_size("index")
    me = lax.axis_index("index")[None]
    y = lax.axis_index("query") // 2
    core = lax.axis_index("query") % 2
    place = jnp.stack([core, y])

    asked = exchange(table(owners[..., 0], offsets, reader_weights))
    vectors = jnp.concatenate([bias_out, gain, shift, jnp.zeros_like(shift)]).reshape(1, 3072)
    hidden, slopes, normed, rstd, ask = forward(tokens, w_in, bias_in, w_out, vectors)
    count, share = picks(me, asked, rstd)
    weight, stat = score(exchange(ask), count, slab)
    partial = pull(me, exchange(stat), weight, share, slab)
    came = exchange(partial.reshape(16, 16, 768))
    resid_grad, out_grad = resid_gradient(came, normed, rstd, vectors)

    def round_y(own, *pieces):
        return [own] + [shifted(piece, 0, step) for piece, step in zip(pieces, (1, 3, 2))]

    away, kept = weight_sums(place, hidden, out_grad)
    pre_grad = (
        jnp.dot(out_grad, w_out.T, preferred_element_type=jnp.float32) * slopes.astype(jnp.float32)
    ).astype(jnp.bfloat16)
    *second, pre_grad = second_pair(place, kept, shifted(away, 1, 0), pre_grad)
    second = round_y(*second)
    away, kept = weight_sums(place, pre_grad, tokens)
    away = hold(away, second[1], second[2])
    *first, packed, pre_grad = first_pair(
        place, kept, shifted(away, 1, 0), pre_grad, mark(second[0])
    )
    first = round_y(*first)
    right = exchange(packed)
    token_grads = (
        resid_grad + jnp.dot(pre_grad, w_in.T, preferred_element_type=jnp.float32)
    ).astype(jnp.bfloat16)

    left = exchange(left_sums(first, second, token_grads).reshape(16, 24, 1152))
    own, one, three, two = right_sums(y[None], right, token_grads)
    right = round_y(own, one, three, two)
    return (token_grads, last_sums(devices, left, *right))


def solution(mesh):
    placed = (
        P(("query", "index"), None),
        P(),
        P(),
        P(),
        P(),
        P(),
        P(),
        P("index", None),
        P(("query", "index"), None, None),
        P(("query", "index"), None),
        P(("query", "index"), None),
    )
    return jax.shard_map(
        body,
        mesh=mesh,
        in_specs=placed,
        out_specs=(P(("query", "index"), None), P(("query", "index"), None)),
        check_vma=False,
    )
```

time: 231 us -> 207 us (0.90)
  waiting for transfers between devices: 49.2 us -> 30.1 us
  matrix products: 28.9 us -> 18.9 us
  local copies, waits for them, and re-layouts: 18.8 us -> 25.9 us
  other arithmetic: 3.64 us -> 0.57 us
    pallas_call x3 -> x9, Pallas kernels: 17.8 us -> 43.2 us  [the longest x2 20.8 us: weight_sums(): pl.pallas_call(weight_kernel, grid_spec=pltpu.PrefetchScalarGridSpec(num_...]
    all_to_all x5, waiting for transfers between devices: 45.8 us -> 24.1 us  [exchange(): return lax.all_to_all(value, 'index', 0, 0, tiled=True)]
    unnamed x42 -> x66, local copies, waits for them, and re-layouts: 10.7 us -> 25.9 us
    dot_general x2 -> x0, matrix products: 10.4 us -> none  [columns_dot(): lax.dot_general(left, right, (((0,), (0,)), ((), ())), preferred_element_...]
    pallas_call x1, Pallas kernels: 15.1 us -> 6.61 us  [score(): pl.pallas_call(score_kernel, out_shape=(jax.ShapeDtypeStruct((32, 256, 12...]
    pallas_call x1, Pallas kernels: 10.3 us -> 5.73 us  [pull(): pl.pallas_call(pull_kernel, grid_spec=pltpu.PrefetchScalarGridSpec(num_sc...]
    pallas_call x1, Pallas kernels: 5.32 us -> 1.08 us  [resid_gradient(): pl.pallas_call(resid_kernel, grid=(4,), in_specs=[whole(16, 16, 768), row...]
    reshape x4 -> x0, local copies, waits for them, and re-layouts: 3.86 us -> none  [the longest x1 1.28 us: forward(): gain.reshape(1, -1)]
  transfers between devices with their start and end apart: 16 -> 16, of which waited for: 7 -> 7; matrix products, arithmetic and copies ran while one was open for 8% -> 9% of each run, Pallas kernels for 9% -> 22%
where the time goes in v3:
time: 207 us; the launch traced here: 205 us
  Pallas kernels  76.9 us (37%)
  starting transfers between devices  40.9 us (20%)
  waiting for transfers between devices  30.1 us (15%)
  local copies, waits for them, and re-layouts  25.9 us (13%)
  matrix products  18.9 us (9%)
  blocking collectives  11.1 us (5%)
    all_to_all x5, starting transfers between devices, exchange(): return lax.all_to_all(value, 'index', 0, 0, tiled=True)  26.1 us
    unnamed x66, local copies, waits for them, and re-layouts  25.9 us
    all_to_all x5, waiting for transfers between devices, exchange(): return lax.all_to_all(value, 'index', 0, 0, tiled=True)  24.1 us
    pallas_call x2, Pallas kernels, weight_sums(): pl.pallas_call(weight_kernel, grid_spec=pltpu.PrefetchScalarGridSpec(num_...  20.8 us
    pallas_call x1, Pallas kernels, forward(): pl.pallas_call(forward_kernel, grid=(3072 // block,), in_specs=[whole(102...  19.3 us
    ppermute x11, starting transfers between devices, shifted(): return lax.ppermute(value, every, pairs)  14.8 us
    all_to_all x1, blocking collectives, exchange(): return lax.all_to_all(value, 'index', 0, 0, tiled=True)  11.1 us
    dot_general x1, matrix products, body(): jnp.dot(pre_grad, w_in.T, preferred_element_type=jnp.float32)  9.97 us
  transfers between devices with their start and end apart: 16, of which 7 were waited for; matrix products, arithmetic and copies ran while one was open for 9% of the time, Pallas kernels for 22%

profile of v3, /device:TPU:0, one launch (start us, length us, event | category | flops | bytes accessed | tf_op | source)
XLA Modules:
  0.0 205.3 jit_solution(7298003963296244590)
XLA Ops:
  0.6 0.0 copy-start.3
  0.7 0.8 copy-done.5
  1.5 0.7 copy-done.6
  2.2 0.7 copy-done.7
  2.9 0.9 shard_map.123
  3.8 8.0 %all-to-all-start.1 = ((bf16[16,16,512]{2,1,0:T(8,128)(2,1)}), bf16[16,16,512]{2,1,0:T(8,128)(2,1)S(1)}, u32[]{:S(2)}, u32[]{:S(2)}) async-start(bf16[16,16,512]{2,1,0:T(8,128)(2,1)} %shard_map.123), calls=%async_computation.1 | async-start | bytes 524288 | tf_op jit(solution)/shard_map/all_to_all | solution.py:38
  11.8 0.0 copy-start.1
  11.8 2.3 %copy-done.1 = bf16[3072,768]{1,0:T(8,128)(2,1)S(1)} copy-done((bf16[3072,768]{1,0:T(8,128)(2,1)S(1)}, bf16[3072,768]{1,0:T(8,128)(2,1)}, u32[]{:S(2)}) %copy-start.1) | copy-done | bytes 4718616
  14.1 2.3 %copy-done.2 = bf16[768,3072]{1,0:T(8,128)(2,1)S(1)} copy-done((bf16[768,3072]{1,0:T(8,128)(2,1)S(1)}, bf16[768,3072]{1,0:T(8,128)(2,1)}, u32[]{:S(2)}) %copy-start.2) | copy-done | bytes 4718616
  16.5 19.3 %shard_map.122 = (bf16[1024,3072]{1,0:T(8,128)(2,1)}, bf16[1024,3072]{1,0:T(8,128)(2,1)}, f32[1024,768]{1,0:T(8,128)S(1)}, f32[1024,1]{1,0:T(8,128)S(1)}, bf16[16,16,1536]{2,1,0:T(8,128)(2,1)}) custom-call(bf16[1024,768]{1,0:T(8,128)(2,1)S(1)} %copy-done.3, bf16[768,3072]{1,0:T(8,128)(2,1)S(1)} %copy-done.2, f32[1,3072]{1,0:T(1,128)S(1)} %bitcast.16, ...), custom_call_target="tpu_custom_call" | custom-call | flops 20000000000 | bytes 1000 | tf_op jit(solution)/shard_map/pallas_call | solution.py:104
  35.8 1.6 copy-done.11
  37.4 0.0 all-to-all-done.1.table_ref
  37.4 7.2 %all-to-all-start = ((bf16[16,16,1536]{2,1,0:T(8,128)(2,1)}), bf16[16,16,1536]{2,1,0:T(8,128)(2,1)S(1)}, u32[]{:S(2)}, u32[]{:S(2)}) async-start(bf16[16,16,1536]{2,1,0:T(8,128)(2,1)} %get-tuple-element.32), calls=%async_computation | async-start | bytes 1572864 | tf_op jit(solution)/shard_map/all_to_all | solution.py:38
  44.6 5.9 %shard_map.124 = (f32[32,256,128]{2,1,0:T(8,128)S(1)}, f32[32,256,128]{2,1,0:T(8,128)S(1)}) custom-call(s32[1]{0:T(128)} %bitcast.me_ref, bf16[16,16,512]{2,1,0:T(8,128)(2,1)S(1)} %all-to-all-done.1.table_ref, f32[1024,1]{1,0:T(8,128)S(1)} %get-tuple-element.33.after_ref.rstd_ref), custom_call_target="tpu_custom_call" | custom-call | flops 10000000000 | bytes 1000 | tf_op jit(solution)/shard_map/pallas_call | solution.py:189
  50.5 1.9 copy-done.9
  52.5 2.0 copy-done.18
  54.4 4.0 %all-to-all-done.ask_ref = bf16[16,16,1536]{2,1,0:T(8,128)(2,1)S(1)} async-done(((bf16[16,16,1536]{2,1,0:T(8,128)(2,1)}), bf16[16,16,1536]{2,1,0:T(8,128)(2,1)S(1)}, u32[]{:S(2)}, u32[]{:S(2)}) %all-to-all-start) | async-done | bytes 786464 | tf_op jit(solution)/shard_map/all_to_all | solution.py:38
  58.4 2.8 %copy-done = bf16[4096,768]{1,0:T(8,128)(2,1)S(1)} copy-done((bf16[4096,768]{1,0:T(8,128)(2,1)S(1)}, bf16[4096,768]{1,0:T(8,128)(2,1)}, u32[]{:S(2)}) %copy-start) | copy-done | bytes 6291480
  61.2 2.2 %copy-done.19 = f32[32,256,128]{2,1,0:T(8,128)S(1)} copy-done((f32[32,256,128]{2,1,0:T(8,128)S(1)}, f32[32,256,128]{2,1,0:T(8,128)}, u32[]{:S(2)}) %copy-start.19) | copy-done | bytes 4194328
  63.4 6.6 %shard_map.125 = (f32[32,256,128]{2,1,0:T(8,128)S(1)}, f32[16,8,256]{2,1,0:T(8,128)S(1)}) custom-call(bf16[16,16,1536]{2,1,0:T(8,128)(2,1)S(1)} %all-to-all-done.ask_ref, f32[32,256,128]{2,1,0:T(8,128)S(1)} %copy-done.19, bf16[4096,768]{1,0:T(8,128)(2,1)S(1)} %copy-done), custom_call_target="tpu_custom_call" | custom-call | flops 8000000000 | bytes 1000 | tf_op jit(solution)/shard_map/pallas_call | solution.py:233
  70.0 11.1 %all_to_all.30.stat_ref = f32[16,8,256]{2,1,0:T(8,128)S(1)} all-to-all(f32[16,8,256]{2,1,0:T(8,128)S(1)} %get-tuple-element.35), channel_id=1, replica_groups=mesh['query'=8,'index'=16] {'index'}, dimensions={0} | all-to-all | bytes 262144 | tf_op jit(solution)/shard_map/all_to_all | solution.py:38
  81.1 5.7 %shard_map.126 = bf16[256,768]{1,0:T(8,128)(2,1)} custom-call(s32[1]{0:T(128)} %bitcast.me_ref, f32[16,8,256]{2,1,0:T(8,128)S(1)} %all_to_all.30.stat_ref, f32[32,256,128]{2,1,0:T(8,128)S(1)} %get-tuple-element.36.weight_ref, f32[32,256,128]{2,1,0:T(8,128)S(1)} %copy-done.10, bf16[4096,768]{1,0:T(8,128)(2,1)S(1)} %copy-done), custom_call_target="tpu_custom_call" | custom-call | flops 5000000000 | bytes 1000 | tf_op jit(solution)/shard_map/pallas_call | solution.py:279
  86.9 3.6 %all-to-all-start.3 = ((bf16[16,16,768]{2,1,0:T(8,128)(2,1)}), bf16[16,16,768]{2,1,0:T(8,128)(2,1)S(1)}, u32[]{:S(2)}, u32[]{:S(2)}) async-start(bf16[16,16,768]{2,1,0:T(8,128)(2,1)} %bitcast.4), calls=%async_computation.3 | async-start | bytes 786432 | tf_op jit(solution)/shard_map/all_to_all | solution.py:38
  90.4 0.6 pad_add_fusion.place_ref
  91.0 8.8 %all-to-all-done.3.came_ref = bf16[16,16,768]{2,1,0:T(8,128)(2,1)S(1)} async-done(((bf16[16,16,768]{2,1,0:T(8,128)(2,1)}), bf16[16,16,768]{2,1,0:T(8,128)(2,1)S(1)}, u32[]{:S(2)}, u32[]{:S(2)}) %all-to-all-start.3) | async-done | bytes 393248 | tf_op jit(solution)/shard_map/all_to_all | solution.py:38
  99.8 1.0 copy-done.17
  100.8 1.1 shard_map.127
  101.9 1.6 copy-done.13
  103.6 1.1 copy-done.14
  104.7 10.6 %shard_map.128 = (bf16[4,384,768]{2,1,0:T(8,128)(2,1)}, bf16[4,384,768]{2,1,0:T(8,128)(2,1)}) custom-call(s32[2]{0:T(128)} %pad_add_fusion.place_ref, bf16[1024,3072]{1,0:T(8,128)(2,1)} %get-tuple-element.40.left_ref, bf16[1024,768]{1,0:T(8,128)(2,1)} %copy-done.14), custom_call_target="tpu_custom_call" | custom-call | flops 40000000000 | bytes 1000 | tf_op jit(solution)/shard_map/pallas_call | solution.py:345
  115.3 0.0 collective-permute-start
  115.3 8.9 %multiply_convert_fusion.carry_ref = bf16[1024,3072]{1,0:T(8,128)(2,1)} fusion(bf16[1024,3072]{1,0:T(8,128)(2,1)} %get-tuple-element.44, bf16[1024,768]{1,0:T(8,128)(2,1)S(1)} %copy-done.15, bf16[3072,768]{1,0:T(8,128)(2,1)S(1)} %bitcast.15), kind=kOutput, calls=%fused_computation | convolution fusion | flops 4841275392 | bytes 18874368 | tf_op jit(solution)/shard_map/dot_general | solution.py:537
  124.2 5.1 %shard_map.129 = (f32[384,768]{1,0:T(8,128)}, bf16[384,768]{1,0:T(8,128)(2,1)}, bf16[384,768]{1,0:T(8,128)(2,1)}, bf16[384,768]{1,0:T(8,128)(2,1)}, bf16[1024,3072]{1,0:T(8,128)(2,1)}) custom-call(s32[2]{0:T(128)} %pad_add_fusion.place_ref, bf16[4,384,768]{2,1,0:T(8,128)(2,1)} %get-tuple-element.42.kept_ref, ...), custom_call_target="tpu_custom_call", output_to_operand_aliasing={{4}: (3, {})} | custom-call | flops 5000000000 | bytes 1000 | tf_op jit(solution)/shard_map/pallas_call | solution.py:368
  129.4 1.6 collective-permute-start.1
  131.0 1.7 collective-permute-start.2
  132.6 10.2 %shard_map.130 = (bf16[4,384,768]{2,1,0:T(8,128)(2,1)}, bf16[4,384,768]{2,1,0:T(8,128)(2,1)}) custom-call(s32[2]{0:T(128)} %pad_add_fusion.place_ref, bf16[1024,3072]{1,0:T(8,128)(2,1)} %get-tuple-element.45.left_ref.refs_0_, bf16[1024,768]{1,0:T(8,128)(2,1)} %right_ref.1), custom_call_target="tpu_custom_call" | custom-call | flops 40000000000 | bytes 1000 | tf_op jit(solution)/shard_map/pallas_call | solution.py:345
  142.8 3.7 %collective-permute-done.1.refs_1_.refs_5_ = bf16[384,768]{1,0:T(8,128)(2,1)S(1)} collective-permute-done((bf16[384,768]{1,0:T(8,128)(2,1)}, bf16[384,768]{1,0:T(8,128)(2,1)S(1)}, u32[]{:S(2)}, u32[]{:S(2)}) %collective-permute-start.1) | collective-permute-done | bytes 589856 | tf_op jit(solution)/shard_map/ppermute | solution.py:47
  146.6 0.0 collective-permute-done.2.refs_2_.refs_6_
  146.6 0.8 copy-done.20
  147.4 0.2 copy-done.21
  147.6 0.0 collective-permute-start.3
  147.6 1.3 shard_map.132.refs_1_
  149.0 2.7 %collective-permute-start.7 = (bf16[384,768]{1,0:T(8,128)(2,1)S(1)}, bf16[384,768]{1,0:T(8,128)(2,1)S(1)}, u32[]{:S(2)}, u32[]{:S(2)}) collective-permute-start(bf16[384,768]{1,0:T(8,128)(2,1)S(1)} %copy-done.26), channel_id=1, source_target_pairs={{0,64},{1,65},{2,66},{3,67},{4,68},{5,69},{6,70},{7,71},{8,72},{9,... | collective-permute-start | bytes 1769480 | tf_op jit(solution)/shard_map/ppermute | solution.py:47
  151.7 0.7 collective-permute-done.3.came_ref
  152.4 1.5 copy-done.25
  153.8 5.1 %shard_map.133 = (f32[384,384]{1,0:T(8,128)}, bf16[384,384]{1,0:T(8,128)(2,1)}, bf16[384,384]{1,0:T(8,128)(2,1)}, bf16[384,384]{1,0:T(8,128)(2,1)}, bf16[16,96,3...) custom-call(s32[2]{0:T(128)} %pad_add_fusion.place_ref, ...), custom_call_target="tpu_custom_call", output_to_operand_aliasing={{5}: (3, {})} | custom-call | flops 5000000000 | bytes 1000 | tf_op jit(solution)/shard_map/pallas_call | solution.py:402
  158.9 1.4 collective-permute-start.4
  160.3 1.8 collective-permute-start.5
  162.1 1.5 collective-permute-start.6
  163.6 3.7 %all-to-all-start.5 = ((bf16[16,96,384]{2,1,0:T(8,128)(2,1)}), bf16[16,96,384]{2,1,0:T(8,128)(2,1)S(1)}, u32[]{:S(2)}, u32[]{:S(2)}) async-start(bf16[16,96,384]{2,1,0:T(8,128)(2,1)} %get-tuple-element.57), calls=%async_computation.5 | async-start | bytes 2359296 | tf_op jit(solution)/shard_map/all_to_all | solution.py:38
  167.3 10.0 %add_convert_fusion.refs_8_.after_ref = bf16[1024,768]{1,0:T(8,128)(2,1)} fusion(f32[1024,768]{1,0:T(8,128)} %copy-done.13, bf16[1024,3072]{1,0:T(8,128)(2,1)} %get-tuple-element.51, bf16[768,3072]{1,0:T(8,128)(2,1)} %w_in_ref.1), kind=kOutput, calls=%fused_computation.1 | convolution fusion | flops 4833411072 | bytes 15728640 | tf_op jit(solution)/shard_map/dot_general | solution.py:549
  177.4 1.5 collective-permute-done.6.refs_3_
  178.9 0.7 copy-done.30
  179.6 4.2 %shard_map.134 = bf16[384,1152]{1,0:T(8,128)(2,1)} custom-call(f32[384,384]{1,0:T(8,128)} %get-tuple-element.52.refs_0_, bf16[384,384]{1,0:T(8,128)(2,1)} %copy-done.28, bf16[384,384]{1,0:T(8,128)(2,1)} %copy-done.29, bf16[384,384]{1,0:T(8,128)(2,1)} %copy-done.30, f32[384,768]{1,0:T(8,128)} %get-tuple-element.50.own_ref.refs_4_, ...), custom_call_target="tpu_custom_call" | custom-call | flops 2000000000 | bytes 1000 | tf_op jit(solution)/shard_map/pallas_call | solution.py:463
  183.8 2.5 %all-to-all-done.5.came_ref = bf16[16,96,384]{2,1,0:T(8,128)(2,1)S(1)} async-done(((bf16[16,96,384]{2,1,0:T(8,128)(2,1)}), bf16[16,96,384]{2,1,0:T(8,128)(2,1)S(1)}, u32[]{:S(2)}, u32[]{:S(2)}) %all-to-all-start.5) | async-done | bytes 1179680 | tf_op jit(solution)/shard_map/all_to_all | solution.py:38
  186.3 3.6 %all-to-all-start.4 = ((bf16[16,24,1152]{2,1,0:T(8,128)(2,1)}), bf16[16,24,1152]{2,1,0:T(8,128)(2,1)S(1)}, u32[]{:S(2)}, u32[]{:S(2)}) async-start(bf16[16,24,1152]{2,1,0:T(8,128)(2,1)} %bitcast.18), calls=%async_computation.4 | async-start | bytes 1769472 | tf_op jit(solution)/shard_map/all_to_all | solution.py:38
  189.9 0.0 copy-start.8
  189.9 1.4 copy-done.8
  191.3 0.2 shard_map.135
  191.5 1.0 collective-permute-start.8
  192.6 2.3 %collective-permute-start.9 = (f32[24,384]{1,0:T(8,128)S(1)}, f32[24,384]{1,0:T(8,128)S(1)}, u32[]{:S(2)}, u32[]{:S(2)}) collective-permute-start(f32[24,384]{1,0:T(8,128)S(1)} %get-tuple-element.60), channel_id=1, source_target_pairs={{0,96},{1,97},{2,98},{3,99},{4,100},{5,101},{6,102},{7,103},{8,104... | collective-permute-start | bytes 110600 | tf_op jit(solution)/shard_map/ppermute | solution.py:47
  194.8 0.8 collective-permute-start.10
  195.7 8.8 %all-to-all-done.4.refs_0_ = bf16[16,24,1152]{2,1,0:T(8,128)(2,1)S(1)} async-done(((bf16[16,24,1152]{2,1,0:T(8,128)(2,1)}), bf16[16,24,1152]{2,1,0:T(8,128)(2,1)S(1)}, u32[]{:S(2)}, u32[]{:S(2)}) %all-to-all-start.4) | async-done | bytes 884768 | tf_op jit(solution)/shard_map/all_to_all | solution.py:38
  204.5 0.8 shard_map.136
  (56 shorter events, 0.1 us)
Async XLA Ops:
  0.6 11.2 %copy-start.3 = (bf16[1024,768]{1,0:T(8,128)(2,1)S(1)}, bf16[1024,768]{1,0:T(8,128)(2,1)}, u32[]{:S(2)}) copy-start(bf16[1024,768]{1,0:T(8,128)(2,1)} %right_ref.1) | copy-start | bytes 4718596
  0.6 11.2 %copy-start.4 = (f32[3072]{0:T(1024)S(1)}, f32[3072]{0:T(1024)}, u32[]{:S(2)}) copy-start(f32[3072]{0:T(1024)} %param.13) | copy-start | bytes 36868
  0.7 0.8 copy-start.5
  1.5 0.7 copy-start.6
  2.2 0.7 copy-start.7
  2.9 8.9 %copy-start.22 = (f32[768]{0:T(1024)S(1)}, f32[768]{0:T(1024)}, u32[]{:S(2)}) copy-start(f32[768]{0:T(1024)} %param.17) | copy-start | bytes 9220
  2.9 8.9 %copy-start.23 = (f32[768]{0:T(1024)S(1)}, f32[768]{0:T(1024)}, u32[]{:S(2)}) copy-start(f32[768]{0:T(1024)} %param.16) | copy-start | bytes 9220
  2.9 8.9 %copy-start.24 = (f32[768]{0:T(1024)S(1)}, f32[768]{0:T(1024)}, u32[]{:S(2)}) copy-start(f32[768]{0:T(1024)} %param.15) | copy-start | bytes 9220
  3.8 33.7 %all-to-all-start.1 = ((bf16[16,16,512]{2,1,0:T(8,128)(2,1)}), bf16[16,16,512]{2,1,0:T(8,128)(2,1)S(1)}, u32[]{:S(2)}, u32[]{:S(2)}) async-start(bf16[16,16,512]{2,1,0:T(8,128)(2,1)} %shard_map.123), calls=%async_computation.1 | async-start | bytes 524288 | tf_op jit(solution)/shard_map/all_to_all | solution.py:38
  11.8 2.3 %copy-start.1 = (bf16[3072,768]{1,0:T(8,128)(2,1)S(1)}, bf16[3072,768]{1,0:T(8,128)(2,1)}, u32[]{:S(2)}) copy-start(bf16[3072,768]{1,0:T(8,128)(2,1)} %w_out_ref.1) | copy-start | bytes 14155780
  14.1 2.3 %copy-start.2 = (bf16[768,3072]{1,0:T(8,128)(2,1)S(1)}, bf16[768,3072]{1,0:T(8,128)(2,1)}, u32[]{:S(2)}) copy-start(bf16[768,3072]{1,0:T(8,128)(2,1)} %w_in_ref.1) | copy-start | bytes 14155780
  35.8 1.7 copy-start.11
  37.4 13.1 %copy-start.16 = (f32[1024,1]{1,0:T(8,128)}, f32[1024,1]{1,0:T(8,128)S(1)}, u32[]{:S(2)}) copy-start(f32[1024,1]{1,0:T(8,128)S(1)} %get-tuple-element.33.after_ref.rstd_ref) | copy-start | bytes 12292
  37.4 21.0 %all-to-all-start = ((bf16[16,16,1536]{2,1,0:T(8,128)(2,1)}), bf16[16,16,1536]{2,1,0:T(8,128)(2,1)S(1)}, u32[]{:S(2)}, u32[]{:S(2)}) async-start(bf16[16,16,1536]{2,1,0:T(8,128)(2,1)} %get-tuple-element.32), calls=%async_computation | async-start | bytes 1572864 | tf_op jit(solution)/shard_map/all_to_all | solution.py:38
  50.5 1.9 copy-start.9
  52.5 2.0 copy-start.18
  58.4 2.8 %copy-start = (bf16[4096,768]{1,0:T(8,128)(2,1)S(1)}, bf16[4096,768]{1,0:T(8,128)(2,1)}, u32[]{:S(2)}) copy-start(bf16[4096,768]{1,0:T(8,128)(2,1)} %slab_ref.1) | copy-start | bytes 18874372
  61.2 2.2 %copy-start.19 = (f32[32,256,128]{2,1,0:T(8,128)S(1)}, f32[32,256,128]{2,1,0:T(8,128)}, u32[]{:S(2)}) copy-start(f32[32,256,128]{2,1,0:T(8,128)} %copy-done.18) | copy-start | bytes 12582916
  63.4 17.7 %copy-start.10 = (f32[32,256,128]{2,1,0:T(8,128)S(1)}, f32[32,256,128]{2,1,0:T(8,128)}, u32[]{:S(2)}) copy-start(f32[32,256,128]{2,1,0:T(8,128)} %copy-done.9) | copy-start | bytes 12582916
  81.1 18.7 %copy-start.12 = (f32[1024,768]{1,0:T(8,128)S(1)}, f32[1024,768]{1,0:T(8,128)}, u32[]{:S(2)}) copy-start(f32[1024,768]{1,0:T(8,128)} %copy-done.11) | copy-start | bytes 9437188
  86.9 12.9 %all-to-all-start.3 = ((bf16[16,16,768]{2,1,0:T(8,128)(2,1)}), bf16[16,16,768]{2,1,0:T(8,128)(2,1)S(1)}, u32[]{:S(2)}, u32[]{:S(2)}) async-start(bf16[16,16,768]{2,1,0:T(8,128)(2,1)} %bitcast.4), calls=%async_computation.3 | async-start | bytes 786432 | tf_op jit(solution)/shard_map/all_to_all | solution.py:38
  99.8 1.0 copy-start.17
  100.8 14.5 %slice-start = ((s8[4718592]{0:T(1024)(128)(4,1)}), s8[4194304]{0:T(1024)(128)(4,1)S(1)}, s32[]{:S(2)}) async-start(s8[4718592]{0:T(1024)(128)(4,1)} %bitcast.14), calls=%async_computation.6 | async-start | bytes 8388608
  101.9 1.6 copy-start.13
  103.5 1.1 copy-start.14
  104.7 10.6 %slice-start.1 = ((s8[4718592]{0:T(1024)(128)(4,1)}), s8[524288]{0:T(1024)(128)(4,1)S(1)}, s32[]{:S(2)}) async-start(s8[4718592]{0:T(1024)(128)(4,1)} %bitcast.14), calls=%async_computation.7 | async-start | bytes 1048576
  104.7 10.6 %copy-start.15 = (bf16[1024,768]{1,0:T(8,128)(2,1)S(1)}, bf16[1024,768]{1,0:T(8,128)(2,1)}, u32[]{:S(2)}) copy-start(bf16[1024,768]{1,0:T(8,128)(2,1)} %copy-done.14) | copy-start | bytes 4718596
  115.3 9.0 %collective-permute-start = (bf16[4,384,768]{2,1,0:T(8,128)(2,1)}, bf16[4,384,768]{2,1,0:T(8,128)(2,1)}, u32[]{:S(2)}, u32[]{:S(2)}) collective-permute-start(bf16[4,384,768]{2,1,0:T(8,128)(2,1)} %get-tuple-element.43), channel_id=1, source_target_pairs={{0,16},{1,17},{2,18},{3,19},{4,20},{5,21},{6,22},{7,23},{8,24},{9,... | collective-permute-start | bytes 7077896 | tf_op jit(solution)/shard_map/ppermute | solution.py:47
  129.4 17.2 %collective-permute-start.1 = (bf16[384,768]{1,0:T(8,128)(2,1)}, bf16[384,768]{1,0:T(8,128)(2,1)S(1)}, u32[]{:S(2)}, u32[]{:S(2)}) collective-permute-start(bf16[384,768]{1,0:T(8,128)(2,1)} %get-tuple-element.48), channel_id=1, source_target_pairs={{0,32},{1,33},{2,34},{3,35},{4,36},{5,37},{6,38},{7,39},{8,40},{9,... | collective-permute-start | bytes 1769480 | tf_op jit(solution)/shard_map/ppermute | solution.py:47
  131.0 15.7 %collective-permute-start.2 = (bf16[384,768]{1,0:T(8,128)(2,1)}, bf16[384,768]{1,0:T(8,128)(2,1)S(1)}, u32[]{:S(2)}, u32[]{:S(2)}) collective-permute-start(bf16[384,768]{1,0:T(8,128)(2,1)} %get-tuple-element.49), channel_id=1, source_target_pairs={{0,96},{1,97},{2,98},{3,99},{4,100},{5,101},{6,102},{7,103},{8,104... | collective-permute-start | bytes 1769480 | tf_op jit(solution)/shard_map/ppermute | solution.py:47
  146.6 0.8 copy-start.20
  146.6 1.0 copy-start.21
  147.6 4.7 %collective-permute-start.3 = (bf16[4,384,768]{2,1,0:T(8,128)(2,1)}, bf16[4,384,768]{2,1,0:T(8,128)(2,1)S(1)}, u32[]{:S(2)}, u32[]{:S(2)}) collective-permute-start(bf16[4,384,768]{2,1,0:T(8,128)(2,1)} %shard_map.131), channel_id=1, source_target_pairs={{0,16},{1,17},{2,18},{3,19},{4,20},{5,21},{6,22},{7,23},{8,24},{9,... | collective-permute-start | bytes 7077896 | tf_op jit(solution)/shard_map/ppermute | solution.py:47
  147.6 1.3 copy-start.26
  149.0 28.4 %collective-permute-start.7 = (bf16[384,768]{1,0:T(8,128)(2,1)S(1)}, bf16[384,768]{1,0:T(8,128)(2,1)S(1)}, u32[]{:S(2)}, u32[]{:S(2)}) collective-permute-start(bf16[384,768]{1,0:T(8,128)(2,1)S(1)} %copy-done.26), channel_id=1, source_target_pairs={{0,64},{1,65},{2,66},{3,67},{4,68},{5,69},{6,70},{7,71},{8,72},{9,... | collective-permute-start | bytes 1769480 | tf_op jit(solution)/shard_map/ppermute | solution.py:47
  152.4 1.5 copy-start.25
  158.9 18.4 %collective-permute-start.4 = (bf16[384,384]{1,0:T(8,128)(2,1)}, bf16[384,384]{1,0:T(8,128)(2,1)S(1)}, u32[]{:S(2)}, u32[]{:S(2)}) collective-permute-start(bf16[384,384]{1,0:T(8,128)(2,1)} %get-tuple-element.53), channel_id=1, source_target_pairs={{0,32},{1,33},{2,34},{3,35},{4,36},{5,37},{6,38},{7,39},{8,40},{9,... | collective-permute-start | bytes 884744 | tf_op jit(solution)/shard_map/ppermute | solution.py:47
  160.3 17.1 %collective-permute-start.5 = (bf16[384,384]{1,0:T(8,128)(2,1)}, bf16[384,384]{1,0:T(8,128)(2,1)S(1)}, u32[]{:S(2)}, u32[]{:S(2)}) collective-permute-start(bf16[384,384]{1,0:T(8,128)(2,1)} %get-tuple-element.54), channel_id=1, source_target_pairs={{0,96},{1,97},{2,98},{3,99},{4,100},{5,101},{6,102},{7,103},{8,104... | collective-permute-start | bytes 884744 | tf_op jit(solution)/shard_map/ppermute | solution.py:47
  162.1 16.8 %collective-permute-start.6 = (bf16[384,384]{1,0:T(8,128)(2,1)}, bf16[384,384]{1,0:T(8,128)(2,1)S(1)}, u32[]{:S(2)}, u32[]{:S(2)}) collective-permute-start(bf16[384,384]{1,0:T(8,128)(2,1)} %get-tuple-element.55), channel_id=1, source_target_pairs={{0,64},{1,65},{2,66},{3,67},{4,68},{5,69},{6,70},{7,71},{8,72},{9,... | collective-permute-start | bytes 884744 | tf_op jit(solution)/shard_map/ppermute | solution.py:47
  163.6 22.6 %all-to-all-start.5 = ((bf16[16,96,384]{2,1,0:T(8,128)(2,1)}), bf16[16,96,384]{2,1,0:T(8,128)(2,1)S(1)}, u32[]{:S(2)}, u32[]{:S(2)}) async-start(bf16[16,96,384]{2,1,0:T(8,128)(2,1)} %get-tuple-element.57), calls=%async_computation.5 | async-start | bytes 2359296 | tf_op jit(solution)/shard_map/all_to_all | solution.py:38
  177.3 1.6 copy-start.27
  177.3 1.6 copy-start.28
  177.3 1.5 copy-start.29
  178.9 0.7 copy-start.30
  186.3 18.2 %all-to-all-start.4 = ((bf16[16,24,1152]{2,1,0:T(8,128)(2,1)}), bf16[16,24,1152]{2,1,0:T(8,128)(2,1)S(1)}, u32[]{:S(2)}, u32[]{:S(2)}) async-start(bf16[16,24,1152]{2,1,0:T(8,128)(2,1)} %bitcast.18), calls=%async_computation.4 | async-start | bytes 1769472 | tf_op jit(solution)/shard_map/all_to_all | solution.py:38
  189.9 1.4 copy-start.8
  191.5 13.0 %collective-permute-start.8 = (f32[24,384]{1,0:T(8,128)S(1)}, f32[24,384]{1,0:T(8,128)S(1)}, u32[]{:S(2)}, u32[]{:S(2)}) collective-permute-start(f32[24,384]{1,0:T(8,128)S(1)} %get-tuple-element.59), channel_id=1, source_target_pairs={{0,32},{1,33},{2,34},{3,35},{4,36},{5,37},{6,38},{7,39},{8,40},{9,... | collective-permute-start | bytes 110600 | tf_op jit(solution)/shard_map/ppermute | solution.py:47
  192.6 11.9 %collective-permute-start.9 = (f32[24,384]{1,0:T(8,128)S(1)}, f32[24,384]{1,0:T(8,128)S(1)}, u32[]{:S(2)}, u32[]{:S(2)}) collective-permute-start(f32[24,384]{1,0:T(8,128)S(1)} %get-tuple-element.60), channel_id=1, source_target_pairs={{0,96},{1,97},{2,98},{3,99},{4,100},{5,101},{6,102},{7,103},{8,104... | collective-permute-start | bytes 110600 | tf_op jit(solution)/shard_map/ppermute | solution.py:47
  194.8 9.7 %collective-permute-start.10 = (f32[24,384]{1,0:T(8,128)S(1)}, f32[24,384]{1,0:T(8,128)S(1)}, u32[]{:S(2)}, u32[]{:S(2)}) collective-permute-start(f32[24,384]{1,0:T(8,128)S(1)} %get-tuple-element.61), channel_id=1, source_target_pairs={{0,64},{1,65},{2,66},{3,67},{4,68},{5,69},{6,70},{7,71},{8,72},{9,... | collective-permute-start | bytes 110600 | tf_op jit(solution)/shard_map/ppermute | solution.py:47

commit v4 on v3

--- a/solution.py
+++ b/solution.py
@@ -120,7 +120,7 @@
             jax.ShapeDtypeStruct((16, 16, 1536), jnp.bfloat16),
         ),
         scratch_shapes=[pltpu.VMEM((1024, 768), jnp.float32), pltpu.VMEM((16, 768), jnp.float32)],
-        compiler_params=limit(36),
+        compiler_params=limit(56),
         cost_estimate=cost(20),
     )(tokens, w_in, bias_in.reshape(1, -1), w_out, vectors)
 
@@ -154,7 +154,7 @@
         in_specs=[vmem] * 3,
         out_specs=vmem,
         out_shape=jax.ShapeDtypeStruct((16, 16, 512), jnp.bfloat16),
-        compiler_params=limit(16),
+        compiler_params=limit(56),
         cost_estimate=cost(1),
     )(owners, offsets, reader_weights)
 
@@ -167,6 +167,7 @@
 
     def source(s, carry):
         meta = table_ref[s].astype(jnp.float32)
+        counts = []
         for g in range(2):
             owner, high, spot, upper, lower = [meta[2 * f + g : 2 * f + g + 1] for f in range(5)]
             key = jnp.where(owner == me, high * 8.0 + turn, -1.0)
@@ -177,8 +178,10 @@
             ).astype(jnp.bfloat16)
             out = dot_rows(left, right)
             at = pl.ds(pl.multiple_of(s * 16 + g * 8, 8), 8)
-            count_ref[:, at, :] = out[:, :128].reshape(32, 8, 128)
+            counts.append(out[:, :128].reshape(32, 8, 128))
             share_ref[:, at, :] = (out[:, 128:256] + out[:, 256:]).reshape(32, 8, 128)
+        at = pl.ds(pl.multiple_of(s * 16, 16), 16)
+        count_ref[:, at, :] = jnp.concatenate(counts, axis=1).astype(jnp.bfloat16)
         return carry
 
     lax.fori_loop(0, 16, source, 0, unroll=2)
@@ -188,7 +191,10 @@
     vmem = pl.BlockSpec(memory_space=pltpu.VMEM)
     return pl.pallas_call(
         picks_kernel,
-        out_shape=(jax.ShapeDtypeStruct((32, 256, 128), jnp.float32),) * 2,
+        out_shape=(
+            jax.ShapeDtypeStruct((32, 256, 128), jnp.bfloat16),
+            jax.ShapeDtypeStruct((32, 256, 128), jnp.float32),
+        ),
         in_specs=[pl.BlockSpec(memory_space=pltpu.SMEM), vmem, anywhere],
         out_specs=(vmem, vmem),
         compiler_params=limit(24),
@@ -196,28 +202,22 @@
     )(me, asked, after)
 
 
-def score_kernel(ask_ref, count_ref, slab_hbm, weight_ref, stat_ref, scores, slab, sems):
-    loads = []
-    for block in range(8):
-        rows = pl.ds(block * 512, 512)
-        loads.append(pltpu.make_async_copy(slab_hbm.at[rows], slab.at[rows], sems.at[block]))
-        loads[-1].start()
+def score_kernel(ask_ref, count_ref, slab, weight_ref, stat_ref, scores):
     both = jnp.concatenate(
         [ask_ref[:, :, :768].reshape(256, 768), ask_ref[:, :, 768:].reshape(256, 768)], axis=0
     )
     top = jnp.full((256, 128), low, jnp.float32)
     for block in range(8):
-        loads[block].wait()
         got = dot_rows(both, slab[block * 512 : block * 512 + 512])
         got = got[:256] + got[256:]
         for i in range(4):
             part = got[:, i * 128 : i * 128 + 128]
             scores[block * 4 + i] = part
-            top = jnp.maximum(top, jnp.where(count_ref[block * 4 + i] > 0, part, low))
+            top = jnp.maximum(top, jnp.where(count_ref[block * 4 + i].astype(jnp.float32) > 0, part, low))
     top = jnp.max(top, axis=1, keepdims=True)
     mass = jnp.zeros((256, 128), jnp.float32)
     for high in range(32):
-        here = count_ref[high]
+        here = count_ref[high].astype(jnp.float32)
         part = jnp.where(here > 0, here * jnp.exp(jnp.minimum(scores[high] - top, 0.0)), 0.0)
         mass = mass + part
         weight_ref[high] = part
@@ -236,14 +236,10 @@
             jax.ShapeDtypeStruct((32, 256, 128), jnp.float32),
             jax.ShapeDtypeStruct((16, 8, 256), jnp.float32),
         ),
-        in_specs=[vmem, vmem, pl.BlockSpec(memory_space=pltpu.MemorySpace.HBM)],
+        in_specs=[vmem, vmem, vmem],
         out_specs=(vmem, vmem),
-        scratch_shapes=[
-            pltpu.VMEM((32, 256, 128), jnp.float32),
-            pltpu.VMEM((4096, 768), jnp.bfloat16),
-            pltpu.SemaphoreType.DMA((8,)),
-        ],
-        compiler_params=limit(28),
+        scratch_shapes=[pltpu.VMEM((32, 256, 128), jnp.float32)],
+        compiler_params=limit(24),
         cost_estimate=cost(8),
     )(asked, count, slab)
 
@@ -351,7 +347,7 @@
             out_specs=(pl.BlockSpec((1, 384, 768), lambda j, place: (j, 0, 0)),) * 2,
         ),
         out_shape=(jax.ShapeDtypeStruct((4, 384, 768), jnp.bfloat16),) * 2,
-        compiler_params=limit(56),
+        compiler_params=limit(24),
         cost_estimate=cost(40),
     )(place, left, right)
 
@@ -377,7 +373,7 @@
         + (jax.ShapeDtypeStruct((384, 768), jnp.bfloat16),) * 3
         + (jax.ShapeDtypeStruct(carry.shape, carry.dtype),),
         input_output_aliases={3: 4},
-        compiler_params=limit(56),
+        compiler_params=limit(16),
         cost_estimate=cost(5),
     )(place, kept, came, carry)
 
@@ -415,7 +411,7 @@
             jax.ShapeDtypeStruct(carry.shape, carry.dtype),
         ),
         input_output_aliases={3: 5},
-        compiler_params=limit(56),
+        compiler_params=limit(16),
         cost_estimate=cost(5),
     )(place, kept, came, carry, *after)
 
@@ -427,7 +423,7 @@
         out_specs=anywhere,
         out_shape=jax.ShapeDtypeStruct(carry.shape, carry.dtype),
         input_output_aliases={0: 0},
-        compiler_params=limit(56),
+        compiler_params=limit(4),
         cost_estimate=cost(1),
     )(carry, *after)
 
@@ -444,7 +440,7 @@
         in_specs=[tile],
         out_specs=tile,
         out_shape=jax.ShapeDtypeStruct((8, 128), jnp.float32),
-        compiler_params=limit(56),
+        compiler_params=limit(4),
         cost_estimate=cost(100),
     )(own)
 
@@ -466,7 +462,7 @@
         in_specs=[narrow] * 4 + [wide] * 4 + [anywhere],
         out_specs=pl.BlockSpec((96, 1152), lambda j: (j, 0)),
         out_shape=jax.ShapeDtypeStruct((384, 1152), jnp.bfloat16),
-        compiler_params=limit(56),
+        compiler_params=limit(16),
         cost_estimate=cost(2),
     )(*first, *second, after)
 
@@ -533,11 +529,11 @@
         return [own] + [shifted(piece, 0, step) for piece, step in zip(pieces, (1, 3, 2))]
 
     away, kept = weight_sums(place, hidden, out_grad)
+    *second, out_grad = second_pair(place, kept, shifted(away, 1, 0), out_grad)
+    second = round_y(*second)
     pre_grad = (
         jnp.dot(out_grad, w_out.T, preferred_element_type=jnp.float32) * slopes.astype(jnp.float32)
     ).astype(jnp.bfloat16)
-    *second, pre_grad = second_pair(place, kept, shifted(away, 1, 0), pre_grad)
-    second = round_y(*second)
     away, kept = weight_sums(place, pre_grad, tokens)
     away = hold(away, second[1], second[2])
     *first, packed, pre_grad = first_pair(

time: 207 us -> 191 us (0.923)
  Pallas kernels: 76.9 us -> 64.3 us
  local copies, waits for them, and re-layouts: 25.9 us -> 20.1 us
  waiting for transfers between devices: 30.1 us -> 33.9 us
    pallas_call x2, Pallas kernels: 20.8 us -> 14.4 us  [weight_sums(): pl.pallas_call(weight_kernel, grid_spec=pltpu.PrefetchScalarGridSpec(num_...]
    unnamed x66 -> x42, local copies, waits for them, and re-layouts: 25.9 us -> 20.1 us
    pallas_call x1, Pallas kernels: 5.14 us -> 1.49 us  [second_pair(): pl.pallas_call(second_kernel, grid_spec=pltpu.PrefetchScalarGridSpec(num_...]
    ppermute x11, waiting for transfers between devices: 6 us -> 9.24 us  [shifted(): return lax.ppermute(value, every, pairs)]
    pallas_call x1, Pallas kernels: 19.3 us -> 22.1 us  [forward(): pl.pallas_call(forward_kernel, grid=(3072 // block,), in_specs=[whole(102...]
    pallas_call x1, Pallas kernels: 5.06 us -> 2.71 us  [first_pair(): pl.pallas_call(first_kernel, grid_spec=pltpu.PrefetchScalarGridSpec(num_s...]
  transfers between devices with their start and end apart: 16 -> 16, of which waited for: 7 -> 7; matrix products, arithmetic and copies ran while one was open for 9% -> 10% of each run, Pallas kernels for 22% -> 22%
where the time goes in v4:
time: 191 us; the launch traced here: 190 us
  Pallas kernels  64.3 us (34%)
  starting transfers between devices  40.6 us (21%)
  waiting for transfers between devices  33.9 us (18%)
  local copies, waits for them, and re-layouts  20.1 us (11%)
  matrix products  17.9 us (9%)
  blocking collectives  11.1 us (6%)
    all_to_all x5, starting transfers between devices, exchange(): return lax.all_to_all(value, 'index', 0, 0, tiled=True)  26.1 us
    all_to_all x5, waiting for transfers between devices, exchange(): return lax.all_to_all(value, 'index', 0, 0, tiled=True)  24.7 us
    pallas_call x1, Pallas kernels, forward(): pl.pallas_call(forward_kernel, grid=(3072 // block,), in_specs=[whole(102...  22.1 us
    unnamed x42, local copies, waits for them, and re-layouts  20.1 us
    ppermute x11, starting transfers between devices, shifted(): return lax.ppermute(value, every, pairs)  14.6 us
    pallas_call x2, Pallas kernels, weight_sums(): pl.pallas_call(weight_kernel, grid_spec=pltpu.PrefetchScalarGridSpec(num_...  14.4 us
    all_to_all x1, blocking collectives, exchange(): return lax.all_to_all(value, 'index', 0, 0, tiled=True)  11.1 us
    ppermute x11, waiting for transfers between devices, shifted(): return lax.ppermute(value, every, pairs)  9.24 us
  transfers between devices with their start and end apart: 16, of which 7 were waited for; matrix products, arithmetic and copies ran while one was open for 10% of the time, Pallas kernels for 22%

profile of v4, /device:TPU:0, one launch (start us, length us, event | category | flops | bytes accessed | tf_op | source)
XLA Modules:
  0.0 189.8 jit_solution(8712587186597962466)
XLA Ops:
  0.7 1.6 shard_map.123
  2.3 8.0 %all-to-all-start.1 = ((bf16[16,16,512]{2,1,0:T(8,128)(2,1)}), bf16[16,16,512]{2,1,0:T(8,128)(2,1)S(1)}, u32[]{:S(2)}, u32[]{:S(2)}) async-start(bf16[16,16,512]{2,1,0:T(8,128)(2,1)} %shard_map.123), calls=%async_computation.1 | async-start | bytes 524288 | tf_op jit(solution)/shard_map/all_to_all | solution.py:38
  10.3 0.6 pad_maximum_fusion
  10.9 22.1 %shard_map.122 = (bf16[1024,3072]{1,0:T(8,128)(2,1)}, bf16[1024,3072]{1,0:T(8,128)(2,1)}, f32[1024,768]{1,0:T(8,128)}, f32[1024,1]{1,0:T(8,128)}, bf16[16,16,1536]{2,1,0:T(8,128)(2,1)}) custom-call(bf16[1024,768]{1,0:T(8,128)(2,1)} %right_ref.1, bf16[768,3072]{1,0:T(8,128)(2,1)} %w_in_ref.1, f32[1,3072]{1,0:T(1,128)} %bitcast.14, ...), custom_call_target="tpu_custom_call" | custom-call | flops 20000000000 | bytes 1000 | tf_op jit(solution)/shard_map/pallas_call | solution.py:104
  33.0 0.0 all-to-all-done.1.table_ref
  33.0 7.2 %all-to-all-start = ((bf16[16,16,1536]{2,1,0:T(8,128)(2,1)}), bf16[16,16,1536]{2,1,0:T(8,128)(2,1)S(1)}, u32[]{:S(2)}, u32[]{:S(2)}) async-start(bf16[16,16,1536]{2,1,0:T(8,128)(2,1)} %get-tuple-element.32), calls=%async_computation | async-start | bytes 1572864 | tf_op jit(solution)/shard_map/all_to_all | solution.py:38
  40.3 1.0 copy-done.15
  41.3 5.9 %shard_map.124 = (bf16[32,256,128]{2,1,0:T(8,128)(2,1)S(1)}, f32[32,256,128]{2,1,0:T(8,128)S(1)}) custom-call(s32[1]{0:T(128)} %bitcast.me_ref, bf16[16,16,512]{2,1,0:T(8,128)(2,1)S(1)} %all-to-all-done.1.table_ref, f32[1024,1]{1,0:T(8,128)S(1)} %copy-done.15), custom_call_target="tpu_custom_call" | custom-call | flops 10000000000 | bytes 1000 | tf_op jit(solution)/shard_map/pallas_call | solution.py:192
  47.2 1.9 %copy-done.10 = f32[32,256,128]{2,1,0:T(8,128)} copy-done((f32[32,256,128]{2,1,0:T(8,128)}, f32[32,256,128]{2,1,0:T(8,128)S(1)}, u32[]{:S(2)}) %copy-start.10) | copy-done | bytes 4194328
  49.1 4.9 %all-to-all-done.ask_ref = bf16[16,16,1536]{2,1,0:T(8,128)(2,1)S(1)} async-done(((bf16[16,16,1536]{2,1,0:T(8,128)(2,1)}), bf16[16,16,1536]{2,1,0:T(8,128)(2,1)S(1)}, u32[]{:S(2)}, u32[]{:S(2)}) %all-to-all-start) | async-done | bytes 786464 | tf_op jit(solution)/shard_map/all_to_all | solution.py:38
  54.0 2.8 %copy-done.1 = bf16[4096,768]{1,0:T(8,128)(2,1)S(1)} copy-done((bf16[4096,768]{1,0:T(8,128)(2,1)S(1)}, bf16[4096,768]{1,0:T(8,128)(2,1)}, u32[]{:S(2)}) %copy-start.1) | copy-done | bytes 6291480
  56.8 4.8 %shard_map.125 = (f32[32,256,128]{2,1,0:T(8,128)S(1)}, f32[16,8,256]{2,1,0:T(8,128)S(1)}) custom-call(bf16[16,16,1536]{2,1,0:T(8,128)(2,1)S(1)} %all-to-all-done.ask_ref, bf16[32,256,128]{2,1,0:T(8,128)(2,1)S(1)} %get-tuple-element.34.count_ref, bf16[4096,768]{1,0:T(8,128)(2,1)S(1)} %copy-done.1), custom_call_target="tpu_custom_call" | custom-call | flops 8000000000 | bytes 1000 | tf_op jit(solution)/shard_map/pallas_call | solution.py:233
  61.6 11.1 %all_to_all.30.stat_ref = f32[16,8,256]{2,1,0:T(8,128)S(1)} all-to-all(f32[16,8,256]{2,1,0:T(8,128)S(1)} %get-tuple-element.35), channel_id=1, replica_groups=mesh['query'=8,'index'=16] {'index'}, dimensions={0} | all-to-all | bytes 262144 | tf_op jit(solution)/shard_map/all_to_all | solution.py:38
  72.7 2.8 %copy-done.2 = bf16[4096,768]{1,0:T(8,128)(2,1)S(1)} copy-done((bf16[4096,768]{1,0:T(8,128)(2,1)S(1)}, bf16[4096,768]{1,0:T(8,128)(2,1)}, u32[]{:S(2)}) %copy-start.2) | copy-done | bytes 6291480
  75.5 5.7 %shard_map.126 = bf16[256,768]{1,0:T(8,128)(2,1)} custom-call(s32[1]{0:T(128)} %bitcast.me_ref, f32[16,8,256]{2,1,0:T(8,128)S(1)} %all_to_all.30.stat_ref, f32[32,256,128]{2,1,0:T(8,128)S(1)} %get-tuple-element.36.weight_ref, f32[32,256,128]{2,1,0:T(8,128)S(1)} %copy-done.11, bf16[4096,768]{1,0:T(8,128)(2,1)S(1)} %copy-done.2), custom_call_target="tpu_custom_call" | custom-call | flops 5000000000 | bytes 1000 | tf_op jit(solution)/shard_map/pallas_call | solution.py:275
  81.2 3.6 %all-to-all-start.3 = ((bf16[16,16,768]{2,1,0:T(8,128)(2,1)}), bf16[16,16,768]{2,1,0:T(8,128)(2,1)S(1)}, u32[]{:S(2)}, u32[]{:S(2)}) async-start(bf16[16,16,768]{2,1,0:T(8,128)(2,1)} %bitcast.4), calls=%async_computation.3 | async-start | bytes 786432 | tf_op jit(solution)/shard_map/all_to_all | solution.py:38
  84.8 0.1 pad_add_fusion.place_ref
  84.9 9.3 %all-to-all-done.3.came_ref = bf16[16,16,768]{2,1,0:T(8,128)(2,1)S(1)} async-done(((bf16[16,16,768]{2,1,0:T(8,128)(2,1)}), bf16[16,16,768]{2,1,0:T(8,128)(2,1)S(1)}, u32[]{:S(2)}, u32[]{:S(2)}) %all-to-all-start.3) | async-done | bytes 393248 | tf_op jit(solution)/shard_map/all_to_all | solution.py:38
  94.2 1.0 copy-done.16
  95.2 1.0 shard_map.127
  96.3 1.6 copy-done.13
  97.9 2.8 %copy-done.17 = bf16[1024,3072]{1,0:T(8,128)(2,1)S(1)} copy-done((bf16[1024,3072]{1,0:T(8,128)(2,1)S(1)}, bf16[1024,3072]{1,0:T(8,128)(2,1)}, u32[]{:S(2)}) %copy-start.17) | copy-done | bytes 6291480
  100.7 7.2 %shard_map.128 = (bf16[4,384,768]{2,1,0:T(8,128)(2,1)S(1)}, bf16[4,384,768]{2,1,0:T(8,128)(2,1)S(1)}) custom-call(s32[2]{0:T(128)S(1)} %pad_add_fusion.place_ref, bf16[1024,3072]{1,0:T(8,128)(2,1)S(1)} %copy-done.17, bf16[1024,768]{1,0:T(8,128)(2,1)S(1)} %get-tuple-element.41.right_ref.carry_ref), custom_call_target="tpu_custom_call" | custom-call | flops 40000000000 | bytes 1000 | tf_op jit(solution)/shard_map/pallas_call | solution.py:341
  107.9 0.1 collective-permute-start
  108.0 4.5 %collective-permute-done.came_ref = bf16[4,384,768]{2,1,0:T(8,128)(2,1)S(1)} collective-permute-done((bf16[4,384,768]{2,1,0:T(8,128)(2,1)S(1)}, bf16[4,384,768]{2,1,0:T(8,128)(2,1)S(1)}, u32[]{:S(2)}, u32[]{:S(2)}) %collective-permute-start) | collective-permute-done | bytes 2359328 | tf_op jit(solution)/shard_map/ppermute | solution.py:47
  112.5 1.5 shard_map.129
  114.0 0.0 copy-start.6
  114.0 1.8 collective-permute-start.1
  115.9 1.7 collective-permute-start.2
  117.5 8.7 %multiply_convert_fusion.left_ref.refs_0_ = bf16[1024,3072]{1,0:T(8,128)(2,1)S(1)} fusion(bf16[1024,3072]{1,0:T(8,128)(2,1)} %get-tuple-element.45, bf16[1024,768]{1,0:T(8,128)(2,1)S(1)} %get-tuple-element.44, bf16[3072,768]{1,0:T(8,128)(2,1)} %w_out_ref.1), kind=kOutput, calls=%fused_computation | convolution fusion | flops 4841275392 | bytes 18874368 | tf_op jit(solution)/shard_map/dot_general | solution.py:535
  126.3 7.2 %shard_map.130 = (bf16[4,384,768]{2,1,0:T(8,128)(2,1)S(1)}, bf16[4,384,768]{2,1,0:T(8,128)(2,1)S(1)}) custom-call(s32[2]{0:T(128)S(1)} %pad_add_fusion.place_ref, bf16[1024,3072]{1,0:T(8,128)(2,1)S(1)} %multiply_convert_fusion.left_ref.refs_0_, bf16[1024,768]{1,0:T(8,128)(2,1)S(1)} %copy-done.3), custom_call_target="tpu_custom_call" | custom-call | flops 40000000000 | bytes 1000 | tf_op jit(solution)/shard_map/pallas_call | solution.py:341
  133.5 0.0 collective-permute-done.1.refs_1_.refs_5_
  133.5 0.0 collective-permute-done.2.refs_2_.refs_6_
  133.5 0.1 collective-permute-start.3
  133.6 2.1 %collective-permute-start.7 = (bf16[384,768]{1,0:T(8,128)(2,1)S(1)}, bf16[384,768]{1,0:T(8,128)(2,1)S(1)}, u32[]{:S(2)}, u32[]{:S(2)}) collective-permute-start(bf16[384,768]{1,0:T(8,128)(2,1)S(1)} %get-tuple-element.56), channel_id=1, source_target_pairs={{0,64},{1,65},{2,66},{3,67},{4,68},{5,69},{6,70},{7,71},{8,72},{9,... | collective-permute-start | bytes 1769480 | tf_op jit(solution)/shard_map/ppermute | solution.py:47
  135.7 2.4 %collective-permute-done.3.came_ref = bf16[4,384,768]{2,1,0:T(8,128)(2,1)S(1)} collective-permute-done((bf16[4,384,768]{2,1,0:T(8,128)(2,1)S(1)}, bf16[4,384,768]{2,1,0:T(8,128)(2,1)S(1)}, u32[]{:S(2)}, u32[]{:S(2)}) %collective-permute-start.3) | collective-permute-done | bytes 2359328 | tf_op jit(solution)/shard_map/ppermute | solution.py:47
  138.1 2.7 %shard_map.133 = (f32[384,384]{1,0:T(8,128)S(1)}, bf16[384,384]{1,0:T(8,128)(2,1)}, bf16[384,384]{1,0:T(8,128)(2,1)}, bf16[384,384]{1,0:T(8,128)(2,1)}, bf16[16,...) custom-call(s32[2]{0:T(128)S(1)} %pad_add_fusion.place_ref, ...), custom_call_target="tpu_custom_call", output_to_operand_aliasing={{5}: (3, {})} | custom-call | flops 5000000000 | bytes 1000 | tf_op jit(solution)/shard_map/pallas_call | solution.py:398
  140.8 0.9 copy-done.8
  141.7 2.7 %copy-done.14 = bf16[1024,3072]{1,0:T(8,128)(2,1)} copy-done((bf16[1024,3072]{1,0:T(8,128)(2,1)}, bf16[1024,3072]{1,0:T(8,128)(2,1)S(1)}, u32[]{:S(2)}) %copy-start.14) | copy-done | bytes 6291480
  144.4 0.4 collective-permute-start.4
  144.8 2.9 %collective-permute-start.5 = (bf16[384,384]{1,0:T(8,128)(2,1)}, bf16[384,384]{1,0:T(8,128)(2,1)}, u32[]{:S(2)}, u32[]{:S(2)}) collective-permute-start(bf16[384,384]{1,0:T(8,128)(2,1)} %get-tuple-element.54), channel_id=1, source_target_pairs={{0,96},{1,97},{2,98},{3,99},{4,100},{5,101},{6,102},{7,103},{8,104... | collective-permute-start | bytes 884744 | tf_op jit(solution)/shard_map/ppermute | solution.py:47
  147.7 0.8 collective-permute-start.6
  148.4 3.7 %all-to-all-start.5 = ((bf16[16,96,384]{2,1,0:T(8,128)(2,1)}), bf16[16,96,384]{2,1,0:T(8,128)(2,1)S(1)}, u32[]{:S(2)}, u32[]{:S(2)}) async-start(bf16[16,96,384]{2,1,0:T(8,128)(2,1)} %get-tuple-element.57), calls=%async_computation.5 | async-start | bytes 2359296 | tf_op jit(solution)/shard_map/all_to_all | solution.py:38
  152.1 0.0 copy-start.7
  152.2 9.2 %add_convert_fusion.refs_8_.after_ref = bf16[1024,768]{1,0:T(8,128)(2,1)S(1)} fusion(f32[1024,768]{1,0:T(8,128)} %copy-done.13, bf16[1024,3072]{1,0:T(8,128)(2,1)} %copy-done.14, bf16[768,3072]{1,0:T(8,128)(2,1)} %w_in_ref.1), kind=kOutput, calls=%fused_computation.1 | convolution fusion | flops 4833411072 | bytes 15728640 | tf_op jit(solution)/shard_map/dot_general | solution.py:545
  161.4 0.0 collective-permute-done.7.refs_7_
  161.4 0.0 collective-permute-done.4.refs_1_
  161.4 0.0 collective-permute-done.5.refs_2_
  161.4 2.3 %collective-permute-done.6.refs_3_ = bf16[384,384]{1,0:T(8,128)(2,1)} collective-permute-done((bf16[384,384]{1,0:T(8,128)(2,1)}, bf16[384,384]{1,0:T(8,128)(2,1)}, u32[]{:S(2)}, u32[]{:S(2)}) %collective-permute-start.6) | collective-permute-done | bytes 294944 | tf_op jit(solution)/shard_map/ppermute | solution.py:47
  163.7 3.5 %shard_map.134 = bf16[384,1152]{1,0:T(8,128)(2,1)} custom-call(f32[384,384]{1,0:T(8,128)S(1)} %copy-done.9, bf16[384,384]{1,0:T(8,128)(2,1)} %collective-permute-done.4.refs_1_, bf16[384,384]{1,0:T(8,128)(2,1)} %collective-permute-done.5.refs_2_, bf16[384,384]{1,0:T(8,128)(2,1)} %collective-permute-done.6.refs_3_, f32[384,768]{1,0:T(8,128)S(1)} %copy-done.7, ...), custom_call_target="tpu_custom_call" | custom-call | flops 2000000000 | bytes 1000 | tf_op jit(solution)/shard_map/pallas_call | solution.py:459
  167.2 1.1 copy-done.4
  168.4 2.7 %all-to-all-done.5.came_ref = bf16[16,96,384]{2,1,0:T(8,128)(2,1)S(1)} async-done(((bf16[16,96,384]{2,1,0:T(8,128)(2,1)}), bf16[16,96,384]{2,1,0:T(8,128)(2,1)S(1)}, u32[]{:S(2)}, u32[]{:S(2)}) %all-to-all-start.5) | async-done | bytes 1179680 | tf_op jit(solution)/shard_map/all_to_all | solution.py:38
  171.1 3.6 %all-to-all-start.4 = ((bf16[16,24,1152]{2,1,0:T(8,128)(2,1)}), bf16[16,24,1152]{2,1,0:T(8,128)(2,1)S(1)}, u32[]{:S(2)}, u32[]{:S(2)}) async-start(bf16[16,24,1152]{2,1,0:T(8,128)(2,1)} %bitcast.7), calls=%async_computation.4 | async-start | bytes 1769472 | tf_op jit(solution)/shard_map/all_to_all | solution.py:38
  174.7 0.0 copy-start.5
  174.7 1.4 copy-done.5
  176.1 0.2 shard_map.135
  176.3 0.7 collective-permute-start.8
  177.1 2.6 %collective-permute-start.9 = (f32[24,384]{1,0:T(8,128)S(1)}, f32[24,384]{1,0:T(8,128)S(1)}, u32[]{:S(2)}, u32[]{:S(2)}) collective-permute-start(f32[24,384]{1,0:T(8,128)S(1)} %get-tuple-element.60), channel_id=1, source_target_pairs={{0,96},{1,97},{2,98},{3,99},{4,100},{5,101},{6,102},{7,103},{8,104... | collective-permute-start | bytes 110600 | tf_op jit(solution)/shard_map/ppermute | solution.py:47
  179.6 1.5 collective-permute-start.10
  181.2 7.8 %all-to-all-done.4.refs_0_ = bf16[16,24,1152]{2,1,0:T(8,128)(2,1)S(1)} async-done(((bf16[16,24,1152]{2,1,0:T(8,128)(2,1)}), bf16[16,24,1152]{2,1,0:T(8,128)(2,1)S(1)}, u32[]{:S(2)}, u32[]{:S(2)}) %all-to-all-start.4) | async-done | bytes 884768 | tf_op jit(solution)/shard_map/all_to_all | solution.py:38
  188.9 0.0 collective-permute-done.8.refs_2_
  189.0 0.0 collective-permute-done.9.refs_3_
  189.0 0.0 collective-permute-done.10.refs_4_
  189.0 0.8 shard_map.136
  (31 shorter events, 0.1 us)
Async XLA Ops:
  0.6 9.7 %copy-start.18 = (f32[768]{0:T(1024)S(1)}, f32[768]{0:T(1024)}, u32[]{:S(2)}) copy-start(f32[768]{0:T(1024)} %param.17) | copy-start | bytes 9220
  0.6 9.7 %copy-start.19 = (f32[768]{0:T(1024)S(1)}, f32[768]{0:T(1024)}, u32[]{:S(2)}) copy-start(f32[768]{0:T(1024)} %param.16) | copy-start | bytes 9220
  0.7 9.7 %copy-start.20 = (f32[768]{0:T(1024)S(1)}, f32[768]{0:T(1024)}, u32[]{:S(2)}) copy-start(f32[768]{0:T(1024)} %param.15) | copy-start | bytes 9220
  2.3 30.7 %all-to-all-start.1 = ((bf16[16,16,512]{2,1,0:T(8,128)(2,1)}), bf16[16,16,512]{2,1,0:T(8,128)(2,1)S(1)}, u32[]{:S(2)}, u32[]{:S(2)}) async-start(bf16[16,16,512]{2,1,0:T(8,128)(2,1)} %shard_map.123), calls=%async_computation.1 | async-start | bytes 524288 | tf_op jit(solution)/shard_map/all_to_all | solution.py:38
  33.0 21.0 %all-to-all-start = ((bf16[16,16,1536]{2,1,0:T(8,128)(2,1)}), bf16[16,16,1536]{2,1,0:T(8,128)(2,1)S(1)}, u32[]{:S(2)}, u32[]{:S(2)}) async-start(bf16[16,16,1536]{2,1,0:T(8,128)(2,1)} %get-tuple-element.32), calls=%async_computation | async-start | bytes 1572864 | tf_op jit(solution)/shard_map/all_to_all | solution.py:38
  40.2 1.0 copy-start.15
  47.2 1.9 %copy-start.10 = (f32[32,256,128]{2,1,0:T(8,128)}, f32[32,256,128]{2,1,0:T(8,128)S(1)}, u32[]{:S(2)}) copy-start(f32[32,256,128]{2,1,0:T(8,128)S(1)} %get-tuple-element.37.share_ref) | copy-start | bytes 12582916
  54.0 2.8 %copy-start.1 = (bf16[4096,768]{1,0:T(8,128)(2,1)S(1)}, bf16[4096,768]{1,0:T(8,128)(2,1)}, u32[]{:S(2)}) copy-start(bf16[4096,768]{1,0:T(8,128)(2,1)} %slab_ref.1) | copy-start | bytes 18874372
  56.8 15.9 %copy-start.11 = (f32[32,256,128]{2,1,0:T(8,128)S(1)}, f32[32,256,128]{2,1,0:T(8,128)}, u32[]{:S(2)}) copy-start(f32[32,256,128]{2,1,0:T(8,128)} %copy-done.10) | copy-start | bytes 12582916
  72.7 2.8 %copy-start.2 = (bf16[4096,768]{1,0:T(8,128)(2,1)S(1)}, bf16[4096,768]{1,0:T(8,128)(2,1)}, u32[]{:S(2)}) copy-start(bf16[4096,768]{1,0:T(8,128)(2,1)} %slab_ref.1) | copy-start | bytes 18874372
  75.5 18.7 %copy-start = (f32[3072]{0:T(1024)S(1)}, f32[3072]{0:T(1024)}, u32[]{:S(2)}) copy-start(f32[3072]{0:T(1024)} %pad_maximum_fusion) | copy-start | bytes 36868
  75.5 18.7 %copy-start.12 = (f32[1024,768]{1,0:T(8,128)S(1)}, f32[1024,768]{1,0:T(8,128)}, u32[]{:S(2)}) copy-start(f32[1024,768]{1,0:T(8,128)} %get-tuple-element.38.normed_ref) | copy-start | bytes 9437188
  81.2 12.9 %all-to-all-start.3 = ((bf16[16,16,768]{2,1,0:T(8,128)(2,1)}), bf16[16,16,768]{2,1,0:T(8,128)(2,1)S(1)}, u32[]{:S(2)}, u32[]{:S(2)}) async-start(bf16[16,16,768]{2,1,0:T(8,128)(2,1)} %bitcast.4), calls=%async_computation.3 | async-start | bytes 786432 | tf_op jit(solution)/shard_map/all_to_all | solution.py:38
  94.2 1.0 copy-start.16
  96.3 1.6 copy-start.13
  97.9 2.8 %copy-start.17 = (bf16[1024,3072]{1,0:T(8,128)(2,1)S(1)}, bf16[1024,3072]{1,0:T(8,128)(2,1)}, u32[]{:S(2)}) copy-start(bf16[1024,3072]{1,0:T(8,128)(2,1)} %get-tuple-element.40.left_ref) | copy-start | bytes 18874372
  107.9 4.6 %collective-permute-start = (bf16[4,384,768]{2,1,0:T(8,128)(2,1)S(1)}, bf16[4,384,768]{2,1,0:T(8,128)(2,1)S(1)}, u32[]{:S(2)}, u32[]{:S(2)}) collective-permute-start(bf16[4,384,768]{2,1,0:T(8,128)(2,1)S(1)} %get-tuple-element.43), channel_id=1, source_target_pairs={{0,16},{1,17},{2,18},{3,19},{4,20},{5,21},{6,22},{7,23},{8,24},{9,... | collective-permute-start | bytes 7077896 | tf_op jit(solution)/shard_map/ppermute | solution.py:47
  114.0 19.6 %copy-start.6 = (f32[384,768]{1,0:T(8,128)}, f32[384,768]{1,0:T(8,128)S(1)}, u32[]{:S(2)}) copy-start(f32[384,768]{1,0:T(8,128)S(1)} %get-tuple-element.50.own_ref.refs_4_) | copy-start | bytes 3538948
  114.0 19.5 %collective-permute-start.1 = (bf16[384,768]{1,0:T(8,128)(2,1)S(1)}, bf16[384,768]{1,0:T(8,128)(2,1)S(1)}, u32[]{:S(2)}, u32[]{:S(2)}) collective-permute-start(bf16[384,768]{1,0:T(8,128)(2,1)S(1)} %get-tuple-element.48), channel_id=1, source_target_pairs={{0,32},{1,33},{2,34},{3,35},{4,36},{5,37},{6,38},{7,39},{8,40},{9,... | collective-permute-start | bytes 1769480 | tf_op jit(solution)/shard_map/ppermute | solution.py:47
  115.9 17.6 %collective-permute-start.2 = (bf16[384,768]{1,0:T(8,128)(2,1)S(1)}, bf16[384,768]{1,0:T(8,128)(2,1)S(1)}, u32[]{:S(2)}, u32[]{:S(2)}) collective-permute-start(bf16[384,768]{1,0:T(8,128)(2,1)S(1)} %get-tuple-element.49), channel_id=1, source_target_pairs={{0,96},{1,97},{2,98},{3,99},{4,100},{5,101},{6,102},{7,103},{8,104... | collective-permute-start | bytes 1769480 | tf_op jit(solution)/shard_map/ppermute | solution.py:47
  117.5 8.7 %copy-start.3 = (bf16[1024,768]{1,0:T(8,128)(2,1)S(1)}, bf16[1024,768]{1,0:T(8,128)(2,1)}, u32[]{:S(2)}) copy-start(bf16[1024,768]{1,0:T(8,128)(2,1)} %right_ref.1) | copy-start | bytes 4718596
  133.5 4.6 %collective-permute-start.3 = (bf16[4,384,768]{2,1,0:T(8,128)(2,1)S(1)}, bf16[4,384,768]{2,1,0:T(8,128)(2,1)S(1)}, u32[]{:S(2)}, u32[]{:S(2)}) collective-permute-start(bf16[4,384,768]{2,1,0:T(8,128)(2,1)S(1)} %shard_map.131), channel_id=1, source_target_pairs={{0,16},{1,17},{2,18},{3,19},{4,20},{5,21},{6,22},{7,23},{8,24},{9,... | collective-permute-start | bytes 7077896 | tf_op jit(solution)/shard_map/ppermute | solution.py:47
  133.6 27.7 %collective-permute-start.7 = (bf16[384,768]{1,0:T(8,128)(2,1)S(1)}, bf16[384,768]{1,0:T(8,128)(2,1)S(1)}, u32[]{:S(2)}, u32[]{:S(2)}) collective-permute-start(bf16[384,768]{1,0:T(8,128)(2,1)S(1)} %get-tuple-element.56), channel_id=1, source_target_pairs={{0,64},{1,65},{2,66},{3,67},{4,68},{5,69},{6,70},{7,71},{8,72},{9,... | collective-permute-start | bytes 1769480 | tf_op jit(solution)/shard_map/ppermute | solution.py:47
  140.8 0.9 copy-start.8
  141.7 2.7 %copy-start.14 = (bf16[1024,3072]{1,0:T(8,128)(2,1)}, bf16[1024,3072]{1,0:T(8,128)(2,1)S(1)}, u32[]{:S(2)}) copy-start(bf16[1024,3072]{1,0:T(8,128)(2,1)S(1)} %get-tuple-element.51) | copy-start | bytes 18874372
  144.4 17.0 %collective-permute-start.4 = (bf16[384,384]{1,0:T(8,128)(2,1)}, bf16[384,384]{1,0:T(8,128)(2,1)}, u32[]{:S(2)}, u32[]{:S(2)}) collective-permute-start(bf16[384,384]{1,0:T(8,128)(2,1)} %get-tuple-element.53), channel_id=1, source_target_pairs={{0,32},{1,33},{2,34},{3,35},{4,36},{5,37},{6,38},{7,39},{8,40},{9,... | collective-permute-start | bytes 884744 | tf_op jit(solution)/shard_map/ppermute | solution.py:47
  144.8 16.6 %collective-permute-start.5 = (bf16[384,384]{1,0:T(8,128)(2,1)}, bf16[384,384]{1,0:T(8,128)(2,1)}, u32[]{:S(2)}, u32[]{:S(2)}) collective-permute-start(bf16[384,384]{1,0:T(8,128)(2,1)} %get-tuple-element.54), channel_id=1, source_target_pairs={{0,96},{1,97},{2,98},{3,99},{4,100},{5,101},{6,102},{7,103},{8,104... | collective-permute-start | bytes 884744 | tf_op jit(solution)/shard_map/ppermute | solution.py:47
  147.7 16.0 %collective-permute-start.6 = (bf16[384,384]{1,0:T(8,128)(2,1)}, bf16[384,384]{1,0:T(8,128)(2,1)}, u32[]{:S(2)}, u32[]{:S(2)}) collective-permute-start(bf16[384,384]{1,0:T(8,128)(2,1)} %get-tuple-element.55), channel_id=1, source_target_pairs={{0,64},{1,65},{2,66},{3,67},{4,68},{5,69},{6,70},{7,71},{8,72},{9,... | collective-permute-start | bytes 884744 | tf_op jit(solution)/shard_map/ppermute | solution.py:47
  148.4 22.6 %all-to-all-start.5 = ((bf16[16,96,384]{2,1,0:T(8,128)(2,1)}), bf16[16,96,384]{2,1,0:T(8,128)(2,1)S(1)}, u32[]{:S(2)}, u32[]{:S(2)}) async-start(bf16[16,96,384]{2,1,0:T(8,128)(2,1)} %get-tuple-element.57), calls=%async_computation.5 | async-start | bytes 2359296 | tf_op jit(solution)/shard_map/all_to_all | solution.py:38
  152.1 11.5 %copy-start.7 = (f32[384,768]{1,0:T(8,128)S(1)}, f32[384,768]{1,0:T(8,128)}, u32[]{:S(2)}) copy-start(f32[384,768]{1,0:T(8,128)} %copy-done.6) | copy-start | bytes 3538948
  152.1 11.5 %copy-start.9 = (f32[384,384]{1,0:T(8,128)S(1)}, f32[384,384]{1,0:T(8,128)}, u32[]{:S(2)}) copy-start(f32[384,384]{1,0:T(8,128)} %copy-done.8) | copy-start | bytes 1769476
  167.2 1.1 copy-start.4
  171.1 17.9 %all-to-all-start.4 = ((bf16[16,24,1152]{2,1,0:T(8,128)(2,1)}), bf16[16,24,1152]{2,1,0:T(8,128)(2,1)S(1)}, u32[]{:S(2)}, u32[]{:S(2)}) async-start(bf16[16,24,1152]{2,1,0:T(8,128)(2,1)} %bitcast.7), calls=%async_computation.4 | async-start | bytes 1769472 | tf_op jit(solution)/shard_map/all_to_all | solution.py:38
  174.7 1.4 copy-start.5
  176.3 12.6 %collective-permute-start.8 = (f32[24,384]{1,0:T(8,128)S(1)}, f32[24,384]{1,0:T(8,128)S(1)}, u32[]{:S(2)}, u32[]{:S(2)}) collective-permute-start(f32[24,384]{1,0:T(8,128)S(1)} %get-tuple-element.59), channel_id=1, source_target_pairs={{0,32},{1,33},{2,34},{3,35},{4,36},{5,37},{6,38},{7,39},{8,40},{9,... | collective-permute-start | bytes 110600 | tf_op jit(solution)/shard_map/ppermute | solution.py:47
  177.1 11.9 %collective-permute-start.9 = (f32[24,384]{1,0:T(8,128)S(1)}, f32[24,384]{1,0:T(8,128)S(1)}, u32[]{:S(2)}, u32[]{:S(2)}) collective-permute-start(f32[24,384]{1,0:T(8,128)S(1)} %get-tuple-element.60), channel_id=1, source_target_pairs={{0,96},{1,97},{2,98},{3,99},{4,100},{5,101},{6,102},{7,103},{8,104... | collective-permute-start | bytes 110600 | tf_op jit(solution)/shard_map/ppermute | solution.py:47
  179.6 9.3 %collective-permute-start.10 = (f32[24,384]{1,0:T(8,128)S(1)}, f32[24,384]{1,0:T(8,128)S(1)}, u32[]{:S(2)}, u32[]{:S(2)}) collective-permute-start(f32[24,384]{1,0:T(8,128)S(1)} %get-tuple-element.61), channel_id=1, source_target_pairs={{0,64},{1,65},{2,66},{3,67},{4,68},{5,69},{6,70},{7,71},{8,72},{9,... | collective-permute-start | bytes 110600 | tf_op jit(solution)/shard_map/ppermute | solution.py:47

commit v5 on v4

--- a/solution.py
+++ b/solution.py
@@ -62,7 +62,7 @@
 
 def forward_kernel(
     tokens_ref, w_in_ref, bias_in_ref, w_out_ref, vectors_ref,
-    hidden_ref, slope_ref, normed_ref, rstd_ref, ask_ref, resid, query,
+    hidden_ref, slope_ref, normed_ref, rstd_ref, ask_ref, resid, query, pres,
 ):
     step = pl.program_id(0)
 
@@ -70,14 +70,19 @@
     def _():
         resid[...] = tokens_ref[...].astype(jnp.float32) + vectors_ref[:, :768]
 
-    for part in range(4):
-        rows = slice(part * 256, part * 256 + 256)
-        pre = jnp.dot(tokens_ref[rows, :], w_in_ref[...], preferred_element_type=jnp.float32) + bias_in_ref[...]
-        value, grad = slope(pre)
-        value = value.astype(jnp.bfloat16)
-        hidden_ref[rows, :] = value
-        slope_ref[rows, :] = grad.astype(jnp.bfloat16)
-        resid[rows, :] += jnp.dot(value, w_out_ref[...], preferred_element_type=jnp.float32)
+    for part in range(10):
+        if part < 8:
+            rows = slice(part * 128, part * 128 + 128)
+            pres[rows, :] = jnp.dot(tokens_ref[rows, :], w_in_ref[...], preferred_element_type=jnp.float32)
+        if 1 <= part < 9:
+            for start in range(part * 128 - 128, part * 128, 16):
+                rows = slice(start, start + 16)
+                value, grad = slope(pres[rows, :] + bias_in_ref[...])
+                hidden_ref[rows, :] = value.astype(jnp.bfloat16)
+                slope_ref[rows, :] = grad.astype(jnp.bfloat16)
+        if 2 <= part:
+            rows = slice(part * 128 - 256, part * 128 - 128)
+            resid[rows, :] += jnp.dot(hidden_ref[rows, :], w_out_ref[...], preferred_element_type=jnp.float32)
 
     @pl.when(step == pl.num_programs(0) - 1)
     def _():
@@ -119,7 +124,11 @@
             jax.ShapeDtypeStruct((1024, 1), jnp.float32),
             jax.ShapeDtypeStruct((16, 16, 1536), jnp.bfloat16),
         ),
-        scratch_shapes=[pltpu.VMEM((1024, 768), jnp.float32), pltpu.VMEM((16, 768), jnp.float32)],
+        scratch_shapes=[
+            pltpu.VMEM((1024, 768), jnp.float32),
+            pltpu.VMEM((16, 768), jnp.float32),
+            pltpu.VMEM((1024, block), jnp.float32),
+        ],
         compiler_params=limit(56),
         cost_estimate=cost(20),
     )(tokens, w_in, bias_in.reshape(1, -1), w_out, vectors)
@@ -159,8 +168,8 @@
     )(owners, offsets, reader_weights)
 
 
-def picks_kernel(me_ref, table_ref, after_ref, count_ref, share_ref):
-    me = me_ref[0].astype(jnp.float32)
+def picks_kernel(place_ref, table_ref, after_ref, count_ref, share_ref):
+    me = place_ref[2].astype(jnp.float32)
     turn = (lax.broadcasted_iota(jnp.int32, (1, 512), 1) // 64).astype(jnp.float32)
     row = lax.broadcasted_iota(jnp.int32, (256, 512), 0).astype(jnp.float32)
     line = lax.broadcasted_iota(jnp.int32, (128, 512), 0).astype(jnp.float32)
@@ -187,7 +196,7 @@
     lax.fori_loop(0, 16, source, 0, unroll=2)
 
 
-def picks(me, asked, after):
+def picks(place, asked, after):
     vmem = pl.BlockSpec(memory_space=pltpu.VMEM)
     return pl.pallas_call(
         picks_kernel,
@@ -199,7 +208,7 @@
         out_specs=(vmem, vmem),
         compiler_params=limit(24),
         cost_estimate=cost(10),
-    )(me, asked, after)
+    )(place, asked, after)
 
 
 def score_kernel(ask_ref, count_ref, slab, weight_ref, stat_ref, scores):
@@ -244,7 +253,7 @@
     )(asked, count, slab)
 
 
-def pull_kernel(me_ref, stat_ref, weight_ref, share_ref, slab_ref, out_ref, factor, total):
+def pull_kernel(place_ref, stat_ref, weight_ref, share_ref, slab_ref, out_ref, factor, total):
     step = pl.program_id(0)
 
     @pl.when(step == 0)
@@ -253,7 +262,7 @@
         tops, masses = stats[:, 0], stats[:, 1]
         best = jnp.max(tops, axis=0, keepdims=True)
         mass = jnp.sum(jnp.exp(tops - best) * masses, axis=0, keepdims=True)
-        mine = stat_ref[me_ref[0]][0:1]
+        mine = stat_ref[place_ref[2]][0:1]
         line = loss_scale * jnp.exp(mine - best) / mass
         factor[...] = jnp.transpose(jnp.broadcast_to(line, (128, 256)))
         total[...] = jnp.zeros_like(total)
@@ -270,21 +279,21 @@
         out_ref[...] = total[...].astype(jnp.bfloat16)
 
 
-def pull(me, stats, weight, share, slab):
-    quarter = pl.BlockSpec((4, 256, 128), lambda j, me: (j, 0, 0))
+def pull(place, stats, weight, share, slab):
+    quarter = pl.BlockSpec((4, 256, 128), lambda j, place: (j, 0, 0))
     return pl.pallas_call(
         pull_kernel,
         grid_spec=pltpu.PrefetchScalarGridSpec(
             num_scalar_prefetch=1,
             grid=(8,),
-            in_specs=[whole(16, 8, 256), quarter, quarter, pl.BlockSpec((512, 768), lambda j, me: (j, 0))],
+            in_specs=[whole(16, 8, 256), quarter, quarter, pl.BlockSpec((512, 768), lambda j, place: (j, 0))],
             out_specs=whole(256, 768),
             scratch_shapes=[pltpu.VMEM((256, 128), jnp.float32), pltpu.VMEM((256, 768), jnp.float32)],
         ),
         out_shape=jax.ShapeDtypeStruct((256, 768), jnp.bfloat16),
         compiler_params=limit(16),
         cost_estimate=cost(5),
-    )(me, stats, weight, share, slab)
+    )(place, stats, weight, share, slab)
 
 
 def resid_kernel(came_ref, normed_ref, rstd_ref, vectors_ref, resid_grad_ref, out_grad_ref, ups):
@@ -411,7 +420,7 @@
             jax.ShapeDtypeStruct(carry.shape, carry.dtype),
         ),
         input_output_aliases={3: 5},
-        compiler_params=limit(16),
+        compiler_params=limit(56),
         cost_estimate=cost(5),
     )(place, kept, came, carry, *after)
 
@@ -455,12 +464,12 @@
 
 
 def left_sums(first, second, after):
-    narrow, wide = (pl.BlockSpec((96, n), lambda j: (j, 0)) for n in (384, 768))
+    narrow, wide = (pl.BlockSpec((192, n), lambda j: (j, 0)) for n in (384, 768))
     return pl.pallas_call(
         left_kernel,
-        grid=(4,),
+        grid=(2,),
         in_specs=[narrow] * 4 + [wide] * 4 + [anywhere],
-        out_specs=pl.BlockSpec((96, 1152), lambda j: (j, 0)),
+        out_specs=pl.BlockSpec((192, 1152), lambda j: (j, 0)),
         out_shape=jax.ShapeDtypeStruct((384, 1152), jnp.bfloat16),
         compiler_params=limit(16),
         cost_estimate=cost(2),
@@ -514,14 +523,14 @@
     me = lax.axis_index("index")[None]
     y = lax.axis_index("query") // 2
     core = lax.axis_index("query") % 2
-    place = jnp.stack([core, y])
+    place = jnp.stack([core, y, me[0]])
 
     asked = exchange(table(owners[..., 0], offsets, reader_weights))
     vectors = jnp.concatenate([bias_out, gain, shift, jnp.zeros_like(shift)]).reshape(1, 3072)
     hidden, slopes, normed, rstd, ask = forward(tokens, w_in, bias_in, w_out, vectors)
-    count, share = picks(me, asked, rstd)
+    count, share = picks(place, asked, rstd)
     weight, stat = score(exchange(ask), count, slab)
-    partial = pull(me, exchange(stat), weight, share, slab)
+    partial = pull(place, exchange(stat), weight, share, slab)
     came = exchange(partial.reshape(16, 16, 768))
     resid_grad, out_grad = resid_gradient(came, normed, rstd, vectors)
 

time: 191 us -> 185 us (0.969)
  blocking collectives: 11.1 us -> 23.6 us
  waiting for transfers between devices: 33.9 us -> 22.9 us
  starting transfers between devices: 40.6 us -> 38.6 us
    all_to_all x1 -> x2, blocking collectives: 11.1 us -> 23.6 us  [exchange(): return lax.all_to_all(value, 'index', 0, 0, tiled=True)]
    all_to_all x5 -> x4, waiting for transfers between devices: 24.7 us -> 14.1 us  [exchange(): return lax.all_to_all(value, 'index', 0, 0, tiled=True)]
    pallas_call x1, Pallas kernels: 22.1 us -> 19.6 us  [forward(): pl.pallas_call(forward_kernel, grid=(3072 // block,), in_specs=[whole(102...]
    pallas_call x1, Pallas kernels: 2.71 us -> 5.11 us  [first_pair(): pl.pallas_call(first_kernel, grid_spec=pltpu.PrefetchScalarGridSpec(num_s...]
    pallas_call x1, Pallas kernels: 3.55 us -> 1.23 us  [left_sums(): pl.pallas_call(left_kernel, grid=(2,), in_specs=[narrow] * 4 + [wide] * 4...]
    all_to_all x5 -> x4, starting transfers between devices: 26.1 us -> 24.6 us  [exchange(): return lax.all_to_all(value, 'index', 0, 0, tiled=True)]
    unnamed x42 -> x52, local copies, waits for them, and re-layouts: 20.1 us -> 18.8 us
  transfers between devices with their start and end apart: 16 -> 15, of which waited for: 7 -> 7; matrix products, arithmetic and copies ran while one was open for 10% -> 9% of each run, Pallas kernels for 22% -> 22%
where the time goes in v5:
time: 185 us
  Pallas kernels  62.4 us (34%)
  starting transfers between devices  38.6 us (21%)
  blocking collectives  23.6 us (13%)
  waiting for transfers between devices  22.9 us (12%)
  local copies, waits for them, and re-layouts  18.8 us (10%)
  matrix products  16.5 us (9%)
    all_to_all x4, starting transfers between devices, exchange(): return lax.all_to_all(value, 'index', 0, 0, tiled=True)  24.6 us
    all_to_all x2, blocking collectives, exchange(): return lax.all_to_all(value, 'index', 0, 0, tiled=True)  23.6 us
    pallas_call x1, Pallas kernels, forward(): pl.pallas_call(forward_kernel, grid=(3072 // block,), in_specs=[whole(102...  19.6 us
    unnamed x52, local copies, waits for them, and re-layouts  18.8 us
    pallas_call x2, Pallas kernels, weight_sums(): pl.pallas_call(weight_kernel, grid_spec=pltpu.PrefetchScalarGridSpec(num_...  14.4 us
    all_to_all x4, waiting for transfers between devices, exchange(): return lax.all_to_all(value, 'index', 0, 0, tiled=True)  14.1 us
    ppermute x11, starting transfers between devices, shifted(): return lax.ppermute(value, every, pairs)  13.9 us
    dot_general x1, matrix products, body(): jnp.dot(pre_grad, w_in.T, preferred_element_type=jnp.float32)  9.21 us
  transfers between devices with their start and end apart: 15, of which 7 were waited for; matrix products, arithmetic and copies ran while one was open for 9% of the time, Pallas kernels for 22%

profile of v5, /device:TPU:0, one launch (start us, length us, event | category | flops | bytes accessed | tf_op | source)
XLA Modules:
  0.0 184.5 jit_solution(5119534945704665584)
XLA Ops:
  0.7 1.6 shard_map.123
  2.3 8.0 %all-to-all-start.1 = ((bf16[16,16,512]{2,1,0:T(8,128)(2,1)}), bf16[16,16,512]{2,1,0:T(8,128)(2,1)S(1)}, u32[]{:S(2)}, u32[]{:S(2)}) async-start(bf16[16,16,512]{2,1,0:T(8,128)(2,1)} %shard_map.123), calls=%async_computation.1 | async-start | bytes 524288 | tf_op jit(solution)/shard_map/all_to_all | solution.py:38
  10.3 0.6 pad_maximum_fusion
  10.9 19.6 %shard_map.122 = (bf16[1024,3072]{1,0:T(8,128)(2,1)}, bf16[1024,3072]{1,0:T(8,128)(2,1)}, f32[1024,768]{1,0:T(8,128)}, f32[1024,1]{1,0:T(8,128)}, bf16[16,16,1536]{2,1,0:T(8,128)(2,1)}) custom-call(bf16[1024,768]{1,0:T(8,128)(2,1)} %right_ref.1, bf16[768,3072]{1,0:T(8,128)(2,1)} %w_in_ref.1, f32[1,3072]{1,0:T(1,128)} %bitcast.17, ...), custom_call_target="tpu_custom_call" | custom-call | flops 20000000000 | bytes 1000 | tf_op jit(solution)/shard_map/pallas_call | solution.py:109
  30.6 0.1 pad_add_fusion.place_ref
  30.7 0.0 all-to-all-done.1.table_ref
  30.7 7.2 %all-to-all-start = ((bf16[16,16,1536]{2,1,0:T(8,128)(2,1)}), bf16[16,16,1536]{2,1,0:T(8,128)(2,1)S(1)}, u32[]{:S(2)}, u32[]{:S(2)}) async-start(bf16[16,16,1536]{2,1,0:T(8,128)(2,1)} %get-tuple-element.32), calls=%async_computation | async-start | bytes 1572864 | tf_op jit(solution)/shard_map/all_to_all | solution.py:38
  37.9 1.0 copy-done.15
  38.9 6.4 %shard_map.124 = (bf16[32,256,128]{2,1,0:T(8,128)(2,1)S(1)}, f32[32,256,128]{2,1,0:T(8,128)S(1)}) custom-call(s32[3]{0:T(128)S(1)} %pad_add_fusion.place_ref, bf16[16,16,512]{2,1,0:T(8,128)(2,1)S(1)} %all-to-all-done.1.table_ref, f32[1024,1]{1,0:T(8,128)S(1)} %copy-done.15), custom_call_target="tpu_custom_call" | custom-call | flops 10000000000 | bytes 1000 | tf_op jit(solution)/shard_map/pallas_call | solution.py:201
  45.3 1.9 %copy-done.10 = f32[32,256,128]{2,1,0:T(8,128)} copy-done((f32[32,256,128]{2,1,0:T(8,128)}, f32[32,256,128]{2,1,0:T(8,128)S(1)}, u32[]{:S(2)}) %copy-start.10) | copy-done | bytes 4194328
  47.3 4.4 %all-to-all-done.ask_ref = bf16[16,16,1536]{2,1,0:T(8,128)(2,1)S(1)} async-done(((bf16[16,16,1536]{2,1,0:T(8,128)(2,1)}), bf16[16,16,1536]{2,1,0:T(8,128)(2,1)S(1)}, u32[]{:S(2)}, u32[]{:S(2)}) %all-to-all-start) | async-done | bytes 786464 | tf_op jit(solution)/shard_map/all_to_all | solution.py:38
  51.7 2.8 %copy-done.2 = bf16[4096,768]{1,0:T(8,128)(2,1)S(1)} copy-done((bf16[4096,768]{1,0:T(8,128)(2,1)S(1)}, bf16[4096,768]{1,0:T(8,128)(2,1)}, u32[]{:S(2)}) %copy-start.2) | copy-done | bytes 6291480
  54.5 4.9 %shard_map.125 = (f32[32,256,128]{2,1,0:T(8,128)S(1)}, f32[16,8,256]{2,1,0:T(8,128)S(1)}) custom-call(bf16[16,16,1536]{2,1,0:T(8,128)(2,1)S(1)} %all-to-all-done.ask_ref, bf16[32,256,128]{2,1,0:T(8,128)(2,1)S(1)} %get-tuple-element.34.count_ref, bf16[4096,768]{1,0:T(8,128)(2,1)S(1)} %copy-done.2), custom_call_target="tpu_custom_call" | custom-call | flops 8000000000 | bytes 1000 | tf_op jit(solution)/shard_map/pallas_call | solution.py:242
  59.3 11.1 %all_to_all.30.stat_ref = f32[16,8,256]{2,1,0:T(8,128)S(1)} all-to-all(f32[16,8,256]{2,1,0:T(8,128)S(1)} %get-tuple-element.35), channel_id=1, replica_groups=mesh['query'=8,'index'=16] {'index'}, dimensions={0} | all-to-all | bytes 262144 | tf_op jit(solution)/shard_map/all_to_all | solution.py:38
  70.4 0.0 copy-done.11
  70.4 2.8 %copy-done.3 = bf16[4096,768]{1,0:T(8,128)(2,1)S(1)} copy-done((bf16[4096,768]{1,0:T(8,128)(2,1)S(1)}, bf16[4096,768]{1,0:T(8,128)(2,1)}, u32[]{:S(2)}) %copy-start.3) | copy-done | bytes 6291480
  73.2 5.5 %shard_map.126 = bf16[256,768]{1,0:T(8,128)(2,1)S(1)} custom-call(s32[3]{0:T(128)S(1)} %pad_add_fusion.place_ref, f32[16,8,256]{2,1,0:T(8,128)S(1)} %all_to_all.30.stat_ref, f32[32,256,128]{2,1,0:T(8,128)S(1)} %get-tuple-element.36.weight_ref, f32[32,256,128]{2,1,0:T(8,128)S(1)} %copy-done.11, bf16[4096,768]{1,0:T(8,128)(2,1)S(1)} %copy-done.3), custom_call_target="tpu_custom_call" | custom-call | flops 5000000000 | bytes 1000 | tf_op jit(solution)/shard_map/pallas_call | solution.py:284
  78.8 12.5 %all_to_all.31.came_ref = bf16[16,16,768]{2,1,0:T(8,128)(2,1)S(1)} all-to-all(bf16[16,16,768]{2,1,0:T(8,128)(2,1)S(1)} %bitcast.12), channel_id=1, replica_groups=mesh['query'=8,'index'=16] {'index'}, dimensions={0} | all-to-all | bytes 786432 | tf_op jit(solution)/shard_map/all_to_all | solution.py:38
  91.3 1.1 shard_map.127
  92.3 0.0 copy-start.13
  92.3 1.6 copy-done.13
  94.0 2.8 %copy-done.18 = bf16[1024,3072]{1,0:T(8,128)(2,1)S(1)} copy-done((bf16[1024,3072]{1,0:T(8,128)(2,1)S(1)}, bf16[1024,3072]{1,0:T(8,128)(2,1)}, u32[]{:S(2)}) %copy-start.18) | copy-done | bytes 6291480
  96.7 7.2 %shard_map.128 = (bf16[4,384,768]{2,1,0:T(8,128)(2,1)S(1)}, bf16[4,384,768]{2,1,0:T(8,128)(2,1)S(1)}) custom-call(s32[3]{0:T(128)S(1)} %pad_add_fusion.place_ref, bf16[1024,3072]{1,0:T(8,128)(2,1)S(1)} %copy-done.18, bf16[1024,768]{1,0:T(8,128)(2,1)S(1)} %get-tuple-element.41.right_ref.carry_ref), custom_call_target="tpu_custom_call" | custom-call | flops 40000000000 | bytes 1000 | tf_op jit(solution)/shard_map/pallas_call | solution.py:350
  104.0 0.1 collective-permute-start
  104.1 4.5 %collective-permute-done.came_ref = bf16[4,384,768]{2,1,0:T(8,128)(2,1)S(1)} collective-permute-done((bf16[4,384,768]{2,1,0:T(8,128)(2,1)S(1)}, bf16[4,384,768]{2,1,0:T(8,128)(2,1)S(1)}, u32[]{:S(2)}, u32[]{:S(2)}) %collective-permute-start) | collective-permute-done | bytes 2359328 | tf_op jit(solution)/shard_map/ppermute | solution.py:47
  108.6 1.5 shard_map.129
  110.1 0.0 copy-start.7
  110.1 1.6 collective-permute-start.1
  111.7 1.7 collective-permute-start.2
  113.4 7.3 %multiply_convert_fusion.left_ref.refs_0_ = bf16[1024,3072]{1,0:T(8,128)(2,1)S(1)} fusion(bf16[1024,3072]{1,0:T(8,128)(2,1)} %get-tuple-element.45, bf16[1024,768]{1,0:T(8,128)(2,1)S(1)} %get-tuple-element.44, bf16[3072,768]{1,0:T(8,128)(2,1)S(1)} %bitcast.16), kind=kOutput, calls=%fused_computation | convolution fusion | flops 4841275392 | bytes 18874368 | tf_op jit(solution)/shard_map/dot_general | solution.py:544
  120.8 7.2 %shard_map.130 = (bf16[4,384,768]{2,1,0:T(8,128)(2,1)S(1)}, bf16[4,384,768]{2,1,0:T(8,128)(2,1)S(1)}) custom-call(s32[3]{0:T(128)S(1)} %pad_add_fusion.place_ref, bf16[1024,3072]{1,0:T(8,128)(2,1)S(1)} %multiply_convert_fusion.left_ref.refs_0_, bf16[1024,768]{1,0:T(8,128)(2,1)S(1)} %copy-done.4), custom_call_target="tpu_custom_call" | custom-call | flops 40000000000 | bytes 1000 | tf_op jit(solution)/shard_map/pallas_call | solution.py:350
  128.1 0.0 collective-permute-done.1.refs_1_.refs_5_
  128.1 0.0 collective-permute-done.2.refs_2_.refs_6_
  128.1 0.1 collective-permute-start.3
  128.2 1.3 copy-done.17
  129.5 0.6 copy-done.19
  130.1 1.9 %collective-permute-start.7 = (bf16[384,768]{1,0:T(8,128)(2,1)S(1)}, bf16[384,768]{1,0:T(8,128)(2,1)S(1)}, u32[]{:S(2)}, u32[]{:S(2)}) collective-permute-start(bf16[384,768]{1,0:T(8,128)(2,1)S(1)} %get-tuple-element.56), channel_id=1, source_target_pairs={{0,64},{1,65},{2,66},{3,67},{4,68},{5,69},{6,70},{7,71},{8,72},{9,... | collective-permute-start | bytes 1769480 | tf_op jit(solution)/shard_map/ppermute | solution.py:47
  132.0 0.7 collective-permute-done.3.came_ref
  132.7 1.4 copy-done.23
  134.1 5.1 %shard_map.133 = (f32[384,384]{1,0:T(8,128)}, bf16[384,384]{1,0:T(8,128)(2,1)}, bf16[384,384]{1,0:T(8,128)(2,1)}, bf16[384,384]{1,0:T(8,128)(2,1)}, bf16[16,96,3...) custom-call(s32[3]{0:T(128)} %copy-done.1, bf16[4,384,768]{2,1,0:T(8,128)(2,1)} %copy-done.17, ...), custom_call_target="tpu_custom_call", output_to_operand_aliasing={{5}: (3, {})} | custom-call | flops 5000000000 | bytes 1000 | tf_op jit(solution)/shard_map/pallas_call | solution.py:407
  139.2 3.7 %all-to-all-start.5 = ((bf16[16,96,384]{2,1,0:T(8,128)(2,1)}), bf16[16,96,384]{2,1,0:T(8,128)(2,1)S(1)}, u32[]{:S(2)}, u32[]{:S(2)}) async-start(bf16[16,96,384]{2,1,0:T(8,128)(2,1)} %get-tuple-element.57), calls=%async_computation.5 | async-start | bytes 2359296 | tf_op jit(solution)/shard_map/all_to_all | solution.py:38
  142.9 0.4 collective-permute-start.4
  143.3 2.9 %collective-permute-start.5 = (bf16[384,384]{1,0:T(8,128)(2,1)}, bf16[384,384]{1,0:T(8,128)(2,1)S(1)}, u32[]{:S(2)}, u32[]{:S(2)}) collective-permute-start(bf16[384,384]{1,0:T(8,128)(2,1)} %get-tuple-element.54), channel_id=1, source_target_pairs={{0,96},{1,97},{2,98},{3,99},{4,100},{5,101},{6,102},{7,103},{8,104... | collective-permute-start | bytes 884744 | tf_op jit(solution)/shard_map/ppermute | solution.py:47
  146.2 0.7 collective-permute-start.6
  146.9 9.2 %add_convert_fusion.refs_8_.after_ref = bf16[1024,768]{1,0:T(8,128)(2,1)S(1)} fusion(f32[1024,768]{1,0:T(8,128)} %copy-done.13, bf16[1024,3072]{1,0:T(8,128)(2,1)} %get-tuple-element.51, bf16[768,3072]{1,0:T(8,128)(2,1)} %w_in_ref.1), kind=kOutput, calls=%fused_computation.1 | convolution fusion | flops 4833411072 | bytes 15728640 | tf_op jit(solution)/shard_map/dot_general | solution.py:554
  156.2 0.0 collective-permute-done.7.refs_7_
  156.2 0.0 collective-permute-done.4.refs_1_
  156.2 3.0 %collective-permute-done.5.refs_2_ = bf16[384,384]{1,0:T(8,128)(2,1)S(1)} collective-permute-done((bf16[384,384]{1,0:T(8,128)(2,1)}, bf16[384,384]{1,0:T(8,128)(2,1)S(1)}, u32[]{:S(2)}, u32[]{:S(2)}) %collective-permute-start.5) | collective-permute-done | bytes 294944 | tf_op jit(solution)/shard_map/ppermute | solution.py:47
  159.1 0.7 collective-permute-done.6.refs_3_
  159.8 1.2 shard_map.134
  161.1 1.1 copy-done.5
  162.2 1.1 all-to-all-done.5.came_ref
  163.3 5.7 %all-to-all-start.4 = ((bf16[16,24,1152]{2,1,0:T(8,128)(2,1)}), bf16[16,24,1152]{2,1,0:T(8,128)(2,1)S(1)}, u32[]{:S(2)}, u32[]{:S(2)}) async-start(bf16[16,24,1152]{2,1,0:T(8,128)(2,1)} %bitcast.7), calls=%async_computation.4 | async-start | bytes 1769472 | tf_op jit(solution)/shard_map/all_to_all | solution.py:38
  169.0 0.0 copy-start.6
  169.1 1.4 copy-done.6
  170.5 0.2 shard_map.135
  170.7 1.2 collective-permute-start.8
  171.9 2.1 %collective-permute-start.9 = (f32[24,384]{1,0:T(8,128)S(1)}, f32[24,384]{1,0:T(8,128)S(1)}, u32[]{:S(2)}, u32[]{:S(2)}) collective-permute-start(f32[24,384]{1,0:T(8,128)S(1)} %get-tuple-element.60), channel_id=1, source_target_pairs={{0,96},{1,97},{2,98},{3,99},{4,100},{5,101},{6,102},{7,103},{8,104... | collective-permute-start | bytes 110600 | tf_op jit(solution)/shard_map/ppermute | solution.py:47
  174.0 1.1 collective-permute-start.10
  175.1 8.6 %all-to-all-done.4.refs_0_ = bf16[16,24,1152]{2,1,0:T(8,128)(2,1)S(1)} async-done(((bf16[16,24,1152]{2,1,0:T(8,128)(2,1)}), bf16[16,24,1152]{2,1,0:T(8,128)(2,1)S(1)}, u32[]{:S(2)}, u32[]{:S(2)}) %all-to-all-start.4) | async-done | bytes 884768 | tf_op jit(solution)/shard_map/all_to_all | solution.py:38
  183.7 0.0 collective-permute-done.8.refs_2_
  183.7 0.0 collective-permute-done.9.refs_3_
  183.7 0.0 collective-permute-done.10.refs_4_
  183.7 0.8 shard_map.136
  (41 shorter events, 0.1 us)
Async XLA Ops:
  0.6 9.7 %copy-start.20 = (f32[768]{0:T(1024)S(1)}, f32[768]{0:T(1024)}, u32[]{:S(2)}) copy-start(f32[768]{0:T(1024)} %param.17) | copy-start | bytes 9220
  0.6 9.7 %copy-start.21 = (f32[768]{0:T(1024)S(1)}, f32[768]{0:T(1024)}, u32[]{:S(2)}) copy-start(f32[768]{0:T(1024)} %param.16) | copy-start | bytes 9220
  0.7 9.7 %copy-start.22 = (f32[768]{0:T(1024)S(1)}, f32[768]{0:T(1024)}, u32[]{:S(2)}) copy-start(f32[768]{0:T(1024)} %param.15) | copy-start | bytes 9220
  2.3 28.3 %all-to-all-start.1 = ((bf16[16,16,512]{2,1,0:T(8,128)(2,1)}), bf16[16,16,512]{2,1,0:T(8,128)(2,1)S(1)}, u32[]{:S(2)}, u32[]{:S(2)}) async-start(bf16[16,16,512]{2,1,0:T(8,128)(2,1)} %shard_map.123), calls=%async_computation.1 | async-start | bytes 524288 | tf_op jit(solution)/shard_map/all_to_all | solution.py:38
  30.7 90.1 %copy-start.1 = (s32[3]{0:T(128)}, s32[3]{0:T(128)S(1)}, u32[]{:S(2)}) copy-start(s32[3]{0:T(128)S(1)} %pad_add_fusion.place_ref) | copy-start | bytes 40
  30.7 21.0 %all-to-all-start = ((bf16[16,16,1536]{2,1,0:T(8,128)(2,1)}), bf16[16,16,1536]{2,1,0:T(8,128)(2,1)S(1)}, u32[]{:S(2)}, u32[]{:S(2)}) async-start(bf16[16,16,1536]{2,1,0:T(8,128)(2,1)} %get-tuple-element.32), calls=%async_computation | async-start | bytes 1572864 | tf_op jit(solution)/shard_map/all_to_all | solution.py:38
  37.9 1.0 copy-start.15
  45.3 1.9 %copy-start.10 = (f32[32,256,128]{2,1,0:T(8,128)}, f32[32,256,128]{2,1,0:T(8,128)S(1)}, u32[]{:S(2)}) copy-start(f32[32,256,128]{2,1,0:T(8,128)S(1)} %get-tuple-element.37.share_ref) | copy-start | bytes 12582916
  51.7 2.8 %copy-start.2 = (bf16[4096,768]{1,0:T(8,128)(2,1)S(1)}, bf16[4096,768]{1,0:T(8,128)(2,1)}, u32[]{:S(2)}) copy-start(bf16[4096,768]{1,0:T(8,128)(2,1)} %slab_ref.1) | copy-start | bytes 18874372
  54.5 16.0 %copy-start.11 = (f32[32,256,128]{2,1,0:T(8,128)S(1)}, f32[32,256,128]{2,1,0:T(8,128)}, u32[]{:S(2)}) copy-start(f32[32,256,128]{2,1,0:T(8,128)} %copy-done.10) | copy-start | bytes 12582916
  70.4 2.8 %copy-start.3 = (bf16[4096,768]{1,0:T(8,128)(2,1)S(1)}, bf16[4096,768]{1,0:T(8,128)(2,1)}, u32[]{:S(2)}) copy-start(bf16[4096,768]{1,0:T(8,128)(2,1)} %slab_ref.1) | copy-start | bytes 18874372
  73.2 18.0 %copy-start = (f32[3072]{0:T(1024)S(1)}, f32[3072]{0:T(1024)}, u32[]{:S(2)}) copy-start(f32[3072]{0:T(1024)} %pad_maximum_fusion) | copy-start | bytes 36868
  73.2 18.0 %copy-start.12 = (f32[1024,768]{1,0:T(8,128)S(1)}, f32[1024,768]{1,0:T(8,128)}, u32[]{:S(2)}) copy-start(f32[1024,768]{1,0:T(8,128)} %get-tuple-element.38.normed_ref) | copy-start | bytes 9437188
  73.2 18.0 %copy-start.16 = (f32[1024,1]{1,0:T(8,128)S(1)}, f32[1024,1]{1,0:T(8,128)}, u32[]{:S(2)}) copy-start(f32[1024,1]{1,0:T(8,128)} %get-tuple-element.33.after_ref.rstd_ref) | copy-start | bytes 12292
  73.2 40.2 %slice-start = ((s8[4718592]{0:T(1024)(128)(4,1)}), s8[4194304]{0:T(1024)(128)(4,1)S(1)}, s32[]{:S(2)}) async-start(s8[4718592]{0:T(1024)(128)(4,1)} %bitcast.15), calls=%async_computation.6 | async-start | bytes 8388608
  92.3 1.6 copy-start.13
  94.0 2.8 %copy-start.18 = (bf16[1024,3072]{1,0:T(8,128)(2,1)S(1)}, bf16[1024,3072]{1,0:T(8,128)(2,1)}, u32[]{:S(2)}) copy-start(bf16[1024,3072]{1,0:T(8,128)(2,1)} %get-tuple-element.40.left_ref) | copy-start | bytes 18874372
  96.7 16.7 %slice-start.1 = ((s8[4718592]{0:T(1024)(128)(4,1)}), s8[524288]{0:T(1024)(128)(4,1)S(1)}, s32[]{:S(2)}) async-start(s8[4718592]{0:T(1024)(128)(4,1)} %bitcast.15), calls=%async_computation.7 | async-start | bytes 1048576
  104.0 4.6 %collective-permute-start = (bf16[4,384,768]{2,1,0:T(8,128)(2,1)S(1)}, bf16[4,384,768]{2,1,0:T(8,128)(2,1)S(1)}, u32[]{:S(2)}, u32[]{:S(2)}) collective-permute-start(bf16[4,384,768]{2,1,0:T(8,128)(2,1)S(1)} %get-tuple-element.43), channel_id=1, source_target_pairs={{0,16},{1,17},{2,18},{3,19},{4,20},{5,21},{6,22},{7,23},{8,24},{9,... | collective-permute-start | bytes 7077896 | tf_op jit(solution)/shard_map/ppermute | solution.py:47
  110.1 18.1 %copy-start.7 = (f32[384,768]{1,0:T(8,128)}, f32[384,768]{1,0:T(8,128)S(1)}, u32[]{:S(2)}) copy-start(f32[384,768]{1,0:T(8,128)S(1)} %get-tuple-element.50.own_ref.refs_4_) | copy-start | bytes 3538948
  110.1 18.0 %collective-permute-start.1 = (bf16[384,768]{1,0:T(8,128)(2,1)S(1)}, bf16[384,768]{1,0:T(8,128)(2,1)S(1)}, u32[]{:S(2)}, u32[]{:S(2)}) collective-permute-start(bf16[384,768]{1,0:T(8,128)(2,1)S(1)} %get-tuple-element.48), channel_id=1, source_target_pairs={{0,32},{1,33},{2,34},{3,35},{4,36},{5,37},{6,38},{7,39},{8,40},{9,... | collective-permute-start | bytes 1769480 | tf_op jit(solution)/shard_map/ppermute | solution.py:47
  111.7 16.3 %collective-permute-start.2 = (bf16[384,768]{1,0:T(8,128)(2,1)S(1)}, bf16[384,768]{1,0:T(8,128)(2,1)S(1)}, u32[]{:S(2)}, u32[]{:S(2)}) collective-permute-start(bf16[384,768]{1,0:T(8,128)(2,1)S(1)} %get-tuple-element.49), channel_id=1, source_target_pairs={{0,96},{1,97},{2,98},{3,99},{4,100},{5,101},{6,102},{7,103},{8,104... | collective-permute-start | bytes 1769480 | tf_op jit(solution)/shard_map/ppermute | solution.py:47
  113.4 7.3 %copy-start.4 = (bf16[1024,768]{1,0:T(8,128)(2,1)S(1)}, bf16[1024,768]{1,0:T(8,128)(2,1)}, u32[]{:S(2)}) copy-start(bf16[1024,768]{1,0:T(8,128)(2,1)} %right_ref.1) | copy-start | bytes 4718596
  120.8 7.2 %copy-start.14 = (bf16[1024,3072]{1,0:T(8,128)(2,1)}, bf16[1024,3072]{1,0:T(8,128)(2,1)S(1)}, u32[]{:S(2)}) copy-start(bf16[1024,3072]{1,0:T(8,128)(2,1)S(1)} %multiply_convert_fusion.left_ref.refs_0_) | copy-start | bytes 18874372
  128.0 1.5 copy-start.17
  128.1 4.6 %collective-permute-start.3 = (bf16[4,384,768]{2,1,0:T(8,128)(2,1)S(1)}, bf16[4,384,768]{2,1,0:T(8,128)(2,1)S(1)}, u32[]{:S(2)}, u32[]{:S(2)}) collective-permute-start(bf16[4,384,768]{2,1,0:T(8,128)(2,1)S(1)} %shard_map.131), channel_id=1, source_target_pairs={{0,16},{1,17},{2,18},{3,19},{4,20},{5,21},{6,22},{7,23},{8,24},{9,... | collective-permute-start | bytes 7077896 | tf_op jit(solution)/shard_map/ppermute | solution.py:47
  129.5 0.6 copy-start.19
  130.1 26.1 %collective-permute-start.7 = (bf16[384,768]{1,0:T(8,128)(2,1)S(1)}, bf16[384,768]{1,0:T(8,128)(2,1)S(1)}, u32[]{:S(2)}, u32[]{:S(2)}) collective-permute-start(bf16[384,768]{1,0:T(8,128)(2,1)S(1)} %get-tuple-element.56), channel_id=1, source_target_pairs={{0,64},{1,65},{2,66},{3,67},{4,68},{5,69},{6,70},{7,71},{8,72},{9,... | collective-permute-start | bytes 1769480 | tf_op jit(solution)/shard_map/ppermute | solution.py:47
  132.7 1.4 copy-start.23
  139.2 24.1 %all-to-all-start.5 = ((bf16[16,96,384]{2,1,0:T(8,128)(2,1)}), bf16[16,96,384]{2,1,0:T(8,128)(2,1)S(1)}, u32[]{:S(2)}, u32[]{:S(2)}) async-start(bf16[16,96,384]{2,1,0:T(8,128)(2,1)} %get-tuple-element.57), calls=%async_computation.5 | async-start | bytes 2359296 | tf_op jit(solution)/shard_map/all_to_all | solution.py:38
  142.9 13.3 %collective-permute-start.4 = (bf16[384,384]{1,0:T(8,128)(2,1)}, bf16[384,384]{1,0:T(8,128)(2,1)S(1)}, u32[]{:S(2)}, u32[]{:S(2)}) collective-permute-start(bf16[384,384]{1,0:T(8,128)(2,1)} %get-tuple-element.53), channel_id=1, source_target_pairs={{0,32},{1,33},{2,34},{3,35},{4,36},{5,37},{6,38},{7,39},{8,40},{9,... | collective-permute-start | bytes 884744 | tf_op jit(solution)/shard_map/ppermute | solution.py:47
  143.3 15.8 %collective-permute-start.5 = (bf16[384,384]{1,0:T(8,128)(2,1)}, bf16[384,384]{1,0:T(8,128)(2,1)S(1)}, u32[]{:S(2)}, u32[]{:S(2)}) collective-permute-start(bf16[384,384]{1,0:T(8,128)(2,1)} %get-tuple-element.54), channel_id=1, source_target_pairs={{0,96},{1,97},{2,98},{3,99},{4,100},{5,101},{6,102},{7,103},{8,104... | collective-permute-start | bytes 884744 | tf_op jit(solution)/shard_map/ppermute | solution.py:47
  146.2 13.6 %collective-permute-start.6 = (bf16[384,384]{1,0:T(8,128)(2,1)}, bf16[384,384]{1,0:T(8,128)(2,1)S(1)}, u32[]{:S(2)}, u32[]{:S(2)}) collective-permute-start(bf16[384,384]{1,0:T(8,128)(2,1)} %get-tuple-element.55), channel_id=1, source_target_pairs={{0,64},{1,65},{2,66},{3,67},{4,68},{5,69},{6,70},{7,71},{8,72},{9,... | collective-permute-start | bytes 884744 | tf_op jit(solution)/shard_map/ppermute | solution.py:47
  146.9 12.9 %copy-start.8 = (f32[384,768]{1,0:T(8,128)S(1)}, f32[384,768]{1,0:T(8,128)}, u32[]{:S(2)}) copy-start(f32[384,768]{1,0:T(8,128)} %copy-done.7) | copy-start | bytes 3538948
  146.9 12.9 %copy-start.9 = (f32[384,384]{1,0:T(8,128)S(1)}, f32[384,384]{1,0:T(8,128)}, u32[]{:S(2)}) copy-start(f32[384,384]{1,0:T(8,128)} %get-tuple-element.52.refs_0_) | copy-start | bytes 1769476
  161.1 1.1 copy-start.5
  163.3 20.4 %all-to-all-start.4 = ((bf16[16,24,1152]{2,1,0:T(8,128)(2,1)}), bf16[16,24,1152]{2,1,0:T(8,128)(2,1)S(1)}, u32[]{:S(2)}, u32[]{:S(2)}) async-start(bf16[16,24,1152]{2,1,0:T(8,128)(2,1)} %bitcast.7), calls=%async_computation.4 | async-start | bytes 1769472 | tf_op jit(solution)/shard_map/all_to_all | solution.py:38
  169.0 1.4 copy-start.6
  170.7 13.0 %collective-permute-start.8 = (f32[24,384]{1,0:T(8,128)S(1)}, f32[24,384]{1,0:T(8,128)S(1)}, u32[]{:S(2)}, u32[]{:S(2)}) collective-permute-start(f32[24,384]{1,0:T(8,128)S(1)} %get-tuple-element.59), channel_id=1, source_target_pairs={{0,32},{1,33},{2,34},{3,35},{4,36},{5,37},{6,38},{7,39},{8,40},{9,... | collective-permute-start | bytes 110600 | tf_op jit(solution)/shard_map/ppermute | solution.py:47
  171.9 11.8 %collective-permute-start.9 = (f32[24,384]{1,0:T(8,128)S(1)}, f32[24,384]{1,0:T(8,128)S(1)}, u32[]{:S(2)}, u32[]{:S(2)}) collective-permute-start(f32[24,384]{1,0:T(8,128)S(1)} %get-tuple-element.60), channel_id=1, source_target_pairs={{0,96},{1,97},{2,98},{3,99},{4,100},{5,101},{6,102},{7,103},{8,104... | collective-permute-start | bytes 110600 | tf_op jit(solution)/shard_map/ppermute | solution.py:47
  174.0 9.7 %collective-permute-start.10 = (f32[24,384]{1,0:T(8,128)S(1)}, f32[24,384]{1,0:T(8,128)S(1)}, u32[]{:S(2)}, u32[]{:S(2)}) collective-permute-start(f32[24,384]{1,0:T(8,128)S(1)} %get-tuple-element.61), channel_id=1, source_target_pairs={{0,64},{1,65},{2,66},{3,67},{4,68},{5,69},{6,70},{7,71},{8,72},{9,... | collective-permute-start | bytes 110600 | tf_op jit(solution)/shard_map/ppermute | solution.py:47

commit v6 on v5

--- a/solution.py
+++ b/solution.py
@@ -361,6 +361,28 @@
     )(place, left, right)
 
 
+def half_kernel(place_ref, left_ref, right_ref, out_ref):
+    out_ref[0] = columns_dot(left_ref[...], right_ref[...]).astype(jnp.bfloat16)
+
+
+def weight_half(place, left, right, other):
+    def units(j, place):
+        return 0, 2 * j + (1 - place[0] if other else place[0])
+
+    return pl.pallas_call(
+        half_kernel,
+        grid_spec=pltpu.PrefetchScalarGridSpec(
+            num_scalar_prefetch=1,
+            grid=(4,),
+            in_specs=[pl.BlockSpec((1024, 384), units), whole(1024, 768)],
+            out_specs=pl.BlockSpec((1, 384, 768), lambda j, place: (j, 0, 0)),
+        ),
+        out_shape=jax.ShapeDtypeStruct((4, 384, 768), jnp.bfloat16),
+        compiler_params=limit(24),
+        cost_estimate=cost(40),
+    )(place, left, right)
+
+
 def second_kernel(place_ref, kept_ref, came_ref, carry_ref, own_ref, one_ref, three_ref, two_ref, carried_ref):
     for out, step in ((own_ref, 0), (one_ref, 1), (three_ref, 3), (two_ref, 2)):
         at = (place_ref[1] + step) % 4
@@ -537,7 +559,8 @@
     def round_y(own, *pieces):
         return [own] + [shifted(piece, 0, step) for piece, step in zip(pieces, (1, 3, 2))]
 
-    away, kept = weight_sums(place, hidden, out_grad)
+    away = weight_half(place, hidden, out_grad, True)
+    kept = weight_half(place, hidden, out_grad, False)
     *second, out_grad = second_pair(place, kept, shifted(away, 1, 0), out_grad)
     second = round_y(*second)
     pre_grad = (

time: 185 us -> 185 us (level)
  waiting for transfers between devices: 22.9 us -> 17.4 us
  local copies, waits for them, and re-layouts: 18.8 us -> 21.8 us
    pallas_call x0 -> x2, Pallas kernels: none -> 8.69 us  [weight_half(): pl.pallas_call(half_kernel, grid_spec=pltpu.PrefetchScalarGridSpec(num_sc...]
    pallas_call x2 -> x1, Pallas kernels: 14.4 us -> 7.21 us  [weight_sums(): pl.pallas_call(weight_kernel, grid_spec=pltpu.PrefetchScalarGridSpec(num_...]
    ppermute x11, waiting for transfers between devices: 8.86 us -> 4.7 us  [shifted(): return lax.ppermute(value, every, pairs)]
    unnamed x52 -> x56, local copies, waits for them, and re-layouts: 18.8 us -> 21.7 us
  transfers between devices with their start and end apart: 15 -> 15, of which waited for: 7 -> 7; matrix products, arithmetic and copies ran while one was open for 9% -> 9% of each run, Pallas kernels for 22% -> 24%
where the time goes in v6:
time: 185 us; the launch traced here: 184 us
  Pallas kernels  63.8 us (34%)
  starting transfers between devices  38.6 us (21%)
  blocking collectives  24.4 us (13%)
  local copies, waits for them, and re-layouts  21.8 us (12%)
  waiting for transfers between devices  17.4 us (9%)
  matrix products  16.5 us (9%)
    all_to_all x4, starting transfers between devices, exchange(): return lax.all_to_all(value, 'index', 0, 0, tiled=True)  24.9 us
    all_to_all x2, blocking collectives, exchange(): return lax.all_to_all(value, 'index', 0, 0, tiled=True)  24.4 us
    unnamed x56, local copies, waits for them, and re-layouts  21.7 us
    pallas_call x1, Pallas kernels, forward(): pl.pallas_call(forward_kernel, grid=(3072 // block,), in_specs=[whole(102...  19.6 us
    ppermute x11, starting transfers between devices, shifted(): return lax.ppermute(value, every, pairs)  13.8 us
    all_to_all x4, waiting for transfers between devices, exchange(): return lax.all_to_all(value, 'index', 0, 0, tiled=True)  12.7 us
    dot_general x1, matrix products, body(): jnp.dot(pre_grad, w_in.T, preferred_element_type=jnp.float32)  9.21 us
    pallas_call x2, Pallas kernels, weight_half(): pl.pallas_call(half_kernel, grid_spec=pltpu.PrefetchScalarGridSpec(num_sc...  8.69 us
  transfers between devices with their start and end apart: 15, of which 7 were waited for; matrix products, arithmetic and copies ran while one was open for 9% of the time, Pallas kernels for 24%

profile of v6, /device:TPU:0, one launch (start us, length us, event | category | flops | bytes accessed | tf_op | source)
XLA Modules:
  0.0 184.3 jit_solution(288759984148860764)
XLA Ops:
  0.7 1.6 shard_map.123
  2.3 8.0 %all-to-all-start.1 = ((bf16[16,16,512]{2,1,0:T(8,128)(2,1)}), bf16[16,16,512]{2,1,0:T(8,128)(2,1)S(1)}, u32[]{:S(2)}, u32[]{:S(2)}) async-start(bf16[16,16,512]{2,1,0:T(8,128)(2,1)} %shard_map.123), calls=%async_computation.1 | async-start | bytes 524288 | tf_op jit(solution)/shard_map/all_to_all | solution.py:38
  10.3 0.6 pad_maximum_fusion
  10.9 19.6 %shard_map.122 = (bf16[1024,3072]{1,0:T(8,128)(2,1)}, bf16[1024,3072]{1,0:T(8,128)(2,1)}, f32[1024,768]{1,0:T(8,128)}, f32[1024,1]{1,0:T(8,128)}, bf16[16,16,1536]{2,1,0:T(8,128)(2,1)}) custom-call(bf16[1024,768]{1,0:T(8,128)(2,1)} %right_ref.1, bf16[768,3072]{1,0:T(8,128)(2,1)} %w_in_ref.1, f32[1,3072]{1,0:T(1,128)} %bitcast.17, ...), custom_call_target="tpu_custom_call" | custom-call | flops 20000000000 | bytes 1000 | tf_op jit(solution)/shard_map/pallas_call | solution.py:109
  30.6 0.1 pad_add_fusion.place_ref
  30.6 0.0 all-to-all-done.1.table_ref
  30.6 7.2 %all-to-all-start = ((bf16[16,16,1536]{2,1,0:T(8,128)(2,1)}), bf16[16,16,1536]{2,1,0:T(8,128)(2,1)S(1)}, u32[]{:S(2)}, u32[]{:S(2)}) async-start(bf16[16,16,1536]{2,1,0:T(8,128)(2,1)} %get-tuple-element.30), calls=%async_computation | async-start | bytes 1572864 | tf_op jit(solution)/shard_map/all_to_all | solution.py:38
  37.9 1.0 copy-done.15
  38.9 6.4 %shard_map.124 = (bf16[32,256,128]{2,1,0:T(8,128)(2,1)S(1)}, f32[32,256,128]{2,1,0:T(8,128)S(1)}) custom-call(s32[3]{0:T(128)S(1)} %pad_add_fusion.place_ref, bf16[16,16,512]{2,1,0:T(8,128)(2,1)S(1)} %all-to-all-done.1.table_ref, f32[1024,1]{1,0:T(8,128)S(1)} %copy-done.15), custom_call_target="tpu_custom_call" | custom-call | flops 10000000000 | bytes 1000 | tf_op jit(solution)/shard_map/pallas_call | solution.py:201
  45.3 1.9 %copy-done.10 = f32[32,256,128]{2,1,0:T(8,128)} copy-done((f32[32,256,128]{2,1,0:T(8,128)}, f32[32,256,128]{2,1,0:T(8,128)S(1)}, u32[]{:S(2)}) %copy-start.10) | copy-done | bytes 4194328
  47.2 1.3 copy-done.18
  48.6 3.1 %all-to-all-done.ask_ref = bf16[16,16,1536]{2,1,0:T(8,128)(2,1)S(1)} async-done(((bf16[16,16,1536]{2,1,0:T(8,128)(2,1)}), bf16[16,16,1536]{2,1,0:T(8,128)(2,1)S(1)}, u32[]{:S(2)}, u32[]{:S(2)}) %all-to-all-start) | async-done | bytes 786464 | tf_op jit(solution)/shard_map/all_to_all | solution.py:38
  51.6 2.8 %copy-done.2 = bf16[4096,768]{1,0:T(8,128)(2,1)S(1)} copy-done((bf16[4096,768]{1,0:T(8,128)(2,1)S(1)}, bf16[4096,768]{1,0:T(8,128)(2,1)}, u32[]{:S(2)}) %copy-start.2) | copy-done | bytes 6291480
  54.4 1.6 copy-done.19
  56.0 4.8 %shard_map.125 = (f32[32,256,128]{2,1,0:T(8,128)S(1)}, f32[16,8,256]{2,1,0:T(8,128)S(1)}) custom-call(bf16[16,16,1536]{2,1,0:T(8,128)(2,1)S(1)} %all-to-all-done.ask_ref, bf16[32,256,128]{2,1,0:T(8,128)(2,1)S(1)} %copy-done.19, bf16[4096,768]{1,0:T(8,128)(2,1)S(1)} %copy-done.2), custom_call_target="tpu_custom_call" | custom-call | flops 8000000000 | bytes 1000 | tf_op jit(solution)/shard_map/pallas_call | solution.py:242
  60.8 12.0 %all_to_all.30.stat_ref = f32[16,8,256]{2,1,0:T(8,128)S(1)} all-to-all(f32[16,8,256]{2,1,0:T(8,128)S(1)} %get-tuple-element.33), channel_id=1, replica_groups=mesh['query'=8,'index'=16] {'index'}, dimensions={0} | all-to-all | bytes 262144 | tf_op jit(solution)/shard_map/all_to_all | solution.py:38
  72.8 2.8 %copy-done.3 = bf16[4096,768]{1,0:T(8,128)(2,1)S(1)} copy-done((bf16[4096,768]{1,0:T(8,128)(2,1)S(1)}, bf16[4096,768]{1,0:T(8,128)(2,1)}, u32[]{:S(2)}) %copy-start.3) | copy-done | bytes 6291480
  75.6 5.5 %shard_map.126 = bf16[256,768]{1,0:T(8,128)(2,1)S(1)} custom-call(s32[3]{0:T(128)S(1)} %pad_add_fusion.place_ref, f32[16,8,256]{2,1,0:T(8,128)S(1)} %all_to_all.30.stat_ref, f32[32,256,128]{2,1,0:T(8,128)S(1)} %get-tuple-element.34.weight_ref, f32[32,256,128]{2,1,0:T(8,128)S(1)} %copy-done.11, bf16[4096,768]{1,0:T(8,128)(2,1)S(1)} %copy-done.3), custom_call_target="tpu_custom_call" | custom-call | flops 5000000000 | bytes 1000 | tf_op jit(solution)/shard_map/pallas_call | solution.py:284
  81.1 12.5 %all_to_all.31.came_ref = bf16[16,16,768]{2,1,0:T(8,128)(2,1)S(1)} all-to-all(bf16[16,16,768]{2,1,0:T(8,128)(2,1)S(1)} %bitcast.12), channel_id=1, replica_groups=mesh['query'=8,'index'=16] {'index'}, dimensions={0} | all-to-all | bytes 786432 | tf_op jit(solution)/shard_map/all_to_all | solution.py:38
  93.6 1.1 shard_map.127
  94.7 1.6 copy-done.13
  96.3 2.8 %copy-done.20 = bf16[1024,3072]{1,0:T(8,128)(2,1)S(1)} copy-done((bf16[1024,3072]{1,0:T(8,128)(2,1)S(1)}, bf16[1024,3072]{1,0:T(8,128)(2,1)}, u32[]{:S(2)}) %copy-start.20) | copy-done | bytes 6291480
  99.1 4.3 %shard_map.129 = bf16[4,384,768]{2,1,0:T(8,128)(2,1)S(1)} custom-call(s32[3]{0:T(128)S(1)} %pad_add_fusion.place_ref, bf16[1024,3072]{1,0:T(8,128)(2,1)S(1)} %copy-done.20, bf16[1024,768]{1,0:T(8,128)(2,1)S(1)} %get-tuple-element.39.right_ref.carry_ref), custom_call_target="tpu_custom_call" | custom-call | flops 40000000000 | bytes 1000 | tf_op jit(solution)/shard_map/pallas_call | solution.py:372
  103.4 0.0 slice-start.1
  103.4 0.1 collective-permute-start
  103.5 4.3 %shard_map.128.kept_ref = bf16[4,384,768]{2,1,0:T(8,128)(2,1)S(1)} custom-call(s32[3]{0:T(128)S(1)} %pad_add_fusion.place_ref, bf16[1024,3072]{1,0:T(8,128)(2,1)S(1)} %copy-done.20, bf16[1024,768]{1,0:T(8,128)(2,1)S(1)} %get-tuple-element.39.right_ref.carry_ref), custom_call_target="tpu_custom_call" | custom-call | flops 40000000000 | bytes 1000 | tf_op jit(solution)/shard_map/pallas_call | solution.py:372
  107.9 0.2 collective-permute-done.came_ref
  108.0 1.5 shard_map.130
  109.5 0.0 copy-start.7
  109.6 1.6 collective-permute-start.1
  111.2 1.7 collective-permute-start.2
  112.9 7.3 %multiply_convert_fusion.left_ref.refs_0_ = bf16[1024,3072]{1,0:T(8,128)(2,1)S(1)} fusion(bf16[1024,3072]{1,0:T(8,128)(2,1)} %get-tuple-element.41, bf16[1024,768]{1,0:T(8,128)(2,1)S(1)} %get-tuple-element.40, bf16[3072,768]{1,0:T(8,128)(2,1)S(1)} %bitcast.16), kind=kOutput, calls=%fused_computation | convolution fusion | flops 4841275392 | bytes 18874368 | tf_op jit(solution)/shard_map/dot_general | solution.py:567
  120.3 7.2 %shard_map.131 = (bf16[4,384,768]{2,1,0:T(8,128)(2,1)S(1)}, bf16[4,384,768]{2,1,0:T(8,128)(2,1)S(1)}) custom-call(s32[3]{0:T(128)S(1)} %pad_add_fusion.place_ref, bf16[1024,3072]{1,0:T(8,128)(2,1)S(1)} %multiply_convert_fusion.left_ref.refs_0_, bf16[1024,768]{1,0:T(8,128)(2,1)S(1)} %copy-done.4), custom_call_target="tpu_custom_call" | custom-call | flops 40000000000 | bytes 1000 | tf_op jit(solution)/shard_map/pallas_call | solution.py:350
  127.5 0.0 collective-permute-done.2.refs_2_.refs_6_
  127.6 0.1 collective-permute-start.3
  127.7 1.3 copy-done.17
  129.0 0.6 copy-done.21
  129.6 1.9 %collective-permute-start.7 = (bf16[384,768]{1,0:T(8,128)(2,1)S(1)}, bf16[384,768]{1,0:T(8,128)(2,1)S(1)}, u32[]{:S(2)}, u32[]{:S(2)}) collective-permute-start(bf16[384,768]{1,0:T(8,128)(2,1)S(1)} %get-tuple-element.52), channel_id=1, source_target_pairs={{0,64},{1,65},{2,66},{3,67},{4,68},{5,69},{6,70},{7,71},{8,72},{9,... | collective-permute-start | bytes 1769480 | tf_op jit(solution)/shard_map/ppermute | solution.py:47
  131.5 0.6 collective-permute-done.3.came_ref
  132.2 1.4 copy-done.25
  133.6 5.1 %shard_map.134 = (f32[384,384]{1,0:T(8,128)}, bf16[384,384]{1,0:T(8,128)(2,1)}, bf16[384,384]{1,0:T(8,128)(2,1)}, bf16[384,384]{1,0:T(8,128)(2,1)}, bf16[16,96,3...) custom-call(s32[3]{0:T(128)} %copy-done.1, bf16[4,384,768]{2,1,0:T(8,128)(2,1)} %copy-done.17, ...), custom_call_target="tpu_custom_call", output_to_operand_aliasing={{5}: (3, {})} | custom-call | flops 5000000000 | bytes 1000 | tf_op jit(solution)/shard_map/pallas_call | solution.py:429
  138.7 3.7 %all-to-all-start.5 = ((bf16[16,96,384]{2,1,0:T(8,128)(2,1)}), bf16[16,96,384]{2,1,0:T(8,128)(2,1)S(1)}, u32[]{:S(2)}, u32[]{:S(2)}) async-start(bf16[16,96,384]{2,1,0:T(8,128)(2,1)} %get-tuple-element.53), calls=%async_computation.5 | async-start | bytes 2359296 | tf_op jit(solution)/shard_map/all_to_all | solution.py:38
  142.4 0.5 collective-permute-start.4
  142.9 2.8 %collective-permute-start.5 = (bf16[384,384]{1,0:T(8,128)(2,1)}, bf16[384,384]{1,0:T(8,128)(2,1)S(1)}, u32[]{:S(2)}, u32[]{:S(2)}) collective-permute-start(bf16[384,384]{1,0:T(8,128)(2,1)} %get-tuple-element.50), channel_id=1, source_target_pairs={{0,96},{1,97},{2,98},{3,99},{4,100},{5,101},{6,102},{7,103},{8,104... | collective-permute-start | bytes 884744 | tf_op jit(solution)/shard_map/ppermute | solution.py:47
  145.7 0.7 collective-permute-start.6
  146.4 9.2 %add_convert_fusion.refs_8_.after_ref = bf16[1024,768]{1,0:T(8,128)(2,1)S(1)} fusion(f32[1024,768]{1,0:T(8,128)} %copy-done.13, bf16[1024,3072]{1,0:T(8,128)(2,1)} %get-tuple-element.47, bf16[768,3072]{1,0:T(8,128)(2,1)} %w_in_ref.1), kind=kOutput, calls=%fused_computation.1 | convolution fusion | flops 4833411072 | bytes 15728640 | tf_op jit(solution)/shard_map/dot_general | solution.py:577
  155.7 0.0 collective-permute-done.4.refs_1_
  155.7 3.0 %collective-permute-done.5.refs_2_ = bf16[384,384]{1,0:T(8,128)(2,1)S(1)} collective-permute-done((bf16[384,384]{1,0:T(8,128)(2,1)}, bf16[384,384]{1,0:T(8,128)(2,1)S(1)}, u32[]{:S(2)}, u32[]{:S(2)}) %collective-permute-start.5) | collective-permute-done | bytes 294944 | tf_op jit(solution)/shard_map/ppermute | solution.py:47
  158.7 0.9 collective-permute-done.6.refs_3_
  159.6 1.3 shard_map.135
  160.8 1.1 copy-done.5
  162.0 0.8 all-to-all-done.5.came_ref
  162.8 6.0 %all-to-all-start.4 = ((bf16[16,24,1152]{2,1,0:T(8,128)(2,1)}), bf16[16,24,1152]{2,1,0:T(8,128)(2,1)S(1)}, u32[]{:S(2)}, u32[]{:S(2)}) async-start(bf16[16,24,1152]{2,1,0:T(8,128)(2,1)} %bitcast.7), calls=%async_computation.4 | async-start | bytes 1769472 | tf_op jit(solution)/shard_map/all_to_all | solution.py:38
  168.8 0.0 copy-start.6
  168.8 1.4 copy-done.6
  170.2 0.2 shard_map.136
  170.4 1.2 collective-permute-start.8
  171.6 2.1 %collective-permute-start.9 = (f32[24,384]{1,0:T(8,128)S(1)}, f32[24,384]{1,0:T(8,128)S(1)}, u32[]{:S(2)}, u32[]{:S(2)}) collective-permute-start(f32[24,384]{1,0:T(8,128)S(1)} %get-tuple-element.56), channel_id=1, source_target_pairs={{0,96},{1,97},{2,98},{3,99},{4,100},{5,101},{6,102},{7,103},{8,104... | collective-permute-start | bytes 110600 | tf_op jit(solution)/shard_map/ppermute | solution.py:47
  173.7 0.9 collective-permute-start.10
  174.7 8.8 %all-to-all-done.4.refs_0_ = bf16[16,24,1152]{2,1,0:T(8,128)(2,1)S(1)} async-done(((bf16[16,24,1152]{2,1,0:T(8,128)(2,1)}), bf16[16,24,1152]{2,1,0:T(8,128)(2,1)S(1)}, u32[]{:S(2)}, u32[]{:S(2)}) %all-to-all-start.4) | async-done | bytes 884768 | tf_op jit(solution)/shard_map/all_to_all | solution.py:38
  183.4 0.0 collective-permute-done.8.refs_2_
  183.4 0.0 collective-permute-done.9.refs_3_
  183.4 0.0 collective-permute-done.10.refs_4_
  183.5 0.8 shard_map.137
  (46 shorter events, 0.1 us)
Async XLA Ops:
  0.6 9.6 %copy-start.22 = (f32[768]{0:T(1024)S(1)}, f32[768]{0:T(1024)}, u32[]{:S(2)}) copy-start(f32[768]{0:T(1024)} %param.17) | copy-start | bytes 9220
  0.6 9.6 %copy-start.23 = (f32[768]{0:T(1024)S(1)}, f32[768]{0:T(1024)}, u32[]{:S(2)}) copy-start(f32[768]{0:T(1024)} %param.16) | copy-start | bytes 9220
  0.7 9.6 %copy-start.24 = (f32[768]{0:T(1024)S(1)}, f32[768]{0:T(1024)}, u32[]{:S(2)}) copy-start(f32[768]{0:T(1024)} %param.15) | copy-start | bytes 9220
  2.3 28.3 %all-to-all-start.1 = ((bf16[16,16,512]{2,1,0:T(8,128)(2,1)}), bf16[16,16,512]{2,1,0:T(8,128)(2,1)S(1)}, u32[]{:S(2)}, u32[]{:S(2)}) async-start(bf16[16,16,512]{2,1,0:T(8,128)(2,1)} %shard_map.123), calls=%async_computation.1 | async-start | bytes 524288 | tf_op jit(solution)/shard_map/all_to_all | solution.py:38
  30.6 89.6 %copy-start.1 = (s32[3]{0:T(128)}, s32[3]{0:T(128)S(1)}, u32[]{:S(2)}) copy-start(s32[3]{0:T(128)S(1)} %pad_add_fusion.place_ref) | copy-start | bytes 40
  30.6 21.0 %all-to-all-start = ((bf16[16,16,1536]{2,1,0:T(8,128)(2,1)}), bf16[16,16,1536]{2,1,0:T(8,128)(2,1)S(1)}, u32[]{:S(2)}, u32[]{:S(2)}) async-start(bf16[16,16,1536]{2,1,0:T(8,128)(2,1)} %get-tuple-element.30), calls=%async_computation | async-start | bytes 1572864 | tf_op jit(solution)/shard_map/all_to_all | solution.py:38
  37.9 1.0 copy-start.15
  45.3 1.9 %copy-start.10 = (f32[32,256,128]{2,1,0:T(8,128)}, f32[32,256,128]{2,1,0:T(8,128)S(1)}, u32[]{:S(2)}) copy-start(f32[32,256,128]{2,1,0:T(8,128)S(1)} %get-tuple-element.35.share_ref) | copy-start | bytes 12582916
  47.2 1.3 copy-start.18
  51.6 2.8 %copy-start.2 = (bf16[4096,768]{1,0:T(8,128)(2,1)S(1)}, bf16[4096,768]{1,0:T(8,128)(2,1)}, u32[]{:S(2)}) copy-start(bf16[4096,768]{1,0:T(8,128)(2,1)} %slab_ref.1) | copy-start | bytes 18874372
  54.4 1.6 copy-start.19
  56.0 16.8 %copy-start.11 = (f32[32,256,128]{2,1,0:T(8,128)S(1)}, f32[32,256,128]{2,1,0:T(8,128)}, u32[]{:S(2)}) copy-start(f32[32,256,128]{2,1,0:T(8,128)} %copy-done.10) | copy-start | bytes 12582916
  72.8 2.8 %copy-start.3 = (bf16[4096,768]{1,0:T(8,128)(2,1)S(1)}, bf16[4096,768]{1,0:T(8,128)(2,1)}, u32[]{:S(2)}) copy-start(bf16[4096,768]{1,0:T(8,128)(2,1)} %slab_ref.1) | copy-start | bytes 18874372
  75.6 18.0 %copy-start = (f32[3072]{0:T(1024)S(1)}, f32[3072]{0:T(1024)}, u32[]{:S(2)}) copy-start(f32[3072]{0:T(1024)} %pad_maximum_fusion) | copy-start | bytes 36868
  75.6 18.0 %copy-start.12 = (f32[1024,768]{1,0:T(8,128)S(1)}, f32[1024,768]{1,0:T(8,128)}, u32[]{:S(2)}) copy-start(f32[1024,768]{1,0:T(8,128)} %get-tuple-element.36.normed_ref) | copy-start | bytes 9437188
  75.6 18.0 %copy-start.16 = (f32[1024,1]{1,0:T(8,128)S(1)}, f32[1024,1]{1,0:T(8,128)}, u32[]{:S(2)}) copy-start(f32[1024,1]{1,0:T(8,128)} %get-tuple-element.31.after_ref.rstd_ref) | copy-start | bytes 12292
  94.7 1.6 copy-start.13
  96.3 2.8 %copy-start.20 = (bf16[1024,3072]{1,0:T(8,128)(2,1)S(1)}, bf16[1024,3072]{1,0:T(8,128)(2,1)}, u32[]{:S(2)}) copy-start(bf16[1024,3072]{1,0:T(8,128)(2,1)} %get-tuple-element.38.left_ref) | copy-start | bytes 18874372
  99.1 13.8 %slice-start = ((s8[4718592]{0:T(1024)(128)(4,1)}), s8[4194304]{0:T(1024)(128)(4,1)S(1)}, s32[]{:S(2)}) async-start(s8[4718592]{0:T(1024)(128)(4,1)} %bitcast.15), calls=%async_computation.6 | async-start | bytes 8388608
  103.4 9.5 %slice-start.1 = ((s8[4718592]{0:T(1024)(128)(4,1)}), s8[524288]{0:T(1024)(128)(4,1)S(1)}, s32[]{:S(2)}) async-start(s8[4718592]{0:T(1024)(128)(4,1)} %bitcast.15), calls=%async_computation.7 | async-start | bytes 1048576
  103.4 4.6 %collective-permute-start = (bf16[4,384,768]{2,1,0:T(8,128)(2,1)S(1)}, bf16[4,384,768]{2,1,0:T(8,128)(2,1)S(1)}, u32[]{:S(2)}, u32[]{:S(2)}) collective-permute-start(bf16[4,384,768]{2,1,0:T(8,128)(2,1)S(1)} %shard_map.129), channel_id=1, source_target_pairs={{0,16},{1,17},{2,18},{3,19},{4,20},{5,21},{6,22},{7,23},{8,24},{9,... | collective-permute-start | bytes 7077896 | tf_op jit(solution)/shard_map/ppermute | solution.py:47
  109.5 18.1 %copy-start.7 = (f32[384,768]{1,0:T(8,128)}, f32[384,768]{1,0:T(8,128)S(1)}, u32[]{:S(2)}) copy-start(f32[384,768]{1,0:T(8,128)S(1)} %get-tuple-element.46.own_ref.refs_4_) | copy-start | bytes 3538948
  109.6 18.0 %collective-permute-start.1 = (bf16[384,768]{1,0:T(8,128)(2,1)S(1)}, bf16[384,768]{1,0:T(8,128)(2,1)S(1)}, u32[]{:S(2)}, u32[]{:S(2)}) collective-permute-start(bf16[384,768]{1,0:T(8,128)(2,1)S(1)} %get-tuple-element.44), channel_id=1, source_target_pairs={{0,32},{1,33},{2,34},{3,35},{4,36},{5,37},{6,38},{7,39},{8,40},{9,... | collective-permute-start | bytes 1769480 | tf_op jit(solution)/shard_map/ppermute | solution.py:47
  111.2 16.3 %collective-permute-start.2 = (bf16[384,768]{1,0:T(8,128)(2,1)S(1)}, bf16[384,768]{1,0:T(8,128)(2,1)S(1)}, u32[]{:S(2)}, u32[]{:S(2)}) collective-permute-start(bf16[384,768]{1,0:T(8,128)(2,1)S(1)} %get-tuple-element.45), channel_id=1, source_target_pairs={{0,96},{1,97},{2,98},{3,99},{4,100},{5,101},{6,102},{7,103},{8,104... | collective-permute-start | bytes 1769480 | tf_op jit(solution)/shard_map/ppermute | solution.py:47
  112.9 7.3 %copy-start.4 = (bf16[1024,768]{1,0:T(8,128)(2,1)S(1)}, bf16[1024,768]{1,0:T(8,128)(2,1)}, u32[]{:S(2)}) copy-start(bf16[1024,768]{1,0:T(8,128)(2,1)} %right_ref.1) | copy-start | bytes 4718596
  120.3 7.2 %copy-start.14 = (bf16[1024,3072]{1,0:T(8,128)(2,1)}, bf16[1024,3072]{1,0:T(8,128)(2,1)S(1)}, u32[]{:S(2)}) copy-start(bf16[1024,3072]{1,0:T(8,128)(2,1)S(1)} %multiply_convert_fusion.left_ref.refs_0_) | copy-start | bytes 18874372
  127.5 1.5 copy-start.17
  127.6 4.6 %collective-permute-start.3 = (bf16[4,384,768]{2,1,0:T(8,128)(2,1)S(1)}, bf16[4,384,768]{2,1,0:T(8,128)(2,1)S(1)}, u32[]{:S(2)}, u32[]{:S(2)}) collective-permute-start(bf16[4,384,768]{2,1,0:T(8,128)(2,1)S(1)} %shard_map.132), channel_id=1, source_target_pairs={{0,16},{1,17},{2,18},{3,19},{4,20},{5,21},{6,22},{7,23},{8,24},{9,... | collective-permute-start | bytes 7077896 | tf_op jit(solution)/shard_map/ppermute | solution.py:47
  129.0 0.6 copy-start.21
  129.6 26.1 %collective-permute-start.7 = (bf16[384,768]{1,0:T(8,128)(2,1)S(1)}, bf16[384,768]{1,0:T(8,128)(2,1)S(1)}, u32[]{:S(2)}, u32[]{:S(2)}) collective-permute-start(bf16[384,768]{1,0:T(8,128)(2,1)S(1)} %get-tuple-element.52), channel_id=1, source_target_pairs={{0,64},{1,65},{2,66},{3,67},{4,68},{5,69},{6,70},{7,71},{8,72},{9,... | collective-permute-start | bytes 1769480 | tf_op jit(solution)/shard_map/ppermute | solution.py:47
  132.2 1.4 copy-start.25
  138.7 24.1 %all-to-all-start.5 = ((bf16[16,96,384]{2,1,0:T(8,128)(2,1)}), bf16[16,96,384]{2,1,0:T(8,128)(2,1)S(1)}, u32[]{:S(2)}, u32[]{:S(2)}) async-start(bf16[16,96,384]{2,1,0:T(8,128)(2,1)} %get-tuple-element.53), calls=%async_computation.5 | async-start | bytes 2359296 | tf_op jit(solution)/shard_map/all_to_all | solution.py:38
  142.4 13.3 %collective-permute-start.4 = (bf16[384,384]{1,0:T(8,128)(2,1)}, bf16[384,384]{1,0:T(8,128)(2,1)S(1)}, u32[]{:S(2)}, u32[]{:S(2)}) collective-permute-start(bf16[384,384]{1,0:T(8,128)(2,1)} %get-tuple-element.49), channel_id=1, source_target_pairs={{0,32},{1,33},{2,34},{3,35},{4,36},{5,37},{6,38},{7,39},{8,40},{9,... | collective-permute-start | bytes 884744 | tf_op jit(solution)/shard_map/ppermute | solution.py:47
  142.9 15.7 %collective-permute-start.5 = (bf16[384,384]{1,0:T(8,128)(2,1)}, bf16[384,384]{1,0:T(8,128)(2,1)S(1)}, u32[]{:S(2)}, u32[]{:S(2)}) collective-permute-start(bf16[384,384]{1,0:T(8,128)(2,1)} %get-tuple-element.50), channel_id=1, source_target_pairs={{0,96},{1,97},{2,98},{3,99},{4,100},{5,101},{6,102},{7,103},{8,104... | collective-permute-start | bytes 884744 | tf_op jit(solution)/shard_map/ppermute | solution.py:47
  145.7 13.8 %collective-permute-start.6 = (bf16[384,384]{1,0:T(8,128)(2,1)}, bf16[384,384]{1,0:T(8,128)(2,1)S(1)}, u32[]{:S(2)}, u32[]{:S(2)}) collective-permute-start(bf16[384,384]{1,0:T(8,128)(2,1)} %get-tuple-element.51), channel_id=1, source_target_pairs={{0,64},{1,65},{2,66},{3,67},{4,68},{5,69},{6,70},{7,71},{8,72},{9,... | collective-permute-start | bytes 884744 | tf_op jit(solution)/shard_map/ppermute | solution.py:47
  146.4 13.1 %copy-start.8 = (f32[384,768]{1,0:T(8,128)S(1)}, f32[384,768]{1,0:T(8,128)}, u32[]{:S(2)}) copy-start(f32[384,768]{1,0:T(8,128)} %copy-done.7) | copy-start | bytes 3538948
  146.4 13.1 %copy-start.9 = (f32[384,384]{1,0:T(8,128)S(1)}, f32[384,384]{1,0:T(8,128)}, u32[]{:S(2)}) copy-start(f32[384,384]{1,0:T(8,128)} %get-tuple-element.48.refs_0_) | copy-start | bytes 1769476
  160.8 1.1 copy-start.5
  162.8 20.7 %all-to-all-start.4 = ((bf16[16,24,1152]{2,1,0:T(8,128)(2,1)}), bf16[16,24,1152]{2,1,0:T(8,128)(2,1)S(1)}, u32[]{:S(2)}, u32[]{:S(2)}) async-start(bf16[16,24,1152]{2,1,0:T(8,128)(2,1)} %bitcast.7), calls=%async_computation.4 | async-start | bytes 1769472 | tf_op jit(solution)/shard_map/all_to_all | solution.py:38
  168.8 1.4 copy-start.6
  170.4 13.0 %collective-permute-start.8 = (f32[24,384]{1,0:T(8,128)S(1)}, f32[24,384]{1,0:T(8,128)S(1)}, u32[]{:S(2)}, u32[]{:S(2)}) collective-permute-start(f32[24,384]{1,0:T(8,128)S(1)} %get-tuple-element.55), channel_id=1, source_target_pairs={{0,32},{1,33},{2,34},{3,35},{4,36},{5,37},{6,38},{7,39},{8,40},{9,... | collective-permute-start | bytes 110600 | tf_op jit(solution)/shard_map/ppermute | solution.py:47
  171.6 11.8 %collective-permute-start.9 = (f32[24,384]{1,0:T(8,128)S(1)}, f32[24,384]{1,0:T(8,128)S(1)}, u32[]{:S(2)}, u32[]{:S(2)}) collective-permute-start(f32[24,384]{1,0:T(8,128)S(1)} %get-tuple-element.56), channel_id=1, source_target_pairs={{0,96},{1,97},{2,98},{3,99},{4,100},{5,101},{6,102},{7,103},{8,104... | collective-permute-start | bytes 110600 | tf_op jit(solution)/shard_map/ppermute | solution.py:47
  173.7 9.7 %collective-permute-start.10 = (f32[24,384]{1,0:T(8,128)S(1)}, f32[24,384]{1,0:T(8,128)S(1)}, u32[]{:S(2)}, u32[]{:S(2)}) collective-permute-start(f32[24,384]{1,0:T(8,128)S(1)} %get-tuple-element.57), channel_id=1, source_target_pairs={{0,64},{1,65},{2,66},{3,67},{4,68},{5,69},{6,70},{7,71},{8,72},{9,... | collective-permute-start | bytes 110600 | tf_op jit(solution)/shard_map/ppermute | solution.py:47
